TPU v7x, 256 devices: a whole 4x4x8 slice. The times are simulated.
256 devices in a mesh: dp: 4 (over y_hi, core), corpus: 64 (over y_lo, x, z).
Axes of the slice: x: 4, y: 4 (y_hi: 2, y_lo: 2; y = y_hi * 2 + y_lo), z: 8, core: 2. Of those that a mesh axis runs over, the one named last changes fastest.
Arguments:
- queries: float32 [32768, 256], P(('dp', 'corpus')), may hold values from -40 to 40
- items: float32 [32768, 256], P('corpus'), may hold values from -6 to 6
- labels: int32 [32768], P(('dp', 'corpus')), may hold values from 0 to 32767
Outputs:
- loss: float32 [], replicated
- query_grad: float32 [32768, 256], P(('dp', 'corpus'))
- item_grad: float32 [32768, 256], P('corpus')
All inputs are finite; a program needn't handle non-finite values.
Results may differ from a plain program's by a relative error of at most 0.0003.
Values sent between devices are 32-bit elements; how exact they have to be, the bound alone decides.
No kernel may reach another device: no remote copies, remote signals or barrier semaphores. Data moves between devices by JAX's collectives and lax.ppermute only.
A program may use at most 128 MiB of HBM per device.

v0:
```python
import math

import jax
import jax.numpy as jnp
from jax import lax
from jax.sharding import PartitionSpec as P

E = 256


def score_rows(query_rows, item_rows):
    return jnp.dot(query_rows, item_rows.T, precision=lax.Precision.HIGHEST) * E ** (-0.5)


def body(queries, items, labels):
    q_count = queries.shape[0]
    i_count = items.shape[0]
    n_corpus = lax.axis_size("corpus")
    position = lax.axis_index("corpus")
    scale = E ** (-0.5)
    columns = jnp.arange(i_count, dtype=jnp.int32)
    group_rows, group_labels = (
        lax.all_gather(queries, "corpus", axis=0, tiled=True),
        lax.all_gather(labels, "corpus", axis=0, tiled=True),
    )
    rows_all = group_rows.shape[0]
    block = math.gcd(rows_all, 1024)
    count = rows_all // block
    local_labels = group_labels - position * i_count
    row_blocks = group_rows.reshape(count, block, E)
    label_blocks = local_labels.reshape(count, block)

    def forward(pair):
        query_rows, label_rows = pair
        scores = score_rows(query_rows, items)
        top = jnp.max(scores, axis=1)
        total = jnp.sum(jnp.exp(scores - top[:, None]), axis=1)
        picked = jnp.sum(jnp.where(columns[None, :] == label_rows[:, None], scores, 0.0))
        return (top, total, picked)

    tops, totals, picks = lax.map(forward, (row_blocks, label_blocks))
    tops = tops.reshape(rows_all)
    totals = totals.reshape(rows_all)
    picked_sum = jnp.sum(picks)
    best = lax.pmax(tops, "corpus")
    whole = lax.psum(totals * jnp.exp(tops - best), "corpus")
    lse = best + jnp.log(whole)
    own_lse = lax.dynamic_slice_in_dim(lse, position * q_count, q_count)
    loss_part = jnp.sum(own_lse) - picked_sum

    def backward(accum, triple):
        query_rows, label_rows, lse_rows = triple
        scores = score_rows(query_rows, items)
        delta = jnp.exp(scores - lse_rows[:, None]) - (
            columns[None, :] == label_rows[:, None]
        ).astype(jnp.float32)
        grad_rows = jnp.dot(delta, items, precision=lax.Precision.HIGHEST) * scale
        accum = accum + jnp.dot(delta.T, query_rows, precision=lax.Precision.HIGHEST) * scale
        return (accum, grad_rows)

    start = jnp.zeros((i_count, E), jnp.float32)
    item_local, grad_blocks = lax.scan(
        backward, start, (row_blocks, label_blocks, lse.reshape(count, block))
    )
    query_grad = lax.psum_scatter(
        grad_blocks.reshape(rows_all, E), "corpus", scatter_dimension=0, tiled=True
    )
    item_grad = lax.psum(item_local, "dp")
    total_queries = q_count * lax.axis_size("dp") * n_corpus
    loss = lax.psum(loss_part, ("dp", "corpus")) / total_queries
    return (loss, query_grad, item_grad)


def solution(mesh):
    in_specs = (P(("dp", "corpus"), None), P("corpus", None), P(("dp", "corpus")))
    out_specs = (P(), P(("dp", "corpus"), None), P("corpus", None))
    return jax.shard_map(body, mesh=mesh, in_specs=in_specs, out_specs=out_specs, check_vma=False)
```

profile of v0, /device:TPU:24, one launch (start us, length us, event | category | flops | bytes accessed | tf_op | source)
XLA Modules:
  0.0 1453.6 jit_solution(1780612957483418395)
XLA Ops:
  8.0 157.4 %all-gather = s32[64,1,128]{2,1,0:T(1,128)S(1)} all-gather(s32[1,1,128]{2,1,0:T(1,128)} %bitcast.78), channel_id=1, replica_groups=mesh['dp'=4,'corpus'=64] {'corpus'}, dimensions={0}, use_global_device_ids=true | all-gather | bytes 33280 | tf_op jit(solution)/shard_map/all_gather | solution.py:24
  165.6 158.4 %all-gather.3.cloned.1.call-done = f32[8192,256]{1,0:T(8,128)} async-done(((f32[128,256]{1,0:T(8,128)}), f32[8192,256]{1,0:T(8,128)}) %all-gather.3.cloned.1.call-update) | async-done | bytes 8388624 | tf_op jit(solution)/shard_map/all_gather | solution.py:23
  323.9 43.4 %while.28 = (s32[]{:T(128)}, f32[8,1024]{1,0:T(8,128)S(1)}, f32[8,1024]{1,0:T(8,128)S(1)}, f32[8]{0:T(128)S(1)}, f32[8,1024,256]{2,1,0:T(8,128)}, /*index=5*/f32...) while((s32[]{:T(128)}, f32[8,1024]{1,0:T(8,128)S(1)}, f32[8,1024]{1,0:T(8,128)S(1)}, ...), condition=%wide.region_4.5_spmd.clone, body=%wide.region_0.4_spmd.clone.sunk | while | flops 1614804992 | bytes 5808761 | solution.py:41
  367.4 307.4 %pmax.7 = f32[8192]{0:T(1024)S(1)} all-reduce(f32[8192]{0:T(1024)S(1)} %bitcast.74), channel_id=1, replica_groups=mesh['dp'=4,'corpus'=64] {'corpus'}, use_global_device_ids=true, to_apply=%region_5.6 | all-reduce | flops 8192 | bytes 65536 | tf_op jit(solution)/shard_map/pmax | solution.py:45
  674.8 302.8 %psum.21 = f32[8192]{0:T(1024)S(1)} all-reduce(f32[8192]{0:T(1024)S(1)} %bitcast_multiply_fusion), channel_id=1, replica_groups=mesh['dp'=4,'corpus'=64] {'corpus'}, use_global_device_ids=true, to_apply=%region_6.7 | all-reduce | flops 8192 | bytes 65536 | tf_op jit(solution)/shard_map/psum | solution.py:46
  977.7 90.3 %while.29 = (s32[]{:T(128)}, f32[512,256]{1,0:T(8,128)S(1)}, f32[8,1024,256]{2,1,0:T(8,128)}, f32[8,1024,256]{2,1,0:T(8,128)}, f32[512,256]{1,0:T(8,128)}, /*ind...) while((s32[]{:T(128)}, f32[512,256]{1,0:T(8,128)S(1)}, ...), condition=%wide.region_11.12_spmd.clone, body=%wide.region_10.11_spmd.clone.sunk | while | flops 4835115008 | bytes 13657739 | solution.py:62
  977.7 3.7 convert_subtract_fusion.2
  984.3 4.7 fusion.38
  989.1 3.7 convert_subtract_fusion.2
  995.6 4.7 fusion.38
  1000.4 3.7 convert_subtract_fusion.2
  1006.8 4.7 fusion.38
  1011.6 3.7 convert_subtract_fusion.2
  1018.1 4.7 fusion.38
  1022.9 3.7 convert_subtract_fusion.2
  1029.4 4.7 fusion.38
  1034.2 3.7 convert_subtract_fusion.2
  1040.7 4.7 fusion.38
  1045.5 3.7 convert_subtract_fusion.2
  1052.0 4.7 fusion.38
  1056.8 3.7 convert_subtract_fusion.2
  1063.2 4.7 fusion.38
  1072.3 73.4 %psum.22 = f32[]{:T(128)} all-reduce(f32[]{:T(128)S(6)} %sub.36), channel_id=1, replica_groups=mesh['dp'=4,'corpus'=64] {'dp','corpus'}, use_global_device_ids=true, to_apply=%region_9.10 | all-reduce | flops 1 | bytes 8 | tf_op jit(solution)/shard_map/psum | solution.py:70
  1146.3 297.8 %reduce-scatter.2.cloned.1.call-done = f32[128,256]{1,0:T(8,128)} async-done(((f32[8192,256]{1,0:T(8,128)}), f32[128,256]{1,0:T(8,128)}) %reduce-scatter.2.cloned.1.call-update) | async-done | bytes 131088 | tf_op jit(solution)/shard_map/reduce_scatter | solution.py:65
  (111 shorter events, 71.4 us)
Async XLA Ops:
  7.2 316.8 %all-gather.3.cloned.1.call-start = ((), (), s32[]{:S(2)}) async-start(), calls=%async_computation.1 | async-start | bytes 8519680 | tf_op jit(solution)/shard_map/all_gather | solution.py:23
  7.9 1138.4 %all-reduce.2.cloned.1.call-start = ((), (), s32[]{:S(2)}) async-start(), calls=%async_computation.3 | async-start | bytes 1048576 | tf_op jit(solution)/shard_map/psum | solution.py:68
  977.7 3.7 copy-start
  989.0 3.7 copy-start
  1000.3 3.7 copy-start
  1011.6 3.7 copy-start
  1022.8 3.7 copy-start
  1034.2 3.7 copy-start
  1045.4 3.7 copy-start
  1056.7 3.7 copy-start
  1068.0 0.8 copy-start.1
  1068.8 375.3 %reduce-scatter.2.cloned.1.call-start = ((), (), s32[]{:S(2)}) async-start(), calls=%async_computation.2 | async-start | bytes 8519680 | tf_op jit(solution)/shard_map/reduce_scatter | solution.py:65
Sparse Core Ops, SparseCore 0:
  9.8 314.0 all-gather.2
  1068.9 39.0 all-reduce.1
  1111.2 332.8 reduce-scatter.1
where the time goes:
time: 1450 us
  blocking collectives  841 us (58%)
  waiting for transfers between devices  458 us (32%)
  matrix products  116 us (8%)
  between operations  17 us (1%)
    pmax x1, blocking collectives, body(): best = lax.pmax(tops, 'corpus')  307 us
    psum x1, blocking collectives, body(): whole = lax.psum(totals * jnp.exp(tops - best), 'corpus')  303 us
    reduce_scatter x1, waiting for transfers between devices, body(): lax.psum_scatter(grad_blocks.reshape(rows_all, E), 'corpus', scatter_dime...  298 us
    all_gather x1, waiting for transfers between devices, body(): lax.all_gather(queries, 'corpus', axis=0, tiled=True)  158 us
    all_gather x1, blocking collectives, body(): lax.all_gather(labels, 'corpus', axis=0, tiled=True)  157 us
    psum x1, blocking collectives, body(): loss = lax.psum(loss_part, ('dp', 'corpus')) / total_queries  73.4 us
    dot_general x16, matrix products, score_rows(): jnp.dot(query_rows, item_rows.T, precision=lax.Precision.HIGHEST)  55.7 us
    dot_general x8, matrix products, backward(): jnp.dot(delta.T, query_rows, precision=lax.Precision.HIGHEST) * scale  37.9 us
  transfers between devices with their start and end apart: 3, of which 2 were waited for; matrix products, arithmetic and copies ran while one was open for 0% of the time, Pallas kernels for 0%

commit v1 on v0

v1 whole, which is shorter than its diff:
```python
import jax
import jax.numpy as jnp
from jax import lax
from jax.experimental import pallas as pl
from jax.experimental.pallas import tpu as pltpu
from jax.sharding import Mesh, PartitionSpec as P

E = 256
ZN, XN, YN = 8, 4, 4
ROWS = 128
PAD = 136
HALF = 256
CUT = HALF // 2
PIECES = 8
LOCAL = PIECES * HALF
AXES = ("yh", "c", "yl", "x", "z")
f32, bf16 = jnp.float32, jnp.bfloat16


def place(i):
    return (i >> 7) & 1, (i >> 6) & 1, (i >> 5) & 1, (i >> 3) & 3, i & 7


def index(yh, c, yl, x, z):
    return yh * 128 + c * 64 + yl * 32 + x * 8 + z


def pairs(dx=0, dy=0, dz=0, dc=0):
    out = []
    for i in range(256):
        yh, c, yl, x, z = place(i)
        y = (yh * 2 + yl + dy) % YN
        out.append((i, index(y >> 1, (c + dc) % 2, y & 1, (x + dx) % XN, (z + dz) % ZN)))
    return out


def send(a, **shift):
    return lax.ppermute(a, AXES, pairs(**shift))


def flip(a, bit):
    return lax.ppermute(a, AXES, [(i, i ^ bit) for i in range(256)])


def after(a, b):
    return lax.optimization_barrier((a, b))[0]


def split(a):
    hi = a.astype(bf16)
    return hi, (a - hi.astype(f32)).astype(bf16)


def dot(a, b, dims):
    return lax.dot_general(a, b, (dims, ((), ())), preferred_element_type=f32)


def cat(parts, axis):
    return jnp.concatenate(parts, axis=axis)


NT = ((1,), (1,))
NN = ((1,), (0,))
SMEM = pl.BlockSpec(memory_space=pltpu.SMEM)
VMEM = pl.BlockSpec(memory_space=pltpu.VMEM)


def shape(*dims, dtype=f32):
    return jax.ShapeDtypeStruct(dims, dtype)


def params(mib):
    return pltpu.CompilerParams(vmem_limit_bytes=mib * 2**20)


def local_labels(pos_ref, q_ref):
    lab = cat([q_ref[0, ROWS : ROWS + 1, :ROWS], q_ref[1, ROWS : ROWS + 1, :ROWS]], 1)
    lab = lab.astype(jnp.int32)
    z, c, yl, x = pos_ref[0], pos_ref[1], pos_ref[2], pos_ref[3]
    here = ((lab >> 9) & 7 == z) & ((lab >> 8) & 1 == c)
    piece = (((lab >> 14) ^ yl) & 1) * 4 + (((lab >> 12) & 3) - x & 3)
    return jnp.where(here, piece * HALF + (lab & 255), -1)


def query_rows(q_ref):
    return cat([q_ref[0, :ROWS, :], q_ref[1, :ROWS, :]], 0) * (E**-0.5)


def small(kernel, ins, outs, smem_out=()):
    return pl.pallas_call(
        kernel,
        in_specs=[SMEM if a.ndim == 1 else VMEM for a in ins],
        out_specs=[SMEM if len(o.shape) == 1 else VMEM for o in outs],
        out_shape=outs,
        compiler_params=params(10),
        name=kernel.__name__,
    )(*ins)


def start_kernel(pos_ref, queries, labels, items, out, own):
    for k in range(ZN):
        out[k, :ROWS, :] = queries[...]
        out[k, ROWS:, :ROWS] = jnp.broadcast_to(labels[...].astype(f32), (PAD - ROWS, ROWS))
        out[k, ROWS:, ROWS:] = jnp.zeros((PAD - ROWS, E - ROWS), f32)
    own[...] = items[pl.ds(pl.multiple_of(pos_ref[1] * HALF, HALF), HALF), :]


def pack_items_kernel(*refs):
    *parts, xh, xl, xth, xtl, token = refs
    token[0] = 0.0
    for d, p in enumerate(parts):
        at = slice(d * HALF, (d + 1) * HALF)
        xh[at, :], xl[at, :] = split(p[...])
        xth[:, at], xtl[:, at] = split(p[...].T)


def hold_kernel(token, a, out):
    out[...] = a[...]


def spread_kernel(mine, other, out):
    for k in range(2 * ZN):
        out[k, 0] = mine[...]
        out[k, 1] = other[...]


def merge_kernel(pos_ref, got, lse_ref, part_ref):
    core = pos_ref[1]
    loss = None
    for h in range(2):
        side = [(k, h ^ ((core ^ (k // ZN)) & 1)) for k in range(2 * ZN)]
        best = got[side[0][0], side[0][1], 0]
        for k, w in side[1:]:
            best = jnp.maximum(best, got[k, w, 0])
        total = pick = jnp.zeros((ZN, ROWS), f32)
        for k, w in side:
            total += got[k, w, 1] * jnp.exp(got[k, w, 0] - best)
            pick += got[k, w, 2]
        lse = best + jnp.log(total)
        lse_ref[h] = lse
        loss = lse - pick if loss is None else loss + (lse - pick)
    part_ref[0] = jnp.sum(loss)


def forward_kernel(pos_ref, xh, xl, q_ref, s0_ref, s1_ref, stat_ref):
    qh, ql = split(query_rows(q_ref))
    qcat = cat([qh, qh, ql], 1)
    lab = local_labels(pos_ref, q_ref)
    rows = lax.broadcasted_iota(jnp.int32, (HALF, 256), 0)
    top = total = None
    pick = jnp.zeros((8, 256), f32)
    for t in range(PIECES):
        at = slice(t * HALF, (t + 1) * HALF)
        s = dot(cat([xh[at], xl[at], xh[at]], 1), qcat, NT)
        (s0_ref, s1_ref)[t // 4][0, t % 4] = s
        pick += jnp.sum(jnp.where(rows == lab - t * HALF, s, 0.0).reshape(32, 8, 256), axis=0)
        s = s.reshape(32, 8, 256)
        best = jnp.max(s, axis=0)
        if top is None:
            total = jnp.sum(jnp.exp(s - best[None]), axis=0)
        else:
            best = jnp.maximum(top, best)
            total = total * jnp.exp(top - best) + jnp.sum(jnp.exp(s - best[None]), axis=0)
        top = best
    best = jnp.max(top, axis=0, keepdims=True)
    total = jnp.sum(total * jnp.exp(top - best), axis=0, keepdims=True)
    pick = jnp.sum(pick, axis=0, keepdims=True)
    for h in range(2):
        z = 2 * pl.program_id(0) + h
        at = slice(h * ROWS, (h + 1) * ROWS)
        stat_ref[0, pl.ds(z, 1), :] = best[:, at]
        stat_ref[1, pl.ds(z, 1), :] = total[:, at]
        stat_ref[2, pl.ds(z, 1), :] = pick[:, at]


def forward(pos, xh, xl, q):
    return pl.pallas_call(
        forward_kernel,
        grid=(4,),
        in_specs=[
            SMEM,
            pl.BlockSpec((LOCAL, E), lambda i: (0, 0)),
            pl.BlockSpec((LOCAL, E), lambda i: (0, 0)),
            pl.BlockSpec((2, PAD, E), lambda i: (i, 0, 0)),
        ],
        out_specs=[
            pl.BlockSpec((1, 4, HALF, 256), lambda i: (i, 0, 0, 0)),
            pl.BlockSpec((1, 4, HALF, 256), lambda i: (i, 0, 0, 0)),
            pl.BlockSpec((3, ZN, ROWS), lambda i: (0, 0, 0)),
        ],
        out_shape=[shape(4, 4, HALF, 256)] * 2 + [shape(3, ZN, ROWS)],
        compiler_params=params(12),
        cost_estimate=pl.CostEstimate(flops=3 * 2**30, bytes_accessed=10 * 2**20, transcendentals=2**21),
        name="forward",
    )(pos, xh, xl, q)


def delta(s, lse, rows, lab, at):
    p = jnp.exp(s - lse)
    return split(jnp.where(rows == lab - at, p - 1.0, p))


def block(i, pos_ref, lse_ref, mine, other):
    q = jnp.where(i < 4, mine[...], other[...])
    qh, ql = split(query_rows(q))
    z = 2 * (i & 3)
    k = i >> 2
    lse = cat([lse_ref[k, pl.ds(z, 1), :], lse_ref[k, pl.ds(z + 1, 1), :]], 1)
    return cat([qh, ql, qh], 0), local_labels(pos_ref, q), lse


def backward_a_kernel(pos_ref, part, xth, xtl, mine, other, lse_ref, sm0, sm1, so0, so1, om, oo, up, down, token, g_acc):
    i = pl.program_id(0)

    @pl.when(i == 0)
    def _():
        g_acc[...] = jnp.zeros_like(g_acc)
        token[0] = 0.0

    qcat, lab, lse = block(i, pos_ref, lse_ref, mine, other)
    rows = lax.broadcasted_iota(jnp.int32, (HALF, 256), 0)
    ot = jnp.zeros((E, 256), f32)
    for t in range(PIECES):
        at = slice(t * HALF, (t + 1) * HALF)
        sm, so = ((sm0, so0), (sm1, so1))[t // 4]
        dh, dl = delta(jnp.where(i < 4, sm[0, t % 4], so[0, t % 4]), lse, rows, lab, t * HALF)
        if t >= 4:
            g_acc[t - 4] += dot(cat([dh, dh, dl], 1), qcat, NN)
        ot += dot(cat([xth[:, at], xtl[:, at], xth[:, at]], 1), cat([dh, dh, dl], 0), NN)
    o = ot.T * (E**-0.5)

    @pl.when(i < 4)
    def _():
        om[2 * i], om[2 * i + 1] = o[:ROWS], o[ROWS:]

    @pl.when(i >= 4)
    def _():
        oo[2 * i - ZN], oo[2 * i - ZN + 1] = o[:ROWS], o[ROWS:]

    @pl.when(i == ZN - 1)
    def _():
        for d in range(4):
            up[d * CUT : (d + 1) * CUT, :] = g_acc[d, :CUT, :]
            down[d * CUT : (d + 1) * CUT, :] = g_acc[d, CUT:, :]
        up[4 * CUT :, :] = down[4 * CUT :, :] = jnp.full((8, E), part[0], f32)


def backward_b_kernel(pos_ref, token, mine, other, lse_ref, sm0, so0, g_ref):
    i = pl.program_id(0)

    @pl.when(i == 0)
    def _():
        g_ref[...] = jnp.zeros_like(g_ref)

    qcat, lab, lse = block(i, pos_ref, lse_ref, mine, other)
    rows = lax.broadcasted_iota(jnp.int32, (HALF, 256), 0)
    for t in range(4):
        dh, dl = delta(jnp.where(i < 4, sm0[0, t], so0[0, t]), lse, rows, lab, t * HALF)
        g_ref[t] += dot(cat([dh, dh, dl], 1), qcat, NN)


Q_SPECS = [
    pl.BlockSpec((2, PAD, E), lambda i: (jnp.minimum(i, 3), 0, 0)),
    pl.BlockSpec((2, PAD, E), lambda i: (jnp.maximum(i, 4) - 4, 0, 0)),
    pl.BlockSpec((2, ZN, ROWS), lambda i: (0, 0, 0)),
]


SM_SPEC = pl.BlockSpec((1, 4, HALF, 256), lambda i: (jnp.minimum(i, 3), 0, 0, 0))
SO_SPEC = pl.BlockSpec((1, 4, HALF, 256), lambda i: (jnp.maximum(i, 4) - 4, 0, 0, 0))


def backward_a(pos, part, xth, xtl, mine, other, lse, *s):
    whole = lambda *dims: pl.BlockSpec(dims, lambda i: (0,) * len(dims))
    return pl.pallas_call(
        backward_a_kernel,
        grid=(ZN,),
        in_specs=[SMEM, SMEM, whole(E, LOCAL), whole(E, LOCAL), *Q_SPECS]
        + [SM_SPEC, SM_SPEC, SO_SPEC, SO_SPEC],
        out_specs=[whole(ZN, ROWS, E)] * 2 + [whole(4 * CUT + 8, E)] * 2 + [SMEM],
        out_shape=[shape(ZN, ROWS, E)] * 2 + [shape(4 * CUT + 8, E)] * 2 + [shape(1)],
        scratch_shapes=[pltpu.VMEM((4, HALF, E), f32)],
        compiler_params=params(14),
        cost_estimate=pl.CostEstimate(flops=9 * 2**30, bytes_accessed=22 * 2**20, transcendentals=2**22),
        name="backward_a",
    )(pos, part, xth, xtl, mine, other, lse, *s)


def backward_b(pos, token, mine, other, lse, *s):
    return pl.pallas_call(
        backward_b_kernel,
        grid=(ZN,),
        in_specs=[SMEM, SMEM, *Q_SPECS, SM_SPEC, SO_SPEC],
        out_specs=pl.BlockSpec((4, HALF, E), lambda i: (0, 0, 0)),
        out_shape=shape(4, HALF, E),
        compiler_params=params(14),
        cost_estimate=pl.CostEstimate(flops=3 * 2**30, bytes_accessed=11 * 2**20, transcendentals=2**21),
        name="backward_b",
    )(pos, token, mine, other, lse, *s)


def gather(qs, own):
    mine = lax.all_to_all(qs, "z", 0, 0, tiled=True)
    y0, x3, x1 = flip(own, 32), send(own, dx=1), send(own, dx=-1)
    y0, x3, x1 = lax.optimization_barrier((y0, x3, x1))
    y3, y1, x2 = send(y0, dx=1), send(y0, dx=-1), send(x3, dx=1)
    y3, y1, x2 = lax.optimization_barrier((y3, y1, x2))
    y2 = send(y1, dx=-1)
    return mine, [own, x1, x2, x3, y0, y1, y2, y3]


def fold_kernel(part, g, a, b, *out):
    for d in range(4):
        at = slice(d * CUT, (d + 1) * CUT)
        out[d][:CUT] = g[d, :CUT] + a[at]
        out[d][CUT:HALF] = g[d, CUT:] + b[at]
        out[d][HALF : HALF + 1] = jnp.full((1, E), part[0], f32)
        out[d][HALF + 1 : HALF + 2] = a[4 * CUT : 4 * CUT + 1]
        out[d][HALF + 2 : HALF + 3] = b[4 * CUT : 4 * CUT + 1]
        out[d][HALF + 3 :] = jnp.zeros((5, E), f32)


def land_kernel(m0, m1, m2, m3, out):
    out[...] = (m0[...] + m2[...]) + (m1[...] + m3[...])


def join_kernel(pos_ref, mine, mine2, other, other2, out, loss):
    c = pos_ref[1]
    out[pl.ds(pl.multiple_of(c * HALF, HALF), HALF), :] = mine[:HALF] + mine2[:HALF]
    out[pl.ds(pl.multiple_of((1 - c) * HALF, HALF), HALF), :] = other[:HALF] + other2[:HALF]
    total = (mine[HALF : HALF + 1] + mine2[HALF : HALF + 1]) + (
        mine[HALF + 1 : HALF + 2] + mine[HALF + 2 : HALF + 3]
    )
    loss[0] = jnp.max(total) / 32768


def sum_kernel(got, out):
    total = got[0]
    for k in range(1, ZN):
        total += got[k]
    out[...] = total


def add_kernel(a, b, out):
    out[...] = a[...] + b[...]


def body(queries, items, labels):
    core, y_lo, x_at, z_at = (lax.axis_index(a) for a in ("c", "yl", "x", "z"))
    pos = jnp.stack([z_at, core, y_lo, x_at]).astype(jnp.int32)
    qs, own = small(
        start_kernel, [pos, queries, labels.reshape(1, ROWS), items], [shape(ZN, PAD, E), shape(HALF, E)]
    )
    mine, parts = gather(qs, own)
    xh, xl, xth, xtl, packed = small(
        pack_items_kernel,
        parts,
        [shape(LOCAL, E, dtype=bf16)] * 2 + [shape(E, LOCAL, dtype=bf16)] * 2 + [shape(1)],
    )
    (mine,) = small(hold_kernel, [packed, mine], [shape(ZN, PAD, E)])
    other = send(mine, dc=1)
    sm0, sm1, stat_m = forward(pos, xh, xl, mine)
    so0, so1, stat_o = forward(pos, xh, xl, other)
    (stats,) = small(spread_kernel, [stat_m, stat_o], [shape(2 * ZN, 2, 3, ZN, ROWS)])
    stats = lax.all_to_all(stats, ("c", "z"), 0, 0, tiled=True)
    lse, part = small(merge_kernel, [pos, stats], [shape(2, ZN, ROWS), shape(1)])
    om, oo, up, down, first = backward_a(pos, part, xth, xtl, mine, other, lse, sm0, sm1, so0, so1)
    a, b = send(up, dy=1), send(down, dy=-1)
    g = backward_b(pos, first, mine, other, lse, sm0, so0)
    (o,) = small(add_kernel, [om, send(oo, dc=1)], [shape(ZN, ROWS, E)])
    o = lax.all_to_all(o, "z", 0, 0, tiled=True)
    m0, m1, m2, m3 = small(fold_kernel, [part, g, a, b], [shape(HALF + 8, E)] * 4)
    m2, m1, m3 = send(m2, dx=2), send(m1, dx=1), send(m3, dx=-1)
    (own,) = small(land_kernel, [m0, m1, m2, m3], [shape(HALF + 8, E)])
    got = send(own, dy=2)
    near = send(own, dc=1)
    item_grad, loss = small(
        join_kernel, [pos, own, got, near, send(got, dc=1)], [shape(2 * HALF, E), shape(1)]
    )
    (query_grad,) = small(sum_kernel, [o], [shape(ROWS, E)])
    return loss.reshape(()), query_grad, item_grad


def solution(mesh):
    grid = Mesh(mesh.devices.reshape(2, 2, 2, 4, 8), AXES)
    corpus = ("yl", "x", "z")
    in_specs = (P(AXES, None), P(corpus, None), P(AXES))
    out_specs = (P(), P(AXES, None), P(corpus, None))
    return jax.shard_map(body, mesh=grid, in_specs=in_specs, out_specs=out_specs, check_vma=False)
```

time: 1450 us -> 157 us (0.11)
  blocking collectives: 841 us -> 19.9 us
  waiting for transfers between devices: 458 us -> 48.7 us
  matrix products: 116 us -> 0 us
  Pallas kernels: 0 us -> 44.2 us
  starting transfers between devices: 0.12 us -> 26.3 us
  between operations: 17 us -> 0.86 us
    psum x2 -> x0, blocking collectives: 376 us -> none  [the longest x1 303 us: body(): whole = lax.psum(totals * jnp.exp(tops - best), 'corpus')]
    pmax x1 -> x0, blocking collectives: 307 us -> none  [body(): best = lax.pmax(tops, 'corpus')]
    reduce_scatter x1 -> x0, waiting for transfers between devices: 298 us -> none  [body(): lax.psum_scatter(grad_blocks.reshape(rows_all, E), 'corpus', scatter_dime...]
    all_gather x1 -> x0, waiting for transfers between devices: 158 us -> none  [body(): lax.all_gather(queries, 'corpus', axis=0, tiled=True)]
    all_gather x1 -> x0, blocking collectives: 157 us -> none  [body(): lax.all_gather(labels, 'corpus', axis=0, tiled=True)]
    dot_general x32 -> x0, matrix products: 116 us -> none  [the longest x16 55.7 us: score_rows(): jnp.dot(query_rows, item_rows.T, precision=lax.Precision.HIGHEST)]
    ppermute x0 -> x17, waiting for transfers between devices: none -> 48.7 us  [the longest x16 48.7 us: send(): return lax.ppermute(a, AXES, pairs(**shift))]
    pallas_call x0 -> x14, Pallas kernels: none -> 44.2 us  [the longest x1 16.7 us: backward_a(): pl.pallas_call(backward_a_kernel, grid=(ZN,), in_specs=[SMEM, SMEM, whole...]
  transfers between devices with their start and end apart: 3 -> 19, of which waited for: 2 -> 12; matrix products, arithmetic and copies ran while one was open for 0% -> 0% of each run, Pallas kernels for 0% -> 11%
where the time goes in v1:
time: 157 us; the launch traced here: 155 us
  waiting for transfers between devices  48.7 us (31%)
  Pallas kernels  44.2 us (28%)
  starting transfers between devices  26.3 us (17%)
  blocking collectives  19.9 us (13%)
  local copies, waits for them, and re-layouts  14.9 us (9%)
    ppermute x16, waiting for transfers between devices, send(): return lax.ppermute(a, AXES, pairs(**shift))  48.7 us
    all_to_all x1, blocking collectives, body(): stats = lax.all_to_all(stats, ('c', 'z'), 0, 0, tiled=True)  19.9 us
    pallas_call x1, Pallas kernels, backward_a(): pl.pallas_call(backward_a_kernel, grid=(ZN,), in_specs=[SMEM, SMEM, whole...  16.7 us
    unnamed x34, local copies, waits for them, and re-layouts  14.9 us
    ppermute x16, starting transfers between devices, send(): return lax.ppermute(a, AXES, pairs(**shift))  12.9 us
    pallas_call x2, Pallas kernels, forward(): pl.pallas_call(forward_kernel, grid=(4,), in_specs=[SMEM, pl.BlockSpec((L...  11.2 us
    pallas_call x10, Pallas kernels, small(): pl.pallas_call(kernel, in_specs=[SMEM if a.ndim == 1 else VMEM for a in i...  8.89 us
    all_to_all x1, starting transfers between devices, gather(): mine = lax.all_to_all(qs, 'z', 0, 0, tiled=True)  8.47 us
  transfers between devices with their start and end apart: 19, of which 12 were waited for; matrix products, arithmetic and copies ran while one was open for 0% of the time, Pallas kernels for 11%

profile of v1, /device:TPU:24, one launch (start us, length us, event | category | flops | bytes accessed | tf_op | source)
XLA Modules:
  0.0 155.0 jit_solution(10866097586011484363)
XLA Ops:
  3.3 1.6 %start_kernel.1 = (f32[8,136,256]{2,1,0:T(8,128)}, f32[256,256]{1,0:T(8,128)S(1)}) custom-call(s32[4]{0:T(128)S(1)} %pad_add_fusion.pos_ref, f32[128,256]{1,0:T(8,128)S(1)} %copy-done.1, s32[1,128]{1,0:T(1,128)S(1)} %bitcast.6, f32[512,256]{1,0:T(8,128)S(1)} %copy-done), custom_call_target="tpu_custom_call" | custom-call | tf_op jit(solution)/shard_map/start_kernel/pallas_call | solution.py:90
  5.0 8.5 %all-to-all-start = ((f32[8,136,256]{2,1,0:T(8,128)}), f32[8,136,256]{2,1,0:T(8,128)S(1)}, u32[]{:S(2)}, u32[]{:S(2)}) async-start(f32[8,136,256]{2,1,0:T(8,128)} %get-tuple-element.45), calls=%async_computation | async-start | bytes 2228224 | tf_op jit(solution)/shard_map/all_to_all | solution.py:303
  13.4 2.8 %collective-permute-start.2 = (f32[256,256]{1,0:T(8,128)S(1)}, f32[256,256]{1,0:T(8,128)S(1)}, u32[]{:S(2)}, u32[]{:S(2)}) collective-permute-start(f32[256,256]{1,0:T(8,128)S(1)} %get-tuple-element.35.refs_0_), channel_id=1, source_target_pairs={{0,24},{1,25},{2,26},{3,27},{4,28},{5,29},{6,30},{7,31},{8,0},{9,1... | collective-permute-start | bytes 786440 | tf_op jit(solution)/shard_map/ppermute | solution.py:38
  16.9 4.5 %collective-permute-done.2.refs_1_ = f32[256,256]{1,0:T(8,128)S(1)} collective-permute-done((f32[256,256]{1,0:T(8,128)S(1)}, f32[256,256]{1,0:T(8,128)S(1)}, u32[]{:S(2)}, u32[]{:S(2)}) %collective-permute-start.2) | collective-permute-done | bytes 262176 | tf_op jit(solution)/shard_map/ppermute | solution.py:38
  21.5 3.4 %collective-permute-done.1.refs_3_ = f32[256,256]{1,0:T(8,128)S(1)} collective-permute-done((f32[256,256]{1,0:T(8,128)S(1)}, f32[256,256]{1,0:T(8,128)S(1)}, u32[]{:S(2)}, u32[]{:S(2)}) %collective-permute-start.1) | collective-permute-done | bytes 262176 | tf_op jit(solution)/shard_map/ppermute | solution.py:38
  24.9 3.2 %collective-permute-start.4 = (f32[256,256]{1,0:T(8,128)S(1)}, f32[256,256]{1,0:T(8,128)S(1)}, u32[]{:S(2)}, u32[]{:S(2)}) collective-permute-start(f32[256,256]{1,0:T(8,128)S(1)} %collective-permute-done.refs_4_), channel_id=1, source_target_pairs={{0,24},{1,25},{2,26},{3,27},{4,28},{5,29},{6,30},{7,31},{8,0},{9,1... | collective-permute-start | bytes 786440 | tf_op jit(solution)/shard_map/ppermute | solution.py:38
  28.1 7.2 %collective-permute-done.5.refs_2_ = f32[256,256]{1,0:T(8,128)S(1)} collective-permute-done((f32[256,256]{1,0:T(8,128)S(1)}, f32[256,256]{1,0:T(8,128)S(1)}, u32[]{:S(2)}, u32[]{:S(2)}) %collective-permute-start.5) | collective-permute-done | bytes 262176 | tf_op jit(solution)/shard_map/ppermute | solution.py:38
  35.3 2.9 %collective-permute-done.3.refs_7_ = f32[256,256]{1,0:T(8,128)S(1)} collective-permute-done((f32[256,256]{1,0:T(8,128)S(1)}, f32[256,256]{1,0:T(8,128)S(1)}, u32[]{:S(2)}, u32[]{:S(2)}) %collective-permute-start.3) | collective-permute-done | bytes 262176 | tf_op jit(solution)/shard_map/ppermute | solution.py:38
  38.5 6.1 %collective-permute-done.6.refs_6_ = f32[256,256]{1,0:T(8,128)S(1)} collective-permute-done((f32[256,256]{1,0:T(8,128)S(1)}, f32[256,256]{1,0:T(8,128)S(1)}, u32[]{:S(2)}, u32[]{:S(2)}) %collective-permute-start.6) | collective-permute-done | bytes 262176 | tf_op jit(solution)/shard_map/ppermute | solution.py:38
  53.1 5.7 %forward.2 = (f32[4,4,256,256]{3,2,1,0:T(8,128)S(1)}, f32[4,4,256,256]{3,2,1,0:T(8,128)S(1)}, f32[3,8,128]{2,1,0:T(8,128)S(1)}) custom-call(s32[4]{0:T(128)S(1)} %pad_add_fusion.pos_ref, bf16[2048,256]{1,0:T(8,128)(2,1)S(1)} %copy-done.8, bf16[2048,256]{1,0:T(8,128)(2,1)S(1)} %copy-done.10, f32[8,136,256]{2,1,0:T(8,128)S(1)} %hold_kernel.1.q_ref.mine), custom_call_target="tpu_custom_call" | custom-call | flops 3221225472 | bytes 10485760 | tf_op jit(solution)/shard_map/forward/pallas_call | solution.py:177
  58.8 5.6 %forward.3 = (f32[4,4,256,256]{3,2,1,0:T(8,128)S(1)}, f32[4,4,256,256]{3,2,1,0:T(8,128)S(1)}, f32[3,8,128]{2,1,0:T(8,128)S(1)}) custom-call(s32[4]{0:T(128)S(1)} %pad_add_fusion.pos_ref, bf16[2048,256]{1,0:T(8,128)(2,1)S(1)} %copy-done.8, bf16[2048,256]{1,0:T(8,128)(2,1)S(1)} %copy-done.10, f32[8,136,256]{2,1,0:T(8,128)S(1)} %collective-permute-done.7.q_ref.other), custom_call_target="tpu_custom_call" | custom-call | flops 3221225472 | bytes 10485760 | tf_op jit(solution)/shard_map/forward/pallas_call | solution.py:177
  64.4 19.9 %all_to_all.15.got = f32[16,2,3,8,128]{4,3,2,1,0:T(8,128)S(1)} all-to-all(f32[16,2,3,8,128]{4,3,2,1,0:T(8,128)S(1)} %spread_kernel.1), channel_id=1, replica_groups=mesh['yh'=2,'c'=2,'yl'=2,'x'=4,'z'=8] {'c','z'}, dimensions={0} | all-to-all | bytes 786432 | tf_op jit(solution)/shard_map/all_to_all | solution.py:365
  85.6 16.7 %backward_a.1 = (f32[8,128,256]{2,1,0:T(8,128)S(1)}, f32[8,128,256]{2,1,0:T(8,128)S(1)}, f32[520,256]{1,0:T(8,128)S(1)}, f32[520,256]{1,0:T(8,128)S(1)}, f32[1]{0:T(128)}) custom-call(s32[4]{0:T(128)S(1)} %pad_add_fusion.pos_ref, f32[1]{0:T(128)} %get-tuple-element.48.part, bf16[256,2048]{1,0:T(8,128)(2,1)S(1)} %copy-done.4, ...), custom_call_target="tpu_custom_call" | custom-call | flops 9663676416 | bytes 23068672 | tf_op jit(solution)/shard_map/backward_a/pallas_call | solution.py:275
  104.0 2.7 %collective-permute-done.16.b = f32[8,128,256]{2,1,0:T(8,128)S(1)} collective-permute-done((f32[8,128,256]{2,1,0:T(8,128)S(1)}, f32[8,128,256]{2,1,0:T(8,128)S(1)}, u32[]{:S(2)}, u32[]{:S(2)}) %collective-permute-start.16) | collective-permute-done | bytes 1048608 | tf_op jit(solution)/shard_map/ppermute | solution.py:38
  107.7 4.2 %all-to-all-start.2 = ((f32[8,128,256]{2,1,0:T(8,128)}), f32[8,128,256]{2,1,0:T(8,128)S(1)}, u32[]{:S(2)}, u32[]{:S(2)}) async-start(f32[8,128,256]{2,1,0:T(8,128)} %add_kernel.1), calls=%async_computation.2 | async-start | bytes 2097152 | tf_op jit(solution)/shard_map/all_to_all | solution.py:371
  112.2 1.8 %collective-permute-start.9 = (f32[520,256]{1,0:T(8,128)}, f32[520,256]{1,0:T(8,128)S(1)}, u32[]{:S(2)}, u32[]{:S(2)}) collective-permute-start(f32[520,256]{1,0:T(8,128)} %copy-done.11), channel_id=1, source_target_pairs={{0,160},{1,161},{2,162},{3,163},{4,164},{5,165},{6,166},{7,167},{8... | collective-permute-start | bytes 1597448 | tf_op jit(solution)/shard_map/ppermute | solution.py:38
  113.9 2.2 %copy-done.14 = f32[4,4,256,256]{3,2,1,0:T(8,128)S(1)} copy-done((f32[4,4,256,256]{3,2,1,0:T(8,128)S(1)}, f32[4,4,256,256]{3,2,1,0:T(8,128)}, u32[]{:S(2)}) %copy-start.14) | copy-done | bytes 4194328
  116.1 2.2 %copy-done.16 = f32[4,4,256,256]{3,2,1,0:T(8,128)S(1)} copy-done((f32[4,4,256,256]{3,2,1,0:T(8,128)S(1)}, f32[4,4,256,256]{3,2,1,0:T(8,128)}, u32[]{:S(2)}) %copy-start.16) | copy-done | bytes 4194328
  118.3 7.3 %backward_b.1.g = f32[4,256,256]{2,1,0:T(8,128)S(1)} custom-call(s32[4]{0:T(128)S(1)} %pad_add_fusion.pos_ref, f32[1]{0:T(128)} %get-tuple-element.56.token, f32[8,136,256]{2,1,0:T(8,128)S(1)} %hold_kernel.1.q_ref.mine, f32[8,136,256]{2,1,0:T(8,128)S(1)} %collective-permute-done.7.q_ref.other, f32[2,8,128]{2,1,0:T(8,128)S(1)} %get-tuple-element.51.lse_ref, ...), custom_call_target="tpu_custom_call" | custom-call | flops 3221225472 | bytes 11534336 | tf_op jit(solution)/shard_map/backward_b/pallas_call | solution.py:290
  128.1 2.9 %collective-permute-start.11 = (f32[264,256]{1,0:T(8,128)S(1)}, f32[264,256]{1,0:T(8,128)S(1)}, u32[]{:S(2)}, u32[]{:S(2)}) collective-permute-start(f32[264,256]{1,0:T(8,128)S(1)} %get-tuple-element.61), channel_id=1, source_target_pairs={{0,16},{1,17},{2,18},{3,19},{4,20},{5,21},{6,22},{7,23},{8,24},{9,... | collective-permute-start | bytes 811016 | tf_op jit(solution)/shard_map/ppermute | solution.py:38
  131.4 10.9 %collective-permute-done.10.m1 = f32[264,256]{1,0:T(8,128)S(1)} collective-permute-done((f32[264,256]{1,0:T(8,128)S(1)}, f32[264,256]{1,0:T(8,128)S(1)}, u32[]{:S(2)}, u32[]{:S(2)}) %collective-permute-start.10) | collective-permute-done | bytes 270368 | tf_op jit(solution)/shard_map/ppermute | solution.py:38
  144.2 7.1 %collective-permute-done.13.mine2 = f32[264,256]{1,0:T(8,128)S(1)} collective-permute-done((f32[264,256]{1,0:T(8,128)S(1)}, f32[264,256]{1,0:T(8,128)S(1)}, u32[]{:S(2)}, u32[]{:S(2)}) %collective-permute-start.13) | collective-permute-done | bytes 270368 | tf_op jit(solution)/shard_map/ppermute | solution.py:38
  151.3 1.5 collective-permute-done.15.other2
  152.8 1.4 join_kernel.1
  (64 shorter events, 21.7 us)
Async XLA Ops:
  5.0 44.8 %all-to-all-start = ((f32[8,136,256]{2,1,0:T(8,128)}), f32[8,136,256]{2,1,0:T(8,128)S(1)}, u32[]{:S(2)}, u32[]{:S(2)}) async-start(f32[8,136,256]{2,1,0:T(8,128)} %get-tuple-element.45), calls=%async_computation | async-start | bytes 2228224 | tf_op jit(solution)/shard_map/all_to_all | solution.py:303
  13.4 8.0 %collective-permute-start.2 = (f32[256,256]{1,0:T(8,128)S(1)}, f32[256,256]{1,0:T(8,128)S(1)}, u32[]{:S(2)}, u32[]{:S(2)}) collective-permute-start(f32[256,256]{1,0:T(8,128)S(1)} %get-tuple-element.35.refs_0_), channel_id=1, source_target_pairs={{0,24},{1,25},{2,26},{3,27},{4,28},{5,29},{6,30},{7,31},{8,0},{9,1... | collective-permute-start | bytes 786440 | tf_op jit(solution)/shard_map/ppermute | solution.py:38
  16.2 8.7 %collective-permute-start.1 = (f32[256,256]{1,0:T(8,128)S(1)}, f32[256,256]{1,0:T(8,128)S(1)}, u32[]{:S(2)}, u32[]{:S(2)}) collective-permute-start(f32[256,256]{1,0:T(8,128)S(1)} %get-tuple-element.35.refs_0_), channel_id=1, source_target_pairs={{0,8},{1,9},{2,10},{3,11},{4,12},{5,13},{6,14},{7,15},{8,16},{9,17... | collective-permute-start | bytes 786440 | tf_op jit(solution)/shard_map/ppermute | solution.py:38
  16.2 8.7 %collective-permute-start = (f32[256,256]{1,0:T(8,128)S(1)}, f32[256,256]{1,0:T(8,128)S(1)}, u32[]{:S(2)}, u32[]{:S(2)}) collective-permute-start(f32[256,256]{1,0:T(8,128)S(1)} %get-tuple-element.35.refs_0_), channel_id=1, source_target_pairs={{0,32},{1,33},{2,34},{3,35},{4,36},{5,37},{6,38},{7,39},{8,40},{9,... | collective-permute-start | bytes 786440 | tf_op jit(solution)/shard_map/ppermute | solution.py:42
  24.9 10.5 %collective-permute-start.5 = (f32[256,256]{1,0:T(8,128)S(1)}, f32[256,256]{1,0:T(8,128)S(1)}, u32[]{:S(2)}, u32[]{:S(2)}) collective-permute-start(f32[256,256]{1,0:T(8,128)S(1)} %collective-permute-done.1.refs_3_), channel_id=1, source_target_pairs={{0,8},{1,9},{2,10},{3,11},{4,12},{5,13},{6,14},{7,15},{8,16},{9,17... | collective-permute-start | bytes 786440 | tf_op jit(solution)/shard_map/ppermute | solution.py:38
  24.9 10.5 %collective-permute-start.4 = (f32[256,256]{1,0:T(8,128)S(1)}, f32[256,256]{1,0:T(8,128)S(1)}, u32[]{:S(2)}, u32[]{:S(2)}) collective-permute-start(f32[256,256]{1,0:T(8,128)S(1)} %collective-permute-done.refs_4_), channel_id=1, source_target_pairs={{0,24},{1,25},{2,26},{3,27},{4,28},{5,29},{6,30},{7,31},{8,0},{9,1... | collective-permute-start | bytes 786440 | tf_op jit(solution)/shard_map/ppermute | solution.py:38
  28.1 10.2 %collective-permute-start.3 = (f32[256,256]{1,0:T(8,128)S(1)}, f32[256,256]{1,0:T(8,128)S(1)}, u32[]{:S(2)}, u32[]{:S(2)}) collective-permute-start(f32[256,256]{1,0:T(8,128)S(1)} %collective-permute-done.refs_4_), channel_id=1, source_target_pairs={{0,8},{1,9},{2,10},{3,11},{4,12},{5,13},{6,14},{7,15},{8,16},{9,17... | collective-permute-start | bytes 786440 | tf_op jit(solution)/shard_map/ppermute | solution.py:38
  38.3 6.4 %collective-permute-start.6 = (f32[256,256]{1,0:T(8,128)S(1)}, f32[256,256]{1,0:T(8,128)S(1)}, u32[]{:S(2)}, u32[]{:S(2)}) collective-permute-start(f32[256,256]{1,0:T(8,128)S(1)} %collective-permute-done.4.refs_5_), channel_id=1, source_target_pairs={{0,24},{1,25},{2,26},{3,27},{4,28},{5,29},{6,30},{7,31},{8,0},{9,1... | collective-permute-start | bytes 786440 | tf_op jit(solution)/shard_map/ppermute | solution.py:38
  50.5 8.2 %collective-permute-start.7 = (f32[8,136,256]{2,1,0:T(8,128)S(1)}, f32[8,136,256]{2,1,0:T(8,128)S(1)}, u32[]{:S(2)}, u32[]{:S(2)}) collective-permute-start(f32[8,136,256]{2,1,0:T(8,128)S(1)} %hold_kernel.1.q_ref.mine), channel_id=1, source_target_pairs={{0,64},{1,65},{2,66},{3,67},{4,68},{5,69},{6,70},{7,71},{8,72},{9,... | collective-permute-start | bytes 3342344 | tf_op jit(solution)/shard_map/ppermute | solution.py:38
  58.8 26.8 %copy-start.13 = (f32[4,4,256,256]{3,2,1,0:T(8,128)}, f32[4,4,256,256]{3,2,1,0:T(8,128)S(1)}, u32[]{:S(2)}) copy-start(f32[4,4,256,256]{3,2,1,0:T(8,128)S(1)} %get-tuple-element.52.sm0) | copy-start | bytes 12582916
  58.8 26.8 %copy-start.4 = (bf16[256,2048]{1,0:T(8,128)(2,1)S(1)}, bf16[256,2048]{1,0:T(8,128)(2,1)}, u32[]{:S(2)}) copy-start(bf16[256,2048]{1,0:T(8,128)(2,1)} %copy-done.3) | copy-start | bytes 3145732
  58.8 26.8 %copy-start.6 = (bf16[256,2048]{1,0:T(8,128)(2,1)S(1)}, bf16[256,2048]{1,0:T(8,128)(2,1)}, u32[]{:S(2)}) copy-start(bf16[256,2048]{1,0:T(8,128)(2,1)} %copy-done.5) | copy-start | bytes 3145732
  64.4 38.0 %copy-start.15 = (f32[4,4,256,256]{3,2,1,0:T(8,128)}, f32[4,4,256,256]{3,2,1,0:T(8,128)S(1)}, u32[]{:S(2)}) copy-start(f32[4,4,256,256]{3,2,1,0:T(8,128)S(1)} %get-tuple-element.54.so0) | copy-start | bytes 12582916
  103.9 2.7 %collective-permute-start.16 = (f32[8,128,256]{2,1,0:T(8,128)S(1)}, f32[8,128,256]{2,1,0:T(8,128)S(1)}, u32[]{:S(2)}, u32[]{:S(2)}) collective-permute-start(f32[8,128,256]{2,1,0:T(8,128)S(1)} %get-tuple-element.65), channel_id=1, source_target_pairs={{0,64},{1,65},{2,66},{3,67},{4,68},{5,69},{6,70},{7,71},{8,72},{9,... | collective-permute-start | bytes 3145736 | tf_op jit(solution)/shard_map/ppermute | solution.py:38
  107.7 46.5 %all-to-all-start.2 = ((f32[8,128,256]{2,1,0:T(8,128)}), f32[8,128,256]{2,1,0:T(8,128)S(1)}, u32[]{:S(2)}, u32[]{:S(2)}) async-start(f32[8,128,256]{2,1,0:T(8,128)} %add_kernel.1), calls=%async_computation.2 | async-start | bytes 2097152 | tf_op jit(solution)/shard_map/all_to_all | solution.py:371
  111.9 14.1 %collective-permute-start.8 = (f32[520,256]{1,0:T(8,128)}, f32[520,256]{1,0:T(8,128)S(1)}, u32[]{:S(2)}, u32[]{:S(2)}) collective-permute-start(f32[520,256]{1,0:T(8,128)} %copy-done.12), channel_id=1, source_target_pairs={{0,32},{1,33},{2,34},{3,35},{4,36},{5,37},{6,38},{7,39},{8,40},{9,... | collective-permute-start | bytes 1597448 | tf_op jit(solution)/shard_map/ppermute | solution.py:38
  112.2 15.1 %collective-permute-start.9 = (f32[520,256]{1,0:T(8,128)}, f32[520,256]{1,0:T(8,128)S(1)}, u32[]{:S(2)}, u32[]{:S(2)}) collective-permute-start(f32[520,256]{1,0:T(8,128)} %copy-done.11), channel_id=1, source_target_pairs={{0,160},{1,161},{2,162},{3,163},{4,164},{5,165},{6,166},{7,167},{8... | collective-permute-start | bytes 1597448 | tf_op jit(solution)/shard_map/ppermute | solution.py:38
  113.9 2.2 %copy-start.14 = (f32[4,4,256,256]{3,2,1,0:T(8,128)S(1)}, f32[4,4,256,256]{3,2,1,0:T(8,128)}, u32[]{:S(2)}) copy-start(f32[4,4,256,256]{3,2,1,0:T(8,128)} %copy-done.13) | copy-start | bytes 12582916
  128.1 14.3 %collective-permute-start.10 = (f32[264,256]{1,0:T(8,128)S(1)}, f32[264,256]{1,0:T(8,128)S(1)}, u32[]{:S(2)}, u32[]{:S(2)}) collective-permute-start(f32[264,256]{1,0:T(8,128)S(1)} %get-tuple-element.60), channel_id=1, source_target_pairs={{0,8},{1,9},{2,10},{3,11},{4,12},{5,13},{6,14},{7,15},{8,16},{9,17... | collective-permute-start | bytes 811016 | tf_op jit(solution)/shard_map/ppermute | solution.py:38
  128.1 14.2 %collective-permute-start.11 = (f32[264,256]{1,0:T(8,128)S(1)}, f32[264,256]{1,0:T(8,128)S(1)}, u32[]{:S(2)}, u32[]{:S(2)}) collective-permute-start(f32[264,256]{1,0:T(8,128)S(1)} %get-tuple-element.61), channel_id=1, source_target_pairs={{0,16},{1,17},{2,18},{3,19},{4,20},{5,21},{6,22},{7,23},{8,24},{9,... | collective-permute-start | bytes 811016 | tf_op jit(solution)/shard_map/ppermute | solution.py:38
  131.1 11.9 %collective-permute-start.12 = (f32[264,256]{1,0:T(8,128)S(1)}, f32[264,256]{1,0:T(8,128)S(1)}, u32[]{:S(2)}, u32[]{:S(2)}) collective-permute-start(f32[264,256]{1,0:T(8,128)S(1)} %get-tuple-element.62), channel_id=1, source_target_pairs={{0,24},{1,25},{2,26},{3,27},{4,28},{5,29},{6,30},{7,31},{8,0},{9,1... | collective-permute-start | bytes 811016 | tf_op jit(solution)/shard_map/ppermute | solution.py:38
  143.0 8.3 %collective-permute-start.13 = (f32[264,256]{1,0:T(8,128)S(1)}, f32[264,256]{1,0:T(8,128)S(1)}, u32[]{:S(2)}, u32[]{:S(2)}) collective-permute-start(f32[264,256]{1,0:T(8,128)S(1)} %land_kernel.1.mine), channel_id=1, source_target_pairs={{0,128},{1,129},{2,130},{3,131},{4,132},{5,133},{6,134},{7,135},{8... | collective-permute-start | bytes 811016 | tf_op jit(solution)/shard_map/ppermute | solution.py:38
  144.2 7.1 %collective-permute-start.14 = (f32[264,256]{1,0:T(8,128)S(1)}, f32[264,256]{1,0:T(8,128)S(1)}, u32[]{:S(2)}, u32[]{:S(2)}) collective-permute-start(f32[264,256]{1,0:T(8,128)S(1)} %land_kernel.1.mine), channel_id=1, source_target_pairs={{0,64},{1,65},{2,66},{3,67},{4,68},{5,69},{6,70},{7,71},{8,72},{9,... | collective-permute-start | bytes 811016 | tf_op jit(solution)/shard_map/ppermute | solution.py:38
  151.3 1.5 collective-permute-start.15
  (12 other events, 12.8 us)

commit v2 on v1

--- a/solution.py
+++ b/solution.py
@@ -42,10 +42,6 @@
     return lax.ppermute(a, AXES, [(i, i ^ bit) for i in range(256)])
 
 
-def after(a, b):
-    return lax.optimization_barrier((a, b))[0]
-
-
 def split(a):
     hi = a.astype(bf16)
     return hi, (a - hi.astype(f32)).astype(bf16)
@@ -61,6 +57,7 @@
 
 NT = ((1,), (1,))
 NN = ((1,), (0,))
+TN = ((0,), (0,))
 SMEM = pl.BlockSpec(memory_space=pltpu.SMEM)
 VMEM = pl.BlockSpec(memory_space=pltpu.VMEM)
 
@@ -106,16 +103,11 @@
 
 
 def pack_items_kernel(*refs):
-    *parts, xh, xl, xth, xtl, token = refs
-    token[0] = 0.0
+    *parts, mine, xh, xl, held = refs
+    held[...] = mine[...]
     for d, p in enumerate(parts):
         at = slice(d * HALF, (d + 1) * HALF)
         xh[at, :], xl[at, :] = split(p[...])
-        xth[:, at], xtl[:, at] = split(p[...].T)
-
-
-def hold_kernel(token, a, out):
-    out[...] = a[...]
 
 
 def spread_kernel(mine, other, out):
@@ -195,21 +187,32 @@
     )(pos, xh, xl, q)
 
 
+def block(i, pos_ref, lse_ref, side, q_ref):
+    qh, ql = split(query_rows(q_ref))
+    lse = cat([lse_ref[side, pl.ds(2 * i, 1), :], lse_ref[side, pl.ds(2 * i + 1, 1), :]], 1)
+    return cat([qh, ql, qh], 0), local_labels(pos_ref, q_ref), lse
+
+
 def delta(s, lse, rows, lab, at):
     p = jnp.exp(s - lse)
     return split(jnp.where(rows == lab - at, p - 1.0, p))
 
 
-def block(i, pos_ref, lse_ref, mine, other):
-    q = jnp.where(i < 4, mine[...], other[...])
-    qh, ql = split(query_rows(q))
-    z = 2 * (i & 3)
-    k = i >> 2
-    lse = cat([lse_ref[k, pl.ds(z, 1), :], lse_ref[k, pl.ds(z + 1, 1), :]], 1)
-    return cat([qh, ql, qh], 0), local_labels(pos_ref, q), lse
-
-
-def backward_a_kernel(pos_ref, part, xth, xtl, mine, other, lse_ref, sm0, sm1, so0, so1, om, oo, up, down, token, g_acc):
+def gradients(g_acc, x, s, operands, first, count, tiles):
+    qcat, lab, lse = operands
+    rows = lax.broadcasted_iota(jnp.int32, (HALF, 256), 0)
+    o = jnp.zeros((256, E), f32)
+    for t in tiles:
+        at = slice(t * HALF, (t + 1) * HALF)
+        dh, dl = delta(s[t // 4][0, t % 4], lse, rows, lab, t * HALF)
+        if first <= t < first + count:
+            g_acc[t - first] += dot(cat([dh, dh, dl], 1), qcat, NN)
+        if x is not None:
+            o += dot(cat([dh, dh, dl], 0), cat([x[0][at], x[1][at], x[0][at]], 0), TN)
+    return o * (E**-0.5)
+
+
+def backward_a_kernel(pos_ref, part, xh, xl, mine, other, lse_ref, sm1, so0, so1, oo, up, down, token, g_acc):
     i = pl.program_id(0)
 
     @pl.when(i == 0)
@@ -217,25 +220,16 @@
         g_acc[...] = jnp.zeros_like(g_acc)
         token[0] = 0.0
 
-    qcat, lab, lse = block(i, pos_ref, lse_ref, mine, other)
-    rows = lax.broadcasted_iota(jnp.int32, (HALF, 256), 0)
-    ot = jnp.zeros((E, 256), f32)
-    for t in range(PIECES):
-        at = slice(t * HALF, (t + 1) * HALF)
-        sm, so = ((sm0, so0), (sm1, so1))[t // 4]
-        dh, dl = delta(jnp.where(i < 4, sm[0, t % 4], so[0, t % 4]), lse, rows, lab, t * HALF)
-        if t >= 4:
-            g_acc[t - 4] += dot(cat([dh, dh, dl], 1), qcat, NN)
-        ot += dot(cat([xth[:, at], xtl[:, at], xth[:, at]], 1), cat([dh, dh, dl], 0), NN)
-    o = ot.T * (E**-0.5)
-
     @pl.when(i < 4)
     def _():
-        om[2 * i], om[2 * i + 1] = o[:ROWS], o[ROWS:]
+        operands = block(i, pos_ref, lse_ref, 0, mine)
+        gradients(g_acc, None, (None, sm1), operands, 4, 4, range(4, 8))
 
     @pl.when(i >= 4)
     def _():
-        oo[2 * i - ZN], oo[2 * i - ZN + 1] = o[:ROWS], o[ROWS:]
+        operands = block(i - 4, pos_ref, lse_ref, 1, other)
+        o = gradients(g_acc, (xh, xl), (so0, so1), operands, 4, 4, range(8))
+        oo[0], oo[1] = o[:ROWS], o[ROWS:]
 
     @pl.when(i == ZN - 1)
     def _():
@@ -245,58 +239,69 @@
         up[4 * CUT :, :] = down[4 * CUT :, :] = jnp.full((8, E), part[0], f32)
 
 
-def backward_b_kernel(pos_ref, token, mine, other, lse_ref, sm0, so0, g_ref):
+def backward_b_kernel(pos_ref, token, xh, xl, mine, other, lse_ref, sm0, sm1, so0, got, om, g_ref):
     i = pl.program_id(0)
 
     @pl.when(i == 0)
     def _():
         g_ref[...] = jnp.zeros_like(g_ref)
 
-    qcat, lab, lse = block(i, pos_ref, lse_ref, mine, other)
-    rows = lax.broadcasted_iota(jnp.int32, (HALF, 256), 0)
-    for t in range(4):
-        dh, dl = delta(jnp.where(i < 4, sm0[0, t], so0[0, t]), lse, rows, lab, t * HALF)
-        g_ref[t] += dot(cat([dh, dh, dl], 1), qcat, NN)
-
-
-Q_SPECS = [
-    pl.BlockSpec((2, PAD, E), lambda i: (jnp.minimum(i, 3), 0, 0)),
-    pl.BlockSpec((2, PAD, E), lambda i: (jnp.maximum(i, 4) - 4, 0, 0)),
-    pl.BlockSpec((2, ZN, ROWS), lambda i: (0, 0, 0)),
-]
-
-
-SM_SPEC = pl.BlockSpec((1, 4, HALF, 256), lambda i: (jnp.minimum(i, 3), 0, 0, 0))
-SO_SPEC = pl.BlockSpec((1, 4, HALF, 256), lambda i: (jnp.maximum(i, 4) - 4, 0, 0, 0))
-
-
-def backward_a(pos, part, xth, xtl, mine, other, lse, *s):
-    whole = lambda *dims: pl.BlockSpec(dims, lambda i: (0,) * len(dims))
+    @pl.when(i < 4)
+    def _():
+        operands = block(i, pos_ref, lse_ref, 1, other)
+        gradients(g_ref, None, (so0, None), operands, 0, 4, range(4))
+
+    @pl.when(i >= 4)
+    def _():
+        operands = block(i - 4, pos_ref, lse_ref, 0, mine)
+        o = gradients(g_ref, (xh, xl), (sm0, sm1), operands, 0, 4, range(8))
+        om[0], om[1] = o[:ROWS] + got[0], o[ROWS:] + got[1]
+
+
+def whole(*dims):
+    return pl.BlockSpec(dims, lambda i: (0,) * len(dims))
+
+
+def early(*dims):
+    return pl.BlockSpec(dims, lambda i: (jnp.minimum(i, 3),) + (0,) * (len(dims) - 1))
+
+
+def late(*dims):
+    return pl.BlockSpec(dims, lambda i: (jnp.maximum(i, 4) - 4,) + (0,) * (len(dims) - 1))
+
+
+X_SPEC = whole(LOCAL, E)
+Q = (2, PAD, E)
+S = (1, 4, HALF, 256)
+
+
+def backward_a(pos, part, xh, xl, mine, other, lse, *s):
     return pl.pallas_call(
         backward_a_kernel,
         grid=(ZN,),
-        in_specs=[SMEM, SMEM, whole(E, LOCAL), whole(E, LOCAL), *Q_SPECS]
-        + [SM_SPEC, SM_SPEC, SO_SPEC, SO_SPEC],
-        out_specs=[whole(ZN, ROWS, E)] * 2 + [whole(4 * CUT + 8, E)] * 2 + [SMEM],
-        out_shape=[shape(ZN, ROWS, E)] * 2 + [shape(4 * CUT + 8, E)] * 2 + [shape(1)],
+        in_specs=[SMEM, SMEM, X_SPEC, X_SPEC, early(*Q), late(*Q), whole(2, ZN, ROWS)]
+        + [early(*S), late(*S), late(*S)],
+        out_specs=[late(2, ROWS, E)] + [whole(4 * CUT + 8, E)] * 2 + [SMEM],
+        out_shape=[shape(ZN, ROWS, E)] + [shape(4 * CUT + 8, E)] * 2 + [shape(1)],
         scratch_shapes=[pltpu.VMEM((4, HALF, E), f32)],
         compiler_params=params(14),
-        cost_estimate=pl.CostEstimate(flops=9 * 2**30, bytes_accessed=22 * 2**20, transcendentals=2**22),
+        cost_estimate=pl.CostEstimate(flops=6 * 2**30, bytes_accessed=16 * 2**20, transcendentals=3 * 2**20),
         name="backward_a",
-    )(pos, part, xth, xtl, mine, other, lse, *s)
-
-
-def backward_b(pos, token, mine, other, lse, *s):
+    )(pos, part, xh, xl, mine, other, lse, *s)
+
+
+def backward_b(pos, token, xh, xl, mine, other, lse, *s):
     return pl.pallas_call(
         backward_b_kernel,
         grid=(ZN,),
-        in_specs=[SMEM, SMEM, *Q_SPECS, SM_SPEC, SO_SPEC],
-        out_specs=pl.BlockSpec((4, HALF, E), lambda i: (0, 0, 0)),
-        out_shape=shape(4, HALF, E),
+        in_specs=[SMEM, SMEM, X_SPEC, X_SPEC, late(*Q), early(*Q), whole(2, ZN, ROWS)]
+        + [late(*S), late(*S), early(*S), late(2, ROWS, E)],
+        out_specs=[late(2, ROWS, E), whole(4, HALF, E)],
+        out_shape=[shape(ZN, ROWS, E), shape(4, HALF, E)],
         compiler_params=params(14),
-        cost_estimate=pl.CostEstimate(flops=3 * 2**30, bytes_accessed=11 * 2**20, transcendentals=2**21),
+        cost_estimate=pl.CostEstimate(flops=6 * 2**30, bytes_accessed=16 * 2**20, transcendentals=3 * 2**20),
         name="backward_b",
-    )(pos, token, mine, other, lse, *s)
+    )(pos, token, xh, xl, mine, other, lse, *s)
 
 
 def gather(qs, own):
@@ -309,7 +314,8 @@
     return mine, [own, x1, x2, x3, y0, y1, y2, y3]
 
 
-def fold_kernel(part, g, a, b, *out):
+def fold_kernel(part, g, a, b, o, held, *out):
+    held[...] = o[...]
     for d in range(4):
         at = slice(d * CUT, (d + 1) * CUT)
         out[d][:CUT] = g[d, :CUT] + a[at]
@@ -341,10 +347,6 @@
     out[...] = total
 
 
-def add_kernel(a, b, out):
-    out[...] = a[...] + b[...]
-
-
 def body(queries, items, labels):
     core, y_lo, x_at, z_at = (lax.axis_index(a) for a in ("c", "yl", "x", "z"))
     pos = jnp.stack([z_at, core, y_lo, x_at]).astype(jnp.int32)
@@ -352,24 +354,20 @@
         start_kernel, [pos, queries, labels.reshape(1, ROWS), items], [shape(ZN, PAD, E), shape(HALF, E)]
     )
     mine, parts = gather(qs, own)
-    xh, xl, xth, xtl, packed = small(
-        pack_items_kernel,
-        parts,
-        [shape(LOCAL, E, dtype=bf16)] * 2 + [shape(E, LOCAL, dtype=bf16)] * 2 + [shape(1)],
+    xh, xl, mine = small(
+        pack_items_kernel, parts + [mine], [shape(LOCAL, E, dtype=bf16)] * 2 + [shape(ZN, PAD, E)]
     )
-    (mine,) = small(hold_kernel, [packed, mine], [shape(ZN, PAD, E)])
     other = send(mine, dc=1)
     sm0, sm1, stat_m = forward(pos, xh, xl, mine)
     so0, so1, stat_o = forward(pos, xh, xl, other)
     (stats,) = small(spread_kernel, [stat_m, stat_o], [shape(2 * ZN, 2, 3, ZN, ROWS)])
     stats = lax.all_to_all(stats, ("c", "z"), 0, 0, tiled=True)
     lse, part = small(merge_kernel, [pos, stats], [shape(2, ZN, ROWS), shape(1)])
-    om, oo, up, down, first = backward_a(pos, part, xth, xtl, mine, other, lse, sm0, sm1, so0, so1)
+    oo, up, down, first = backward_a(pos, part, xh, xl, mine, other, lse, sm1, so0, so1)
     a, b = send(up, dy=1), send(down, dy=-1)
-    g = backward_b(pos, first, mine, other, lse, sm0, so0)
-    (o,) = small(add_kernel, [om, send(oo, dc=1)], [shape(ZN, ROWS, E)])
+    o, g = backward_b(pos, first, xh, xl, mine, other, lse, sm0, sm1, so0, send(oo, dc=1))
+    o, m0, m1, m2, m3 = small(fold_kernel, [part, g, a, b, o], [shape(ZN, ROWS, E)] + [shape(HALF + 8, E)] * 4)
     o = lax.all_to_all(o, "z", 0, 0, tiled=True)
-    m0, m1, m2, m3 = small(fold_kernel, [part, g, a, b], [shape(HALF + 8, E)] * 4)
     m2, m1, m3 = send(m2, dx=2), send(m1, dx=1), send(m3, dx=-1)
     (own,) = small(land_kernel, [m0, m1, m2, m3], [shape(HALF + 8, E)])
     got = send(own, dy=2)

time: 157 us -> 141 us (0.90)
  local copies, waits for them, and re-layouts: 14.9 us -> 2.6 us
  Pallas kernels: 44.2 us -> 40 us
    unnamed x34 -> x6, local copies, waits for them, and re-layouts: 14.9 us -> 2.6 us
    pallas_call x2, Pallas kernels: 24.1 us -> 21.6 us  [the longest x1 11.2 us: backward_a(): pl.pallas_call(backward_a_kernel, grid=(ZN,), in_specs=[SMEM, SMEM, X_SPE...]
    all_to_all x1, waiting for transfers between devices: 0.01 us -> 1.85 us  [body(): o = lax.all_to_all(o, 'z', 0, 0, tiled=True)]
    pallas_call x10 -> x8, Pallas kernels: 8.89 us -> 7.3 us  [small(): pl.pallas_call(kernel, in_specs=[SMEM if a.ndim == 1 else VMEM for a in i...]
  transfers between devices with their start and end apart: 19 -> 19, of which waited for: 12 -> 13; matrix products, arithmetic and copies ran while one was open for 0% -> 0% of each run, Pallas kernels for 11% -> 13%
where the time goes in v2:
time: 141 us; the launch traced here: 139 us
  waiting for transfers between devices  49.3 us (35%)
  Pallas kernels  40 us (28%)
  starting transfers between devices  26.5 us (19%)
  blocking collectives  19.9 us (14%)
  local copies, waits for them, and re-layouts  2.6 us (2%)
    ppermute x16, waiting for transfers between devices, send(): return lax.ppermute(a, AXES, pairs(**shift))  47.4 us
    all_to_all x1, blocking collectives, body(): stats = lax.all_to_all(stats, ('c', 'z'), 0, 0, tiled=True)  19.9 us
    ppermute x16, starting transfers between devices, send(): return lax.ppermute(a, AXES, pairs(**shift))  13.3 us
    pallas_call x1, Pallas kernels, backward_a(): pl.pallas_call(backward_a_kernel, grid=(ZN,), in_specs=[SMEM, SMEM, X_SPE...  11.2 us
    pallas_call x2, Pallas kernels, forward(): pl.pallas_call(forward_kernel, grid=(4,), in_specs=[SMEM, pl.BlockSpec((L...  11 us
    pallas_call x1, Pallas kernels, backward_b(): pl.pallas_call(backward_b_kernel, grid=(ZN,), in_specs=[SMEM, SMEM, X_SPE...  10.4 us
    all_to_all x1, starting transfers between devices, gather(): mine = lax.all_to_all(qs, 'z', 0, 0, tiled=True)  8.47 us
    pallas_call x8, Pallas kernels, small(): pl.pallas_call(kernel, in_specs=[SMEM if a.ndim == 1 else VMEM for a in i...  7.3 us
  transfers between devices with their start and end apart: 19, of which 13 were waited for; matrix products, arithmetic and copies ran while one was open for 0% of the time, Pallas kernels for 13%

profile of v2, /device:TPU:24, one launch (start us, length us, event | category | flops | bytes accessed | tf_op | source)
XLA Modules:
  0.0 139.1 jit_solution(8706101832728213380)
XLA Ops:
  3.3 1.6 %start_kernel.1 = (f32[8,136,256]{2,1,0:T(8,128)}, f32[256,256]{1,0:T(8,128)S(1)}) custom-call(s32[4]{0:T(128)S(1)} %pad_add_fusion.pos_ref, f32[128,256]{1,0:T(8,128)S(1)} %copy-done.1, s32[1,128]{1,0:T(1,128)S(1)} %bitcast.6, f32[512,256]{1,0:T(8,128)S(1)} %copy-done), custom_call_target="tpu_custom_call" | custom-call | tf_op jit(solution)/shard_map/start_kernel/pallas_call | solution.py:87
  5.0 8.5 %all-to-all-start = ((f32[8,136,256]{2,1,0:T(8,128)}), f32[8,136,256]{2,1,0:T(8,128)S(1)}, u32[]{:S(2)}, u32[]{:S(2)}) async-start(f32[8,136,256]{2,1,0:T(8,128)} %get-tuple-element.42), calls=%async_computation | async-start | bytes 2228224 | tf_op jit(solution)/shard_map/all_to_all | solution.py:308
  13.4 2.8 %collective-permute-start.2 = (f32[256,256]{1,0:T(8,128)S(1)}, f32[256,256]{1,0:T(8,128)S(1)}, u32[]{:S(2)}, u32[]{:S(2)}) collective-permute-start(f32[256,256]{1,0:T(8,128)S(1)} %get-tuple-element.35.refs_0_), channel_id=1, source_target_pairs={{0,24},{1,25},{2,26},{3,27},{4,28},{5,29},{6,30},{7,31},{8,0},{9,1... | collective-permute-start | bytes 786440 | tf_op jit(solution)/shard_map/ppermute | solution.py:38
  16.9 4.5 %collective-permute-done.2.refs_1_ = f32[256,256]{1,0:T(8,128)S(1)} collective-permute-done((f32[256,256]{1,0:T(8,128)S(1)}, f32[256,256]{1,0:T(8,128)S(1)}, u32[]{:S(2)}, u32[]{:S(2)}) %collective-permute-start.2) | collective-permute-done | bytes 262176 | tf_op jit(solution)/shard_map/ppermute | solution.py:38
  21.5 3.4 %collective-permute-done.1.refs_3_ = f32[256,256]{1,0:T(8,128)S(1)} collective-permute-done((f32[256,256]{1,0:T(8,128)S(1)}, f32[256,256]{1,0:T(8,128)S(1)}, u32[]{:S(2)}, u32[]{:S(2)}) %collective-permute-start.1) | collective-permute-done | bytes 262176 | tf_op jit(solution)/shard_map/ppermute | solution.py:38
  24.9 3.2 %collective-permute-start.4 = (f32[256,256]{1,0:T(8,128)S(1)}, f32[256,256]{1,0:T(8,128)S(1)}, u32[]{:S(2)}, u32[]{:S(2)}) collective-permute-start(f32[256,256]{1,0:T(8,128)S(1)} %collective-permute-done.refs_4_), channel_id=1, source_target_pairs={{0,24},{1,25},{2,26},{3,27},{4,28},{5,29},{6,30},{7,31},{8,0},{9,1... | collective-permute-start | bytes 786440 | tf_op jit(solution)/shard_map/ppermute | solution.py:38
  28.1 7.2 %collective-permute-done.5.refs_2_ = f32[256,256]{1,0:T(8,128)S(1)} collective-permute-done((f32[256,256]{1,0:T(8,128)S(1)}, f32[256,256]{1,0:T(8,128)S(1)}, u32[]{:S(2)}, u32[]{:S(2)}) %collective-permute-start.5) | collective-permute-done | bytes 262176 | tf_op jit(solution)/shard_map/ppermute | solution.py:38
  35.3 2.9 %collective-permute-done.3.refs_7_ = f32[256,256]{1,0:T(8,128)S(1)} collective-permute-done((f32[256,256]{1,0:T(8,128)S(1)}, f32[256,256]{1,0:T(8,128)S(1)}, u32[]{:S(2)}, u32[]{:S(2)}) %collective-permute-start.3) | collective-permute-done | bytes 262176 | tf_op jit(solution)/shard_map/ppermute | solution.py:38
  38.5 6.1 %collective-permute-done.6.refs_6_ = f32[256,256]{1,0:T(8,128)S(1)} collective-permute-done((f32[256,256]{1,0:T(8,128)S(1)}, f32[256,256]{1,0:T(8,128)S(1)}, u32[]{:S(2)}, u32[]{:S(2)}) %collective-permute-start.6) | collective-permute-done | bytes 262176 | tf_op jit(solution)/shard_map/ppermute | solution.py:38
  45.1 5.5 %forward.2 = (f32[4,4,256,256]{3,2,1,0:T(8,128)S(1)}, f32[4,4,256,256]{3,2,1,0:T(8,128)S(1)}, f32[3,8,128]{2,1,0:T(8,128)S(1)}) custom-call(s32[4]{0:T(128)S(1)} %pad_add_fusion.pos_ref, bf16[2048,256]{1,0:T(8,128)(2,1)S(1)} %get-tuple-element.43.xh, bf16[2048,256]{1,0:T(8,128)(2,1)S(1)} %get-tuple-element.44.xl, f32[8,136,256]{2,1,0:T(8,128)S(1)} %get-tuple-element.45.q_ref.mine), custom_call_target="tpu_custom_call" | custom-call | flops 3221225472 | bytes 10485760 | tf_op jit(solution)/shard_map/forward/pallas_call | solution.py:169
  50.7 5.6 %forward.3 = (f32[4,4,256,256]{3,2,1,0:T(8,128)S(1)}, f32[4,4,256,256]{3,2,1,0:T(8,128)S(1)}, f32[3,8,128]{2,1,0:T(8,128)S(1)}) custom-call(s32[4]{0:T(128)S(1)} %pad_add_fusion.pos_ref, bf16[2048,256]{1,0:T(8,128)(2,1)S(1)} %get-tuple-element.43.xh, bf16[2048,256]{1,0:T(8,128)(2,1)S(1)} %get-tuple-element.44.xl, ...), custom_call_target="tpu_custom_call" | custom-call | flops 3221225472 | bytes 10485760 | tf_op jit(solution)/shard_map/forward/pallas_call | solution.py:169
  56.3 19.9 %all_to_all.15.got = f32[16,2,3,8,128]{4,3,2,1,0:T(8,128)S(1)} all-to-all(f32[16,2,3,8,128]{4,3,2,1,0:T(8,128)S(1)} %spread_kernel.1), channel_id=1, replica_groups=mesh['yh'=2,'c'=2,'yl'=2,'x'=4,'z'=8] {'c','z'}, dimensions={0} | all-to-all | bytes 786432 | tf_op jit(solution)/shard_map/all_to_all | solution.py:364
  77.4 11.2 %backward_a.1 = (f32[8,128,256]{2,1,0:T(8,128)S(1)}, f32[520,256]{1,0:T(8,128)S(1)}, f32[520,256]{1,0:T(8,128)S(1)}, f32[1]{0:T(128)}) custom-call(s32[4]{0:T(128)S(1)} %pad_add_fusion.pos_ref, f32[1]{0:T(128)} %get-tuple-element.48.part, bf16[2048,256]{1,0:T(8,128)(2,1)S(1)} %get-tuple-element.43.xh, bf16[2048,256]{1,0:T(8,128)(2,1)S(1)} %get-tuple-element.44.xl, ...), custom_call_target="tpu_custom_call" | custom-call | flops 6442450944 | bytes 16777216 | tf_op jit(solution)/shard_map/backward_a/pallas_call | solution.py:279
  89.2 1.8 %collective-permute-start.10 = (f32[520,256]{1,0:T(8,128)S(1)}, f32[520,256]{1,0:T(8,128)S(1)}, u32[]{:S(2)}, u32[]{:S(2)}) collective-permute-start(f32[520,256]{1,0:T(8,128)S(1)} %get-tuple-element.58), channel_id=1, source_target_pairs={{0,160},{1,161},{2,162},{3,163},{4,164},{5,165},{6,166},{7,167},{8... | collective-permute-start | bytes 1597448 | tf_op jit(solution)/shard_map/ppermute | solution.py:38
  91.4 10.4 %backward_b.1 = (f32[8,128,256]{2,1,0:T(8,128)S(1)}, f32[4,256,256]{2,1,0:T(8,128)S(1)}) custom-call(s32[4]{0:T(128)S(1)} %pad_add_fusion.pos_ref, f32[1]{0:T(128)} %get-tuple-element.53.token, bf16[2048,256]{1,0:T(8,128)(2,1)S(1)} %get-tuple-element.43.xh, bf16[2048,256]{1,0:T(8,128)(2,1)S(1)} %get-tuple-element.44.xl, ...), custom_call_target="tpu_custom_call" | custom-call | flops 6442450944 | bytes 16777216 | tf_op jit(solution)/shard_map/backward_b/pallas_call | solution.py:294
  101.8 1.4 %collective-permute-done.9.a = f32[520,256]{1,0:T(8,128)S(1)} collective-permute-done((f32[520,256]{1,0:T(8,128)S(1)}, f32[520,256]{1,0:T(8,128)S(1)}, u32[]{:S(2)}, u32[]{:S(2)}) %collective-permute-start.9) | collective-permute-done | bytes 532512 | tf_op jit(solution)/shard_map/ppermute | solution.py:38
  104.4 1.8 %fold_kernel.1 = (f32[8,128,256]{2,1,0:T(8,128)}, f32[264,256]{1,0:T(8,128)S(1)}, f32[264,256]{1,0:T(8,128)S(1)}, f32[264,256]{1,0:T(8,128)S(1)}, f32[264,256]{1,0:T(8,128)S(1)}) custom-call(f32[1]{0:T(128)} %get-tuple-element.48.part, f32[4,256,256]{2,1,0:T(8,128)S(1)} %get-tuple-element.56.g, f32[520,256]{1,0:T(8,128)S(1)} %collective-permute-done.9.a, ...), custom_call_target="tpu_custom_call" | custom-call | tf_op jit(solution)/shard_map/fold_kernel/pallas_call | solution.py:87
  106.3 4.0 %all-to-all-start.2 = ((f32[8,128,256]{2,1,0:T(8,128)}), f32[8,128,256]{2,1,0:T(8,128)S(1)}, u32[]{:S(2)}, u32[]{:S(2)}) async-start(f32[8,128,256]{2,1,0:T(8,128)} %get-tuple-element.65), calls=%async_computation.2 | async-start | bytes 2097152 | tf_op jit(solution)/shard_map/all_to_all | solution.py:370
  110.3 2.9 %collective-permute-start.12 = (f32[264,256]{1,0:T(8,128)S(1)}, f32[264,256]{1,0:T(8,128)S(1)}, u32[]{:S(2)}, u32[]{:S(2)}) collective-permute-start(f32[264,256]{1,0:T(8,128)S(1)} %get-tuple-element.62), channel_id=1, source_target_pairs={{0,16},{1,17},{2,18},{3,19},{4,20},{5,21},{6,22},{7,23},{8,24},{9,... | collective-permute-start | bytes 811016 | tf_op jit(solution)/shard_map/ppermute | solution.py:38
  113.5 11.1 %collective-permute-done.11.m1 = f32[264,256]{1,0:T(8,128)S(1)} collective-permute-done((f32[264,256]{1,0:T(8,128)S(1)}, f32[264,256]{1,0:T(8,128)S(1)}, u32[]{:S(2)}, u32[]{:S(2)}) %collective-permute-start.11) | collective-permute-done | bytes 270368 | tf_op jit(solution)/shard_map/ppermute | solution.py:38
  126.6 7.0 %collective-permute-done.14.mine2 = f32[264,256]{1,0:T(8,128)S(1)} collective-permute-done((f32[264,256]{1,0:T(8,128)S(1)}, f32[264,256]{1,0:T(8,128)S(1)}, u32[]{:S(2)}, u32[]{:S(2)}) %collective-permute-start.14) | collective-permute-done | bytes 270368 | tf_op jit(solution)/shard_map/ppermute | solution.py:38
  133.6 1.5 %collective-permute-done.16.other2 = f32[264,256]{1,0:T(8,128)S(1)} collective-permute-done((f32[264,256]{1,0:T(8,128)S(1)}, f32[264,256]{1,0:T(8,128)S(1)}, u32[]{:S(2)}, u32[]{:S(2)}) %collective-permute-start.16) | collective-permute-done | bytes 270368 | tf_op jit(solution)/shard_map/ppermute | solution.py:38
  135.1 1.4 %join_kernel.1 = (f32[512,256]{1,0:T(8,128)}, f32[1]{0:T(128)}) custom-call(s32[4]{0:T(128)S(1)} %pad_add_fusion.pos_ref, f32[264,256]{1,0:T(8,128)S(1)} %land_kernel.1.mine, f32[264,256]{1,0:T(8,128)S(1)} %collective-permute-done.14.mine2, f32[264,256]{1,0:T(8,128)S(1)} %collective-permute-done.15.other, f32[264,256]{1,0:T(8,128)S(1)} %collective-permute-done.16.other2), custom_call_target="tpu_custom_call" | custom-call | tf_op jit(solution)/shard_map/join_kernel/pallas_call | solution.py:87
  136.5 1.8 %all-to-all-done.2.got = f32[8,128,256]{2,1,0:T(8,128)S(1)} async-done(((f32[8,128,256]{2,1,0:T(8,128)}), f32[8,128,256]{2,1,0:T(8,128)S(1)}, u32[]{:S(2)}, u32[]{:S(2)}) %all-to-all-start.2) | async-done | bytes 1048608 | tf_op jit(solution)/shard_map/all_to_all | solution.py:370
  (34 shorter events, 10.6 us)
Async XLA Ops:
  0.7 1.0 copy-start
  1.8 0.9 copy-start.1
  2.7 0.7 copy-start.2
  5.0 39.7 %all-to-all-start = ((f32[8,136,256]{2,1,0:T(8,128)}), f32[8,136,256]{2,1,0:T(8,128)S(1)}, u32[]{:S(2)}, u32[]{:S(2)}) async-start(f32[8,136,256]{2,1,0:T(8,128)} %get-tuple-element.42), calls=%async_computation | async-start | bytes 2228224 | tf_op jit(solution)/shard_map/all_to_all | solution.py:308
  13.4 8.0 %collective-permute-start.2 = (f32[256,256]{1,0:T(8,128)S(1)}, f32[256,256]{1,0:T(8,128)S(1)}, u32[]{:S(2)}, u32[]{:S(2)}) collective-permute-start(f32[256,256]{1,0:T(8,128)S(1)} %get-tuple-element.35.refs_0_), channel_id=1, source_target_pairs={{0,24},{1,25},{2,26},{3,27},{4,28},{5,29},{6,30},{7,31},{8,0},{9,1... | collective-permute-start | bytes 786440 | tf_op jit(solution)/shard_map/ppermute | solution.py:38
  16.2 8.7 %collective-permute-start.1 = (f32[256,256]{1,0:T(8,128)S(1)}, f32[256,256]{1,0:T(8,128)S(1)}, u32[]{:S(2)}, u32[]{:S(2)}) collective-permute-start(f32[256,256]{1,0:T(8,128)S(1)} %get-tuple-element.35.refs_0_), channel_id=1, source_target_pairs={{0,8},{1,9},{2,10},{3,11},{4,12},{5,13},{6,14},{7,15},{8,16},{9,17... | collective-permute-start | bytes 786440 | tf_op jit(solution)/shard_map/ppermute | solution.py:38
  16.2 8.7 %collective-permute-start = (f32[256,256]{1,0:T(8,128)S(1)}, f32[256,256]{1,0:T(8,128)S(1)}, u32[]{:S(2)}, u32[]{:S(2)}) collective-permute-start(f32[256,256]{1,0:T(8,128)S(1)} %get-tuple-element.35.refs_0_), channel_id=1, source_target_pairs={{0,32},{1,33},{2,34},{3,35},{4,36},{5,37},{6,38},{7,39},{8,40},{9,... | collective-permute-start | bytes 786440 | tf_op jit(solution)/shard_map/ppermute | solution.py:42
  24.9 10.5 %collective-permute-start.5 = (f32[256,256]{1,0:T(8,128)S(1)}, f32[256,256]{1,0:T(8,128)S(1)}, u32[]{:S(2)}, u32[]{:S(2)}) collective-permute-start(f32[256,256]{1,0:T(8,128)S(1)} %collective-permute-done.1.refs_3_), channel_id=1, source_target_pairs={{0,8},{1,9},{2,10},{3,11},{4,12},{5,13},{6,14},{7,15},{8,16},{9,17... | collective-permute-start | bytes 786440 | tf_op jit(solution)/shard_map/ppermute | solution.py:38
  24.9 10.5 %collective-permute-start.4 = (f32[256,256]{1,0:T(8,128)S(1)}, f32[256,256]{1,0:T(8,128)S(1)}, u32[]{:S(2)}, u32[]{:S(2)}) collective-permute-start(f32[256,256]{1,0:T(8,128)S(1)} %collective-permute-done.refs_4_), channel_id=1, source_target_pairs={{0,24},{1,25},{2,26},{3,27},{4,28},{5,29},{6,30},{7,31},{8,0},{9,1... | collective-permute-start | bytes 786440 | tf_op jit(solution)/shard_map/ppermute | solution.py:38
  28.1 10.2 %collective-permute-start.3 = (f32[256,256]{1,0:T(8,128)S(1)}, f32[256,256]{1,0:T(8,128)S(1)}, u32[]{:S(2)}, u32[]{:S(2)}) collective-permute-start(f32[256,256]{1,0:T(8,128)S(1)} %collective-permute-done.refs_4_), channel_id=1, source_target_pairs={{0,8},{1,9},{2,10},{3,11},{4,12},{5,13},{6,14},{7,15},{8,16},{9,17... | collective-permute-start | bytes 786440 | tf_op jit(solution)/shard_map/ppermute | solution.py:38
  38.3 6.4 %collective-permute-start.6 = (f32[256,256]{1,0:T(8,128)S(1)}, f32[256,256]{1,0:T(8,128)S(1)}, u32[]{:S(2)}, u32[]{:S(2)}) collective-permute-start(f32[256,256]{1,0:T(8,128)S(1)} %collective-permute-done.4.refs_5_), channel_id=1, source_target_pairs={{0,24},{1,25},{2,26},{3,27},{4,28},{5,29},{6,30},{7,31},{8,0},{9,1... | collective-permute-start | bytes 786440 | tf_op jit(solution)/shard_map/ppermute | solution.py:38
  45.0 5.6 %collective-permute-start.7 = (f32[8,136,256]{2,1,0:T(8,128)S(1)}, f32[8,136,256]{2,1,0:T(8,128)S(1)}, u32[]{:S(2)}, u32[]{:S(2)}) collective-permute-start(f32[8,136,256]{2,1,0:T(8,128)S(1)} %get-tuple-element.45.q_ref.mine), channel_id=1, source_target_pairs={{0,64},{1,65},{2,66},{3,67},{4,68},{5,69},{6,70},{7,71},{8,72},{9,... | collective-permute-start | bytes 3342344 | tf_op jit(solution)/shard_map/ppermute | solution.py:38
  88.6 2.7 %collective-permute-start.8 = (f32[8,128,256]{2,1,0:T(8,128)S(1)}, f32[8,128,256]{2,1,0:T(8,128)S(1)}, u32[]{:S(2)}, u32[]{:S(2)}) collective-permute-start(f32[8,128,256]{2,1,0:T(8,128)S(1)} %get-tuple-element.55), channel_id=1, source_target_pairs={{0,64},{1,65},{2,66},{3,67},{4,68},{5,69},{6,70},{7,71},{8,72},{9,... | collective-permute-start | bytes 3145736 | tf_op jit(solution)/shard_map/ppermute | solution.py:38
  88.7 14.5 %collective-permute-start.9 = (f32[520,256]{1,0:T(8,128)S(1)}, f32[520,256]{1,0:T(8,128)S(1)}, u32[]{:S(2)}, u32[]{:S(2)}) collective-permute-start(f32[520,256]{1,0:T(8,128)S(1)} %get-tuple-element.57), channel_id=1, source_target_pairs={{0,32},{1,33},{2,34},{3,35},{4,36},{5,37},{6,38},{7,39},{8,40},{9,... | collective-permute-start | bytes 1597448 | tf_op jit(solution)/shard_map/ppermute | solution.py:38
  89.2 15.3 %collective-permute-start.10 = (f32[520,256]{1,0:T(8,128)S(1)}, f32[520,256]{1,0:T(8,128)S(1)}, u32[]{:S(2)}, u32[]{:S(2)}) collective-permute-start(f32[520,256]{1,0:T(8,128)S(1)} %get-tuple-element.58), channel_id=1, source_target_pairs={{0,160},{1,161},{2,162},{3,163},{4,164},{5,165},{6,166},{7,167},{8... | collective-permute-start | bytes 1597448 | tf_op jit(solution)/shard_map/ppermute | solution.py:38
  106.3 32.1 %all-to-all-start.2 = ((f32[8,128,256]{2,1,0:T(8,128)}), f32[8,128,256]{2,1,0:T(8,128)S(1)}, u32[]{:S(2)}, u32[]{:S(2)}) async-start(f32[8,128,256]{2,1,0:T(8,128)} %get-tuple-element.65), calls=%async_computation.2 | async-start | bytes 2097152 | tf_op jit(solution)/shard_map/all_to_all | solution.py:370
  110.3 14.3 %collective-permute-start.11 = (f32[264,256]{1,0:T(8,128)S(1)}, f32[264,256]{1,0:T(8,128)S(1)}, u32[]{:S(2)}, u32[]{:S(2)}) collective-permute-start(f32[264,256]{1,0:T(8,128)S(1)} %get-tuple-element.61), channel_id=1, source_target_pairs={{0,8},{1,9},{2,10},{3,11},{4,12},{5,13},{6,14},{7,15},{8,16},{9,17... | collective-permute-start | bytes 811016 | tf_op jit(solution)/shard_map/ppermute | solution.py:38
  110.3 14.3 %collective-permute-start.12 = (f32[264,256]{1,0:T(8,128)S(1)}, f32[264,256]{1,0:T(8,128)S(1)}, u32[]{:S(2)}, u32[]{:S(2)}) collective-permute-start(f32[264,256]{1,0:T(8,128)S(1)} %get-tuple-element.62), channel_id=1, source_target_pairs={{0,16},{1,17},{2,18},{3,19},{4,20},{5,21},{6,22},{7,23},{8,24},{9,... | collective-permute-start | bytes 811016 | tf_op jit(solution)/shard_map/ppermute | solution.py:38
  113.2 12.0 %collective-permute-start.13 = (f32[264,256]{1,0:T(8,128)S(1)}, f32[264,256]{1,0:T(8,128)S(1)}, u32[]{:S(2)}, u32[]{:S(2)}) collective-permute-start(f32[264,256]{1,0:T(8,128)S(1)} %get-tuple-element.63), channel_id=1, source_target_pairs={{0,24},{1,25},{2,26},{3,27},{4,28},{5,29},{6,30},{7,31},{8,0},{9,1... | collective-permute-start | bytes 811016 | tf_op jit(solution)/shard_map/ppermute | solution.py:38
  125.3 8.3 %collective-permute-start.14 = (f32[264,256]{1,0:T(8,128)S(1)}, f32[264,256]{1,0:T(8,128)S(1)}, u32[]{:S(2)}, u32[]{:S(2)}) collective-permute-start(f32[264,256]{1,0:T(8,128)S(1)} %land_kernel.1.mine), channel_id=1, source_target_pairs={{0,128},{1,129},{2,130},{3,131},{4,132},{5,133},{6,134},{7,135},{8... | collective-permute-start | bytes 811016 | tf_op jit(solution)/shard_map/ppermute | solution.py:38
  126.6 7.0 %collective-permute-start.15 = (f32[264,256]{1,0:T(8,128)S(1)}, f32[264,256]{1,0:T(8,128)S(1)}, u32[]{:S(2)}, u32[]{:S(2)}) collective-permute-start(f32[264,256]{1,0:T(8,128)S(1)} %land_kernel.1.mine), channel_id=1, source_target_pairs={{0,64},{1,65},{2,66},{3,67},{4,68},{5,69},{6,70},{7,71},{8,72},{9,... | collective-permute-start | bytes 811016 | tf_op jit(solution)/shard_map/ppermute | solution.py:38
  133.6 1.5 %collective-permute-start.16 = (f32[264,256]{1,0:T(8,128)S(1)}, f32[264,256]{1,0:T(8,128)S(1)}, u32[]{:S(2)}, u32[]{:S(2)}) collective-permute-start(f32[264,256]{1,0:T(8,128)S(1)} %collective-permute-done.14.mine2), channel_id=1, source_target_pairs={{0,64},{1,65},{2,66},{3,67},{4,68},{5,69},{6,70},{7,71},{8,72},{9,... | collective-permute-start | bytes 811016 | tf_op jit(solution)/shard_map/ppermute | solution.py:38

commit v3 on v2

--- a/solution.py
+++ b/solution.py
@@ -38,8 +38,9 @@
     return lax.ppermute(a, AXES, pairs(**shift))
 
 
-def flip(a, bit):
-    return lax.ppermute(a, AXES, [(i, i ^ bit) for i in range(256)])
+def twin(a, axis, hops=1):
+    up, down = pairs(**{axis: hops}), pairs(**{axis: -hops})
+    return lax.ppermute(a, AXES, [(down if (i >> 6) & 1 else up)[i] for i in range(256)])
 
 
 def split(a):
@@ -94,44 +95,91 @@
     )(*ins)
 
 
-def start_kernel(pos_ref, queries, labels, items, out, own):
+def at(start, n):
+    return pl.ds(pl.multiple_of(start, 8), n)
+
+
+def start_kernel(pos_ref, queries, labels, items, q, own):
+    q[:ROWS, :] = queries[...]
+    q[ROWS:, :ROWS] = jnp.broadcast_to(labels[...].astype(f32), (PAD - ROWS, ROWS))
+    q[ROWS:, ROWS:] = jnp.zeros((PAD - ROWS, E - ROWS), f32)
+    own[...] = items[at(pos_ref[1] * HALF, HALF), :]
+
+
+def pair_kernel(pos_ref, mine, other, out):
+    n, c = mine.shape[0], pos_ref[1]
+    out[at(c * n, n), :] = mine[...]
+    out[at((1 - c) * n, n), :] = other[...]
+
+
+def part_kernel(pos_ref, both, *refs):
+    *_, mine, other = refs
+    n, c = mine.shape[0], pos_ref[1]
+    mine[...] = both[at(c * n, n), :]
+    other[...] = both[at((1 - c) * n, n), :]
+
+
+def stack_kernel(a, b, c, out):
+    for k, ref in enumerate((a, b, c)):
+        out[k * HALF : (k + 1) * HALF, :] = ref[...]
+
+
+def pack_queries_kernel(pos_ref, q, qo, q4, qo4, r1, r2, r3, s1, s2, s3, mine, other):
+    z, c = pos_ref[0], pos_ref[1]
+    mine[z], other[z] = q[...], qo[...]
+    mine[(z + 4) & 7], other[(z + 4) & 7] = q4[...], qo4[...]
+    for k, r, s in ((1, r1, s1), (2, r2, s2), (3, r3, s3)):
+        step = k - 2 * c * k
+        for ref, where in ((r, (z - step) & 7), (s, (z + step) & 7)):
+            mine[where] = ref[at(c * PAD, PAD), :]
+            other[where] = ref[at((1 - c) * PAD, PAD), :]
+
+
+def pack_items_kernel(pos_ref, own, near, across, far, y_own, y_rest, xh, xl):
+    c = pos_ref[1]
+
+    def put(slot, rows):
+        xh[at(slot * HALF, HALF), :], xl[at(slot * HALF, HALF), :] = split(rows)
+
+    put(0, own[...])
+    put(3 - 2 * c, near[...])
+    put(1 + 2 * c, across[...])
+    put(2, far[...])
+    put(4, y_own[...])
+    put(7 - 2 * c, y_rest[:HALF, :])
+    put(5 + 2 * c, y_rest[HALF : 2 * HALF, :])
+    put(6, y_rest[2 * HALF :, :])
+
+
+def join_stats(a, b):
+    best = jnp.maximum(a[0], b[0])
+    return best, a[1] * jnp.exp(a[0] - best) + b[1] * jnp.exp(b[0] - best)
+
+
+def spread_kernel(mine, got, out):
+    best, total = join_stats(mine, got)
     for k in range(ZN):
-        out[k, :ROWS, :] = queries[...]
-        out[k, ROWS:, :ROWS] = jnp.broadcast_to(labels[...].astype(f32), (PAD - ROWS, ROWS))
-        out[k, ROWS:, ROWS:] = jnp.zeros((PAD - ROWS, E - ROWS), f32)
-    own[...] = items[pl.ds(pl.multiple_of(pos_ref[1] * HALF, HALF), HALF), :]
-
-
-def pack_items_kernel(*refs):
-    *parts, mine, xh, xl, held = refs
-    held[...] = mine[...]
-    for d, p in enumerate(parts):
-        at = slice(d * HALF, (d + 1) * HALF)
-        xh[at, :], xl[at, :] = split(p[...])
-
-
-def spread_kernel(mine, other, out):
-    for k in range(2 * ZN):
-        out[k, 0] = mine[...]
-        out[k, 1] = other[...]
-
-
-def merge_kernel(pos_ref, got, lse_ref, part_ref):
-    core = pos_ref[1]
-    loss = None
-    for h in range(2):
-        side = [(k, h ^ ((core ^ (k // ZN)) & 1)) for k in range(2 * ZN)]
-        best = got[side[0][0], side[0][1], 0]
-        for k, w in side[1:]:
-            best = jnp.maximum(best, got[k, w, 0])
-        total = pick = jnp.zeros((ZN, ROWS), f32)
-        for k, w in side:
-            total += got[k, w, 1] * jnp.exp(got[k, w, 0] - best)
-            pick += got[k, w, 2]
-        lse = best + jnp.log(total)
-        lse_ref[h] = lse
-        loss = lse - pick if loss is None else loss + (lse - pick)
-    part_ref[0] = jnp.sum(loss)
+        out[k, 0] = best
+        out[k, 1] = total
+        out[k, 2] = mine[2] + got[2]
+
+
+def merge_kernel(got, out):
+    best = got[0, 0]
+    for k in range(1, ZN):
+        best = jnp.maximum(best, got[k, 0])
+    total = pick = jnp.zeros((ZN, ROWS), f32)
+    for k in range(ZN):
+        total += got[k, 1] * jnp.exp(got[k, 0] - best)
+        pick += got[k, 2]
+    lse = best + jnp.log(total)
+    out[:ZN] = lse
+    out[ZN:] = jnp.full((8, ROWS), jnp.sum(lse - pick), f32)
+
+
+def line_loss(own, other):
+    row = own[ZN : ZN + 1, :] + other[ZN : ZN + 1, :]
+    return cat([row, row], 1)
 
 
 def forward_kernel(pos_ref, xh, xl, q_ref, s0_ref, s1_ref, stat_ref):
@@ -187,9 +235,9 @@
     )(pos, xh, xl, q)
 
 
-def block(i, pos_ref, lse_ref, side, q_ref):
+def block(i, pos_ref, lse_ref, q_ref):
     qh, ql = split(query_rows(q_ref))
-    lse = cat([lse_ref[side, pl.ds(2 * i, 1), :], lse_ref[side, pl.ds(2 * i + 1, 1), :]], 1)
+    lse = cat([lse_ref[pl.ds(2 * i, 1), :], lse_ref[pl.ds(2 * i + 1, 1), :]], 1)
     return cat([qh, ql, qh], 0), local_labels(pos_ref, q_ref), lse
 
 
@@ -212,7 +260,7 @@
     return o * (E**-0.5)
 
 
-def backward_a_kernel(pos_ref, part, xh, xl, mine, other, lse_ref, sm1, so0, so1, oo, up, down, token, g_acc):
+def backward_a_kernel(pos_ref, xh, xl, mine, other, lse_m, lse_o, sm1, so0, so1, oo, up, down, token, g_acc):
     i = pl.program_id(0)
 
     @pl.when(i == 0)
@@ -222,12 +270,12 @@
 
     @pl.when(i < 4)
     def _():
-        operands = block(i, pos_ref, lse_ref, 0, mine)
+        operands = block(i, pos_ref, lse_m, mine)
         gradients(g_acc, None, (None, sm1), operands, 4, 4, range(4, 8))
 
     @pl.when(i >= 4)
     def _():
-        operands = block(i - 4, pos_ref, lse_ref, 1, other)
+        operands = block(i - 4, pos_ref, lse_o, other)
         o = gradients(g_acc, (xh, xl), (so0, so1), operands, 4, 4, range(8))
         oo[0], oo[1] = o[:ROWS], o[ROWS:]
 
@@ -236,10 +284,10 @@
         for d in range(4):
             up[d * CUT : (d + 1) * CUT, :] = g_acc[d, :CUT, :]
             down[d * CUT : (d + 1) * CUT, :] = g_acc[d, CUT:, :]
-        up[4 * CUT :, :] = down[4 * CUT :, :] = jnp.full((8, E), part[0], f32)
-
-
-def backward_b_kernel(pos_ref, token, xh, xl, mine, other, lse_ref, sm0, sm1, so0, got, om, g_ref):
+        up[4 * CUT :, :] = down[4 * CUT :, :] = jnp.broadcast_to(line_loss(lse_m, lse_o), (8, E))
+
+
+def backward_b_kernel(pos_ref, token, xh, xl, mine, other, lse_m, lse_o, sm0, sm1, so0, got, om, g_ref):
     i = pl.program_id(0)
 
     @pl.when(i == 0)
@@ -248,12 +296,12 @@
 
     @pl.when(i < 4)
     def _():
-        operands = block(i, pos_ref, lse_ref, 1, other)
+        operands = block(i, pos_ref, lse_o, other)
         gradients(g_ref, None, (so0, None), operands, 0, 4, range(4))
 
     @pl.when(i >= 4)
     def _():
-        operands = block(i - 4, pos_ref, lse_ref, 0, mine)
+        operands = block(i - 4, pos_ref, lse_m, mine)
         o = gradients(g_ref, (xh, xl), (sm0, sm1), operands, 0, 4, range(8))
         om[0], om[1] = o[:ROWS] + got[0], o[ROWS:] + got[1]
 
@@ -271,15 +319,16 @@
 
 
 X_SPEC = whole(LOCAL, E)
+LSE = whole(2 * ZN, ROWS)
 Q = (2, PAD, E)
 S = (1, 4, HALF, 256)
 
 
-def backward_a(pos, part, xh, xl, mine, other, lse, *s):
+def backward_a(pos, *operands):
     return pl.pallas_call(
         backward_a_kernel,
         grid=(ZN,),
-        in_specs=[SMEM, SMEM, X_SPEC, X_SPEC, early(*Q), late(*Q), whole(2, ZN, ROWS)]
+        in_specs=[SMEM, X_SPEC, X_SPEC, early(*Q), late(*Q), LSE, LSE]
         + [early(*S), late(*S), late(*S)],
         out_specs=[late(2, ROWS, E)] + [whole(4 * CUT + 8, E)] * 2 + [SMEM],
         out_shape=[shape(ZN, ROWS, E)] + [shape(4 * CUT + 8, E)] * 2 + [shape(1)],
@@ -287,40 +336,58 @@
         compiler_params=params(14),
         cost_estimate=pl.CostEstimate(flops=6 * 2**30, bytes_accessed=16 * 2**20, transcendentals=3 * 2**20),
         name="backward_a",
-    )(pos, part, xh, xl, mine, other, lse, *s)
-
-
-def backward_b(pos, token, xh, xl, mine, other, lse, *s):
+    )(pos, *operands)
+
+
+def backward_b(pos, *operands):
     return pl.pallas_call(
         backward_b_kernel,
         grid=(ZN,),
-        in_specs=[SMEM, SMEM, X_SPEC, X_SPEC, late(*Q), early(*Q), whole(2, ZN, ROWS)]
+        in_specs=[SMEM, SMEM, X_SPEC, X_SPEC, late(*Q), early(*Q), LSE, LSE]
         + [late(*S), late(*S), early(*S), late(2, ROWS, E)],
         out_specs=[late(2, ROWS, E), whole(4, HALF, E)],
         out_shape=[shape(ZN, ROWS, E), shape(4, HALF, E)],
         compiler_params=params(14),
         cost_estimate=pl.CostEstimate(flops=6 * 2**30, bytes_accessed=16 * 2**20, transcendentals=3 * 2**20),
         name="backward_b",
-    )(pos, token, xh, xl, mine, other, lse, *s)
-
-
-def gather(qs, own):
-    mine = lax.all_to_all(qs, "z", 0, 0, tiled=True)
-    y0, x3, x1 = flip(own, 32), send(own, dx=1), send(own, dx=-1)
-    y0, x3, x1 = lax.optimization_barrier((y0, x3, x1))
-    y3, y1, x2 = send(y0, dx=1), send(y0, dx=-1), send(x3, dx=1)
-    y3, y1, x2 = lax.optimization_barrier((y3, y1, x2))
-    y2 = send(y1, dx=-1)
-    return mine, [own, x1, x2, x3, y0, y1, y2, y3]
-
-
-def fold_kernel(part, g, a, b, o, held, *out):
+    )(pos, *operands)
+
+
+def gather(pos, q, own, items):
+    chunk, two = shape(PAD, E), shape(2 * PAD, E)
+    half = shape(HALF, E)
+    x1 = twin(items, "dx")
+    qo = send(q, dc=1)
+    (r0,) = small(pair_kernel, [pos, q, qo], [two])
+    r1 = twin(r0, "dz")
+    r2 = twin(r0, "dz", 2)
+    far = twin(own, "dx", 2)
+    y0 = twin(own, "dy")
+    near, rest = small(part_kernel, [pos, x1, y0, r2], [half, half])
+    across = send(rest, dc=1)
+    (rest,) = small(stack_kernel, [near, across, far], [shape(3 * HALF, E)])
+    y_rest = twin(rest, "dy")
+    r3 = twin(r2, "dz")
+    s1, s2 = send(r1, dc=1), send(r2, dc=1)
+    third, _ = small(part_kernel, [pos, r2, far], [chunk, chunk])
+    q4 = twin(third, "dz", 2)
+    s3 = send(r3, dc=1)
+    mine, other = small(
+        pack_queries_kernel, [pos, q, qo, q4, send(q4, dc=1), r1, r2, r3, s1, s2, s3], [shape(ZN, PAD, E)] * 2
+    )
+    xh, xl = small(
+        pack_items_kernel, [pos, own, near, across, far, y0, y_rest], [shape(LOCAL, E, dtype=bf16)] * 2
+    )
+    return mine, other, xh, xl
+
+
+def fold_kernel(lse_m, lse_o, g, a, b, o, held, *out):
     held[...] = o[...]
     for d in range(4):
         at = slice(d * CUT, (d + 1) * CUT)
         out[d][:CUT] = g[d, :CUT] + a[at]
         out[d][CUT:HALF] = g[d, CUT:] + b[at]
-        out[d][HALF : HALF + 1] = jnp.full((1, E), part[0], f32)
+        out[d][HALF : HALF + 1] = line_loss(lse_m, lse_o)
         out[d][HALF + 1 : HALF + 2] = a[4 * CUT : 4 * CUT + 1]
         out[d][HALF + 2 : HALF + 3] = b[4 * CUT : 4 * CUT + 1]
         out[d][HALF + 3 :] = jnp.zeros((5, E), f32)
@@ -350,23 +417,20 @@
 def body(queries, items, labels):
     core, y_lo, x_at, z_at = (lax.axis_index(a) for a in ("c", "yl", "x", "z"))
     pos = jnp.stack([z_at, core, y_lo, x_at]).astype(jnp.int32)
-    qs, own = small(
-        start_kernel, [pos, queries, labels.reshape(1, ROWS), items], [shape(ZN, PAD, E), shape(HALF, E)]
+    q, own = small(
+        start_kernel, [pos, queries, labels.reshape(1, ROWS), items], [shape(PAD, E), shape(HALF, E)]
     )
-    mine, parts = gather(qs, own)
-    xh, xl, mine = small(
-        pack_items_kernel, parts + [mine], [shape(LOCAL, E, dtype=bf16)] * 2 + [shape(ZN, PAD, E)]
-    )
-    other = send(mine, dc=1)
+    mine, other, xh, xl = gather(pos, q, own, items)
     sm0, sm1, stat_m = forward(pos, xh, xl, mine)
     so0, so1, stat_o = forward(pos, xh, xl, other)
-    (stats,) = small(spread_kernel, [stat_m, stat_o], [shape(2 * ZN, 2, 3, ZN, ROWS)])
-    stats = lax.all_to_all(stats, ("c", "z"), 0, 0, tiled=True)
-    lse, part = small(merge_kernel, [pos, stats], [shape(2, ZN, ROWS), shape(1)])
-    oo, up, down, first = backward_a(pos, part, xh, xl, mine, other, lse, sm1, so0, so1)
+    (stats,) = small(spread_kernel, [stat_m, send(stat_o, dc=1)], [shape(ZN, 3, ZN, ROWS)])
+    stats = lax.all_to_all(stats, "z", 0, 0, tiled=True)
+    (lse,) = small(merge_kernel, [stats], [shape(2 * ZN, ROWS)])
+    lse = [lse, send(lse, dc=1)]
+    oo, up, down, first = backward_a(pos, xh, xl, mine, other, *lse, sm1, so0, so1)
     a, b = send(up, dy=1), send(down, dy=-1)
-    o, g = backward_b(pos, first, xh, xl, mine, other, lse, sm0, sm1, so0, send(oo, dc=1))
-    o, m0, m1, m2, m3 = small(fold_kernel, [part, g, a, b, o], [shape(ZN, ROWS, E)] + [shape(HALF + 8, E)] * 4)
+    o, g = backward_b(pos, first, xh, xl, mine, other, *lse, sm0, sm1, so0, send(oo, dc=1))
+    o, m0, m1, m2, m3 = small(fold_kernel, [*lse, g, a, b, o], [shape(ZN, ROWS, E)] + [shape(HALF + 8, E)] * 4)
     o = lax.all_to_all(o, "z", 0, 0, tiled=True)
     m2, m1, m3 = send(m2, dx=2), send(m1, dx=1), send(m3, dx=-1)
     (own,) = small(land_kernel, [m0, m1, m2, m3], [shape(HALF + 8, E)])

time: 141 us -> 131 us (0.929)
  waiting for transfers between devices: 49.3 us -> 40.3 us
  blocking collectives: 19.9 us -> 15.1 us
  starting transfers between devices: 26.5 us -> 31.2 us
    ppermute x16 -> x17, waiting for transfers between devices: 47.4 us -> 28.4 us  [send(): return lax.ppermute(a, AXES, pairs(**shift))]
    ppermute x1 -> x8, starting transfers between devices: 0.74 us -> 15.1 us  [twin(): lax.ppermute(a, AXES, [(down if i >> 6 & 1 else up)[i] for i in range(256)])]
    ppermute x1 -> x8, waiting for transfers between devices: 0.01 us -> 10.9 us  [twin(): lax.ppermute(a, AXES, [(down if i >> 6 & 1 else up)[i] for i in range(256)])]
    all_to_all x1 -> x0, starting transfers between devices: 8.47 us -> none  [gather(): mine = lax.all_to_all(qs, 'z', 0, 0, tiled=True)]
    all_to_all x1, blocking collectives: 19.9 us -> 15.1 us  [body(): stats = lax.all_to_all(stats, 'z', 0, 0, tiled=True)]
    pallas_call x8 -> x13, Pallas kernels: 7.3 us -> 8.07 us  [small(): pl.pallas_call(kernel, in_specs=[SMEM if a.ndim == 1 else VMEM for a in i...]
    ppermute x16 -> x17, starting transfers between devices: 13.3 us -> 12.6 us  [send(): return lax.ppermute(a, AXES, pairs(**shift))]
  transfers between devices with their start and end apart: 19 -> 26, of which waited for: 13 -> 16; matrix products, arithmetic and copies ran while one was open for 0% -> 0% of each run, Pallas kernels for 13% -> 16%
where the time goes in v3:
time: 131 us; the launch traced here: 130 us
  waiting for transfers between devices  40.3 us (31%)
  Pallas kernels  40 us (31%)
  starting transfers between devices  31.2 us (24%)
  blocking collectives  15.1 us (12%)
  local copies, waits for them, and re-layouts  2.6 us (2%)
    ppermute x17, waiting for transfers between devices, send(): return lax.ppermute(a, AXES, pairs(**shift))  28.4 us
    ppermute x8, starting transfers between devices, twin(): lax.ppermute(a, AXES, [(down if i >> 6 & 1 else up)[i] for i in range(256)])  15.1 us
    all_to_all x1, blocking collectives, body(): stats = lax.all_to_all(stats, 'z', 0, 0, tiled=True)  15.1 us
    ppermute x17, starting transfers between devices, send(): return lax.ppermute(a, AXES, pairs(**shift))  12.6 us
    pallas_call x2, Pallas kernels, forward(): pl.pallas_call(forward_kernel, grid=(4,), in_specs=[SMEM, pl.BlockSpec((L...  11 us
    ppermute x8, waiting for transfers between devices, twin(): lax.ppermute(a, AXES, [(down if i >> 6 & 1 else up)[i] for i in range(256)])  10.9 us
    pallas_call x1, Pallas kernels, backward_b(): pl.pallas_call(backward_b_kernel, grid=(ZN,), in_specs=[SMEM, SMEM, X_SPE...  10.5 us
    pallas_call x1, Pallas kernels, backward_a(): pl.pallas_call(backward_a_kernel, grid=(ZN,), in_specs=[SMEM, X_SPEC, X_S...  10.5 us
  transfers between devices with their start and end apart: 26, of which 16 were waited for; matrix products, arithmetic and copies ran while one was open for 0% of the time, Pallas kernels for 16%

profile of v3, /device:TPU:24, one launch (start us, length us, event | category | flops | bytes accessed | tf_op | source)
XLA Modules:
  0.0 130.1 jit_solution(1351784596022059346)
XLA Ops:
  0.6 1.6 %collective-permute-start = (f32[512,256]{1,0:T(8,128)}, f32[512,256]{1,0:T(8,128)S(1)}, u32[]{:S(2)}, u32[]{:S(2)}) collective-permute-start(f32[512,256]{1,0:T(8,128)} %items.1), channel_id=1, source_target_pairs={{0,8},{1,9},{2,10},{3,11},{4,12},{5,13},{6,14},{7,15},{8,16},{9,17... | collective-permute-start | bytes 1572872 | tf_op jit(solution)/shard_map/ppermute | solution.py:43
  7.9 3.3 %collective-permute-start.3 = (f32[272,256]{1,0:T(8,128)S(1)}, f32[272,256]{1,0:T(8,128)S(1)}, u32[]{:S(2)}, u32[]{:S(2)}) collective-permute-start(f32[272,256]{1,0:T(8,128)S(1)} %pair_kernel.1), channel_id=1, source_target_pairs={{0,2},{1,3},{2,4},{3,5},{4,6},{5,7},{6,0},{7,1},{8,10},{9,11},{10,... | collective-permute-start | bytes 835592 | tf_op jit(solution)/shard_map/ppermute | solution.py:43
  11.5 2.3 %collective-permute-start.5 = (f32[256,256]{1,0:T(8,128)S(1)}, f32[256,256]{1,0:T(8,128)S(1)}, u32[]{:S(2)}, u32[]{:S(2)}) collective-permute-start(f32[256,256]{1,0:T(8,128)S(1)} %get-tuple-element.31.own), channel_id=1, source_target_pairs={{0,16},{1,17},{2,18},{3,19},{4,20},{5,21},{6,22},{7,23},{8,24},{9,... | collective-permute-start | bytes 786440 | tf_op jit(solution)/shard_map/ppermute | solution.py:43
  13.8 3.9 %collective-permute-done.1.refs_0_.y_own = f32[256,256]{1,0:T(8,128)S(1)} collective-permute-done((f32[256,256]{1,0:T(8,128)S(1)}, f32[256,256]{1,0:T(8,128)S(1)}, u32[]{:S(2)}, u32[]{:S(2)}) %collective-permute-start.1) | collective-permute-done | bytes 262176 | tf_op jit(solution)/shard_map/ppermute | solution.py:43
  17.7 1.8 %collective-permute-done.3.refs_1_.both.r2 = f32[272,256]{1,0:T(8,128)S(1)} collective-permute-done((f32[272,256]{1,0:T(8,128)S(1)}, f32[272,256]{1,0:T(8,128)S(1)}, u32[]{:S(2)}, u32[]{:S(2)}) %collective-permute-start.3) | collective-permute-done | bytes 278560 | tf_op jit(solution)/shard_map/ppermute | solution.py:43
  20.0 1.5 %collective-permute-start.4 = (f32[256,256]{1,0:T(8,128)S(1)}, f32[256,256]{1,0:T(8,128)S(1)}, u32[]{:S(2)}, u32[]{:S(2)}) collective-permute-start(f32[256,256]{1,0:T(8,128)S(1)} %get-tuple-element.34), channel_id=1, source_target_pairs={{0,64},{1,65},{2,66},{3,67},{4,68},{5,69},{6,70},{7,71},{8,72},{9,... | collective-permute-start | bytes 786440 | tf_op jit(solution)/shard_map/ppermute | solution.py:38
  23.1 2.3 %collective-permute-start.9 = (f32[272,256]{1,0:T(8,128)S(1)}, f32[272,256]{1,0:T(8,128)S(1)}, u32[]{:S(2)}, u32[]{:S(2)}) collective-permute-start(f32[272,256]{1,0:T(8,128)S(1)} %pair_kernel.1), channel_id=1, source_target_pairs={{0,1},{1,2},{2,3},{3,4},{4,5},{5,6},{6,7},{7,0},{8,9},{9,10},{10,1... | collective-permute-start | bytes 835592 | tf_op jit(solution)/shard_map/ppermute | solution.py:43
  27.7 4.0 %collective-permute-start.7 = (f32[136,256]{1,0:T(8,128)S(1)}, f32[136,256]{1,0:T(8,128)S(1)}, u32[]{:S(2)}, u32[]{:S(2)}) collective-permute-start(f32[136,256]{1,0:T(8,128)S(1)} %get-tuple-element.37), channel_id=1, source_target_pairs={{0,2},{1,3},{2,4},{3,5},{4,6},{5,7},{6,0},{7,1},{8,10},{9,11},{10,... | collective-permute-start | bytes 417800 | tf_op jit(solution)/shard_map/ppermute | solution.py:43
  32.2 1.9 %collective-permute-done.10.r3 = f32[272,256]{1,0:T(8,128)S(1)} collective-permute-done((f32[272,256]{1,0:T(8,128)S(1)}, f32[272,256]{1,0:T(8,128)S(1)}, u32[]{:S(2)}, u32[]{:S(2)}) %collective-permute-start.10) | collective-permute-done | bytes 278560 | tf_op jit(solution)/shard_map/ppermute | solution.py:43
  34.6 3.3 %collective-permute-done.7.q4 = f32[136,256]{1,0:T(8,128)S(1)} collective-permute-done((f32[136,256]{1,0:T(8,128)S(1)}, f32[136,256]{1,0:T(8,128)S(1)}, u32[]{:S(2)}, u32[]{:S(2)}) %collective-permute-start.7) | collective-permute-done | bytes 139296 | tf_op jit(solution)/shard_map/ppermute | solution.py:43
  40.9 5.5 %forward.3 = (f32[4,4,256,256]{3,2,1,0:T(8,128)S(1)}, f32[4,4,256,256]{3,2,1,0:T(8,128)S(1)}, f32[3,8,128]{2,1,0:T(8,128)S(1)}) custom-call(s32[4]{0:T(128)S(1)} %pad_add_fusion.pos_ref, bf16[2048,256]{1,0:T(8,128)(2,1)S(1)} %get-tuple-element.35.xh, bf16[2048,256]{1,0:T(8,128)(2,1)S(1)} %get-tuple-element.36.xl, ...), custom_call_target="tpu_custom_call" | custom-call | flops 3221225472 | bytes 10485760 | tf_op jit(solution)/shard_map/forward/pallas_call | solution.py:217
  46.8 5.5 %forward.2 = (f32[4,4,256,256]{3,2,1,0:T(8,128)S(1)}, f32[4,4,256,256]{3,2,1,0:T(8,128)S(1)}, f32[3,8,128]{2,1,0:T(8,128)S(1)}) custom-call(s32[4]{0:T(128)S(1)} %pad_add_fusion.pos_ref, bf16[2048,256]{1,0:T(8,128)(2,1)S(1)} %get-tuple-element.35.xh, bf16[2048,256]{1,0:T(8,128)(2,1)S(1)} %get-tuple-element.36.xl, f32[8,136,256]{2,1,0:T(8,128)S(1)} %get-tuple-element.38.q_ref.mine), custom_call_target="tpu_custom_call" | custom-call | flops 3221225472 | bytes 10485760 | tf_op jit(solution)/shard_map/forward/pallas_call | solution.py:217
  52.3 15.1 %all_to_all.10.got = f32[8,3,8,128]{3,2,1,0:T(8,128)S(1)} all-to-all(f32[8,3,8,128]{3,2,1,0:T(8,128)S(1)} %spread_kernel.1), channel_id=1, replica_groups=mesh['yh'=2,'c'=2,'yl'=2,'x'=4,'z'=8] {'z'}, dimensions={0} | all-to-all | bytes 196608 | tf_op jit(solution)/shard_map/all_to_all | solution.py:427
  68.8 10.5 %backward_a.1 = (f32[8,128,256]{2,1,0:T(8,128)S(1)}, f32[520,256]{1,0:T(8,128)S(1)}, f32[520,256]{1,0:T(8,128)S(1)}, f32[1]{0:T(128)}) custom-call(s32[4]{0:T(128)S(1)} %pad_add_fusion.pos_ref, bf16[2048,256]{1,0:T(8,128)(2,1)S(1)} %get-tuple-element.35.xh, bf16[2048,256]{1,0:T(8,128)(2,1)S(1)} %get-tuple-element.36.xl, ...), custom_call_target="tpu_custom_call" | custom-call | flops 6442450944 | bytes 16777216 | tf_op jit(solution)/shard_map/backward_a/pallas_call | solution.py:328
  79.5 1.6 %collective-permute-start.17 = (f32[520,256]{1,0:T(8,128)S(1)}, f32[520,256]{1,0:T(8,128)S(1)}, u32[]{:S(2)}, u32[]{:S(2)}) collective-permute-start(f32[520,256]{1,0:T(8,128)S(1)} %get-tuple-element.49), channel_id=1, source_target_pairs={{0,32},{1,33},{2,34},{3,35},{4,36},{5,37},{6,38},{7,39},{8,40},{9,... | collective-permute-start | bytes 1597448 | tf_op jit(solution)/shard_map/ppermute | solution.py:38
  82.0 10.5 %backward_b.1 = (f32[8,128,256]{2,1,0:T(8,128)S(1)}, f32[4,256,256]{2,1,0:T(8,128)S(1)}) custom-call(s32[4]{0:T(128)S(1)} %pad_add_fusion.pos_ref, f32[1]{0:T(128)} %get-tuple-element.45.token, bf16[2048,256]{1,0:T(8,128)(2,1)S(1)} %get-tuple-element.35.xh, bf16[2048,256]{1,0:T(8,128)(2,1)S(1)} %get-tuple-element.36.xl, ...), custom_call_target="tpu_custom_call" | custom-call | flops 6442450944 | bytes 16777216 | tf_op jit(solution)/shard_map/backward_b/pallas_call | solution.py:343
  92.6 1.4 %collective-permute-done.17.a = f32[520,256]{1,0:T(8,128)S(1)} collective-permute-done((f32[520,256]{1,0:T(8,128)S(1)}, f32[520,256]{1,0:T(8,128)S(1)}, u32[]{:S(2)}, u32[]{:S(2)}) %collective-permute-start.17) | collective-permute-done | bytes 532512 | tf_op jit(solution)/shard_map/ppermute | solution.py:38
  94.0 2.4 %collective-permute-done.18.b = f32[520,256]{1,0:T(8,128)S(1)} collective-permute-done((f32[520,256]{1,0:T(8,128)S(1)}, f32[520,256]{1,0:T(8,128)S(1)}, u32[]{:S(2)}, u32[]{:S(2)}) %collective-permute-start.18) | collective-permute-done | bytes 532512 | tf_op jit(solution)/shard_map/ppermute | solution.py:38
  97.5 3.6 %all-to-all-start.1 = ((f32[8,128,256]{2,1,0:T(8,128)}), f32[8,128,256]{2,1,0:T(8,128)S(1)}, u32[]{:S(2)}, u32[]{:S(2)}) async-start(f32[8,128,256]{2,1,0:T(8,128)} %get-tuple-element.57), calls=%async_computation.1 | async-start | bytes 2097152 | tf_op jit(solution)/shard_map/all_to_all | solution.py:434
  102.2 1.7 %collective-permute-start.20 = (f32[264,256]{1,0:T(8,128)S(1)}, f32[264,256]{1,0:T(8,128)S(1)}, u32[]{:S(2)}, u32[]{:S(2)}) collective-permute-start(f32[264,256]{1,0:T(8,128)S(1)} %get-tuple-element.54), channel_id=1, source_target_pairs={{0,16},{1,17},{2,18},{3,19},{4,20},{5,21},{6,22},{7,23},{8,24},{9,... | collective-permute-start | bytes 811016 | tf_op jit(solution)/shard_map/ppermute | solution.py:38
  103.9 2.2 %collective-permute-start.21 = (f32[264,256]{1,0:T(8,128)S(1)}, f32[264,256]{1,0:T(8,128)S(1)}, u32[]{:S(2)}, u32[]{:S(2)}) collective-permute-start(f32[264,256]{1,0:T(8,128)S(1)} %get-tuple-element.55), channel_id=1, source_target_pairs={{0,24},{1,25},{2,26},{3,27},{4,28},{5,29},{6,30},{7,31},{8,0},{9,1... | collective-permute-start | bytes 811016 | tf_op jit(solution)/shard_map/ppermute | solution.py:38
  106.1 9.6 %collective-permute-done.19.m1 = f32[264,256]{1,0:T(8,128)S(1)} collective-permute-done((f32[264,256]{1,0:T(8,128)S(1)}, f32[264,256]{1,0:T(8,128)S(1)}, u32[]{:S(2)}, u32[]{:S(2)}) %collective-permute-start.19) | collective-permute-done | bytes 270368 | tf_op jit(solution)/shard_map/ppermute | solution.py:38
  117.7 7.7 %collective-permute-done.22.mine2 = f32[264,256]{1,0:T(8,128)S(1)} collective-permute-done((f32[264,256]{1,0:T(8,128)S(1)}, f32[264,256]{1,0:T(8,128)S(1)}, u32[]{:S(2)}, u32[]{:S(2)}) %collective-permute-start.22) | collective-permute-done | bytes 270368 | tf_op jit(solution)/shard_map/ppermute | solution.py:38
  125.4 1.5 %collective-permute-done.24.other2 = f32[264,256]{1,0:T(8,128)S(1)} collective-permute-done((f32[264,256]{1,0:T(8,128)S(1)}, f32[264,256]{1,0:T(8,128)S(1)}, u32[]{:S(2)}, u32[]{:S(2)}) %collective-permute-start.24) | collective-permute-done | bytes 270368 | tf_op jit(solution)/shard_map/ppermute | solution.py:38
  (53 shorter events, 24.7 us)
Async XLA Ops:
  0.6 18.8 %collective-permute-start = (f32[512,256]{1,0:T(8,128)}, f32[512,256]{1,0:T(8,128)S(1)}, u32[]{:S(2)}, u32[]{:S(2)}) collective-permute-start(f32[512,256]{1,0:T(8,128)} %items.1), channel_id=1, source_target_pairs={{0,8},{1,9},{2,10},{3,11},{4,12},{5,13},{6,14},{7,15},{8,16},{9,17... | collective-permute-start | bytes 1572872 | tf_op jit(solution)/shard_map/ppermute | solution.py:43
  5.5 1.9 %collective-permute-start.2 = (f32[136,256]{1,0:T(8,128)S(1)}, f32[136,256]{1,0:T(8,128)S(1)}, u32[]{:S(2)}, u32[]{:S(2)}) collective-permute-start(f32[136,256]{1,0:T(8,128)S(1)} %get-tuple-element.32.mine.q), channel_id=1, source_target_pairs={{0,64},{1,65},{2,66},{3,67},{4,68},{5,69},{6,70},{7,71},{8,72},{9,... | collective-permute-start | bytes 417800 | tf_op jit(solution)/shard_map/ppermute | solution.py:38
  7.9 11.5 %collective-permute-start.3 = (f32[272,256]{1,0:T(8,128)S(1)}, f32[272,256]{1,0:T(8,128)S(1)}, u32[]{:S(2)}, u32[]{:S(2)}) collective-permute-start(f32[272,256]{1,0:T(8,128)S(1)} %pair_kernel.1), channel_id=1, source_target_pairs={{0,2},{1,3},{2,4},{3,5},{4,6},{5,7},{6,0},{7,1},{8,10},{9,11},{10,... | collective-permute-start | bytes 835592 | tf_op jit(solution)/shard_map/ppermute | solution.py:43
  11.3 6.4 %collective-permute-start.1 = (f32[256,256]{1,0:T(8,128)S(1)}, f32[256,256]{1,0:T(8,128)S(1)}, u32[]{:S(2)}, u32[]{:S(2)}) collective-permute-start(f32[256,256]{1,0:T(8,128)S(1)} %get-tuple-element.31.own), channel_id=1, source_target_pairs={{0,32},{1,33},{2,34},{3,35},{4,36},{5,37},{6,38},{7,39},{8,40},{9,... | collective-permute-start | bytes 786440 | tf_op jit(solution)/shard_map/ppermute | solution.py:43
  11.5 10.0 %collective-permute-start.5 = (f32[256,256]{1,0:T(8,128)S(1)}, f32[256,256]{1,0:T(8,128)S(1)}, u32[]{:S(2)}, u32[]{:S(2)}) collective-permute-start(f32[256,256]{1,0:T(8,128)S(1)} %get-tuple-element.31.own), channel_id=1, source_target_pairs={{0,16},{1,17},{2,18},{3,19},{4,20},{5,21},{6,22},{7,23},{8,24},{9,... | collective-permute-start | bytes 786440 | tf_op jit(solution)/shard_map/ppermute | solution.py:43
  20.0 2.7 %collective-permute-start.4 = (f32[256,256]{1,0:T(8,128)S(1)}, f32[256,256]{1,0:T(8,128)S(1)}, u32[]{:S(2)}, u32[]{:S(2)}) collective-permute-start(f32[256,256]{1,0:T(8,128)S(1)} %get-tuple-element.34), channel_id=1, source_target_pairs={{0,64},{1,65},{2,66},{3,67},{4,68},{5,69},{6,70},{7,71},{8,72},{9,... | collective-permute-start | bytes 786440 | tf_op jit(solution)/shard_map/ppermute | solution.py:38
  22.8 17.3 %collective-permute-start.6 = (f32[768,256]{1,0:T(8,128)S(1)}, f32[768,256]{1,0:T(8,128)S(1)}, u32[]{:S(2)}, u32[]{:S(2)}) collective-permute-start(f32[768,256]{1,0:T(8,128)S(1)} %stack_kernel.1), channel_id=1, source_target_pairs={{0,32},{1,33},{2,34},{3,35},{4,36},{5,37},{6,38},{7,39},{8,40},{9,... | collective-permute-start | bytes 2359304 | tf_op jit(solution)/shard_map/ppermute | solution.py:43
  23.1 8.6 %collective-permute-start.9 = (f32[272,256]{1,0:T(8,128)S(1)}, f32[272,256]{1,0:T(8,128)S(1)}, u32[]{:S(2)}, u32[]{:S(2)}) collective-permute-start(f32[272,256]{1,0:T(8,128)S(1)} %pair_kernel.1), channel_id=1, source_target_pairs={{0,1},{1,2},{2,3},{3,4},{4,5},{5,6},{6,7},{7,0},{8,9},{9,10},{10,1... | collective-permute-start | bytes 835592 | tf_op jit(solution)/shard_map/ppermute | solution.py:43
  25.4 8.7 %collective-permute-start.10 = (f32[272,256]{1,0:T(8,128)S(1)}, f32[272,256]{1,0:T(8,128)S(1)}, u32[]{:S(2)}, u32[]{:S(2)}) collective-permute-start(f32[272,256]{1,0:T(8,128)S(1)} %collective-permute-done.3.refs_1_.both.r2), channel_id=1, source_target_pairs={{0,1},{1,2},{2,3},{3,4},{4,5},{5,6},{6,7},{7,0},{8,9},{9,10},{10,1... | collective-permute-start | bytes 835592 | tf_op jit(solution)/shard_map/ppermute | solution.py:43
  27.7 10.2 %collective-permute-start.7 = (f32[136,256]{1,0:T(8,128)S(1)}, f32[136,256]{1,0:T(8,128)S(1)}, u32[]{:S(2)}, u32[]{:S(2)}) collective-permute-start(f32[136,256]{1,0:T(8,128)S(1)} %get-tuple-element.37), channel_id=1, source_target_pairs={{0,2},{1,3},{2,4},{3,5},{4,6},{5,7},{6,0},{7,1},{8,10},{9,11},{10,... | collective-permute-start | bytes 417800 | tf_op jit(solution)/shard_map/ppermute | solution.py:43
  31.7 6.3 %collective-permute-start.11 = (f32[272,256]{1,0:T(8,128)S(1)}, f32[272,256]{1,0:T(8,128)S(1)}, u32[]{:S(2)}, u32[]{:S(2)}) collective-permute-start(f32[272,256]{1,0:T(8,128)S(1)} %collective-permute-done.9.r1), channel_id=1, source_target_pairs={{0,64},{1,65},{2,66},{3,67},{4,68},{5,69},{6,70},{7,71},{8,72},{9,... | collective-permute-start | bytes 835592 | tf_op jit(solution)/shard_map/ppermute | solution.py:38
  31.7 7.6 %collective-permute-start.12 = (f32[272,256]{1,0:T(8,128)S(1)}, f32[272,256]{1,0:T(8,128)S(1)}, u32[]{:S(2)}, u32[]{:S(2)}) collective-permute-start(f32[272,256]{1,0:T(8,128)S(1)} %collective-permute-done.3.refs_1_.both.r2), channel_id=1, source_target_pairs={{0,64},{1,65},{2,66},{3,67},{4,68},{5,69},{6,70},{7,71},{8,72},{9,... | collective-permute-start | bytes 835592 | tf_op jit(solution)/shard_map/ppermute | solution.py:38
  34.1 5.3 %collective-permute-start.13 = (f32[272,256]{1,0:T(8,128)S(1)}, f32[272,256]{1,0:T(8,128)S(1)}, u32[]{:S(2)}, u32[]{:S(2)}) collective-permute-start(f32[272,256]{1,0:T(8,128)S(1)} %collective-permute-done.10.r3), channel_id=1, source_target_pairs={{0,64},{1,65},{2,66},{3,67},{4,68},{5,69},{6,70},{7,71},{8,72},{9,... | collective-permute-start | bytes 835592 | tf_op jit(solution)/shard_map/ppermute | solution.py:38
  46.4 5.9 %collective-permute-start.14 = (f32[3,8,128]{2,1,0:T(8,128)S(1)}, f32[3,8,128]{2,1,0:T(8,128)S(1)}, u32[]{:S(2)}, u32[]{:S(2)}) collective-permute-start(f32[3,8,128]{2,1,0:T(8,128)S(1)} %get-tuple-element.41), channel_id=1, source_target_pairs={{0,64},{1,65},{2,66},{3,67},{4,68},{5,69},{6,70},{7,71},{8,72},{9,... | collective-permute-start | bytes 36872 | tf_op jit(solution)/shard_map/ppermute | solution.py:38
  79.3 2.7 %collective-permute-start.16 = (f32[8,128,256]{2,1,0:T(8,128)S(1)}, f32[8,128,256]{2,1,0:T(8,128)S(1)}, u32[]{:S(2)}, u32[]{:S(2)}) collective-permute-start(f32[8,128,256]{2,1,0:T(8,128)S(1)} %get-tuple-element.47), channel_id=1, source_target_pairs={{0,64},{1,65},{2,66},{3,67},{4,68},{5,69},{6,70},{7,71},{8,72},{9,... | collective-permute-start | bytes 3145736 | tf_op jit(solution)/shard_map/ppermute | solution.py:38
  79.5 14.5 %collective-permute-start.17 = (f32[520,256]{1,0:T(8,128)S(1)}, f32[520,256]{1,0:T(8,128)S(1)}, u32[]{:S(2)}, u32[]{:S(2)}) collective-permute-start(f32[520,256]{1,0:T(8,128)S(1)} %get-tuple-element.49), channel_id=1, source_target_pairs={{0,32},{1,33},{2,34},{3,35},{4,36},{5,37},{6,38},{7,39},{8,40},{9,... | collective-permute-start | bytes 1597448 | tf_op jit(solution)/shard_map/ppermute | solution.py:38
  81.1 15.3 %collective-permute-start.18 = (f32[520,256]{1,0:T(8,128)S(1)}, f32[520,256]{1,0:T(8,128)S(1)}, u32[]{:S(2)}, u32[]{:S(2)}) collective-permute-start(f32[520,256]{1,0:T(8,128)S(1)} %get-tuple-element.50), channel_id=1, source_target_pairs={{0,160},{1,161},{2,162},{3,163},{4,164},{5,165},{6,166},{7,167},{8... | collective-permute-start | bytes 1597448 | tf_op jit(solution)/shard_map/ppermute | solution.py:38
  97.5 31.9 %all-to-all-start.1 = ((f32[8,128,256]{2,1,0:T(8,128)}), f32[8,128,256]{2,1,0:T(8,128)S(1)}, u32[]{:S(2)}, u32[]{:S(2)}) async-start(f32[8,128,256]{2,1,0:T(8,128)} %get-tuple-element.57), calls=%async_computation.1 | async-start | bytes 2097152 | tf_op jit(solution)/shard_map/all_to_all | solution.py:434
  101.1 14.7 %collective-permute-start.19 = (f32[264,256]{1,0:T(8,128)S(1)}, f32[264,256]{1,0:T(8,128)S(1)}, u32[]{:S(2)}, u32[]{:S(2)}) collective-permute-start(f32[264,256]{1,0:T(8,128)S(1)} %get-tuple-element.53), channel_id=1, source_target_pairs={{0,8},{1,9},{2,10},{3,11},{4,12},{5,13},{6,14},{7,15},{8,16},{9,17... | collective-permute-start | bytes 811016 | tf_op jit(solution)/shard_map/ppermute | solution.py:38
  102.2 13.6 %collective-permute-start.20 = (f32[264,256]{1,0:T(8,128)S(1)}, f32[264,256]{1,0:T(8,128)S(1)}, u32[]{:S(2)}, u32[]{:S(2)}) collective-permute-start(f32[264,256]{1,0:T(8,128)S(1)} %get-tuple-element.54), channel_id=1, source_target_pairs={{0,16},{1,17},{2,18},{3,19},{4,20},{5,21},{6,22},{7,23},{8,24},{9,... | collective-permute-start | bytes 811016 | tf_op jit(solution)/shard_map/ppermute | solution.py:38
  103.9 12.5 %collective-permute-start.21 = (f32[264,256]{1,0:T(8,128)S(1)}, f32[264,256]{1,0:T(8,128)S(1)}, u32[]{:S(2)}, u32[]{:S(2)}) collective-permute-start(f32[264,256]{1,0:T(8,128)S(1)} %get-tuple-element.55), channel_id=1, source_target_pairs={{0,24},{1,25},{2,26},{3,27},{4,28},{5,29},{6,30},{7,31},{8,0},{9,1... | collective-permute-start | bytes 811016 | tf_op jit(solution)/shard_map/ppermute | solution.py:38
  116.5 8.9 %collective-permute-start.22 = (f32[264,256]{1,0:T(8,128)S(1)}, f32[264,256]{1,0:T(8,128)S(1)}, u32[]{:S(2)}, u32[]{:S(2)}) collective-permute-start(f32[264,256]{1,0:T(8,128)S(1)} %land_kernel.1.mine), channel_id=1, source_target_pairs={{0,128},{1,129},{2,130},{3,131},{4,132},{5,133},{6,134},{7,135},{8... | collective-permute-start | bytes 811016 | tf_op jit(solution)/shard_map/ppermute | solution.py:38
  117.7 7.7 %collective-permute-start.23 = (f32[264,256]{1,0:T(8,128)S(1)}, f32[264,256]{1,0:T(8,128)S(1)}, u32[]{:S(2)}, u32[]{:S(2)}) collective-permute-start(f32[264,256]{1,0:T(8,128)S(1)} %land_kernel.1.mine), channel_id=1, source_target_pairs={{0,64},{1,65},{2,66},{3,67},{4,68},{5,69},{6,70},{7,71},{8,72},{9,... | collective-permute-start | bytes 811016 | tf_op jit(solution)/shard_map/ppermute | solution.py:38
  125.4 1.5 %collective-permute-start.24 = (f32[264,256]{1,0:T(8,128)S(1)}, f32[264,256]{1,0:T(8,128)S(1)}, u32[]{:S(2)}, u32[]{:S(2)}) collective-permute-start(f32[264,256]{1,0:T(8,128)S(1)} %collective-permute-done.22.mine2), channel_id=1, source_target_pairs={{0,64},{1,65},{2,66},{3,67},{4,68},{5,69},{6,70},{7,71},{8,72},{9,... | collective-permute-start | bytes 811016 | tf_op jit(solution)/shard_map/ppermute | solution.py:38
  (5 other events, 5.2 us)

commit v4 on v3

--- a/solution.py
+++ b/solution.py
@@ -119,20 +119,24 @@
     other[...] = both[at((1 - c) * n, n), :]
 
 
-def stack_kernel(a, b, c, out):
-    for k, ref in enumerate((a, b, c)):
-        out[k * HALF : (k + 1) * HALF, :] = ref[...]
-
-
-def pack_queries_kernel(pos_ref, q, qo, q4, qo4, r1, r2, r3, s1, s2, s3, mine, other):
+def stack_kernel(*refs):
+    *parts, out = refs
+    row = 0
+    for ref in parts:
+        n = ref.shape[0]
+        out[row : row + n, :] = ref[...]
+        row += n
+
+
+def pack_queries_kernel(pos_ref, q, qo, r2, r314, s2, s314, mine, other):
     z, c = pos_ref[0], pos_ref[1]
     mine[z], other[z] = q[...], qo[...]
-    mine[(z + 4) & 7], other[(z + 4) & 7] = q4[...], qo4[...]
-    for k, r, s in ((1, r1, s1), (2, r2, s2), (3, r3, s3)):
+    mine[(z + 4) & 7], other[(z + 4) & 7] = r314[4 * PAD :, :], s314[4 * PAD :, :]
+    for k, r, s, row in ((2, r2, s2, 0), (3, r314, s314, 0), (1, r314, s314, 2 * PAD)):
         step = k - 2 * c * k
         for ref, where in ((r, (z - step) & 7), (s, (z + step) & 7)):
-            mine[where] = ref[at(c * PAD, PAD), :]
-            other[where] = ref[at((1 - c) * PAD, PAD), :]
+            mine[where] = ref[at(row + c * PAD, PAD), :]
+            other[where] = ref[at(row + (1 - c) * PAD, PAD), :]
 
 
 def pack_items_kernel(pos_ref, own, near, across, far, y_own, y_rest, xh, xl):
@@ -359,21 +363,21 @@
     x1 = twin(items, "dx")
     qo = send(q, dc=1)
     (r0,) = small(pair_kernel, [pos, q, qo], [two])
-    r1 = twin(r0, "dz")
     r2 = twin(r0, "dz", 2)
     far = twin(own, "dx", 2)
     y0 = twin(own, "dy")
-    near, rest = small(part_kernel, [pos, x1, y0, r2], [half, half])
+    third, _ = small(part_kernel, [pos, r2, y0, far], [chunk, chunk])
+    (r20,) = small(stack_kernel, [r2, r0], [shape(4 * PAD, E)])
+    r31, q4 = twin(r20, "dz"), twin(third, "dz", 2)
+    near, rest = small(part_kernel, [pos, x1, third], [half, half])
     across = send(rest, dc=1)
     (rest,) = small(stack_kernel, [near, across, far], [shape(3 * HALF, E)])
     y_rest = twin(rest, "dy")
-    r3 = twin(r2, "dz")
-    s1, s2 = send(r1, dc=1), send(r2, dc=1)
-    third, _ = small(part_kernel, [pos, r2, far], [chunk, chunk])
-    q4 = twin(third, "dz", 2)
-    s3 = send(r3, dc=1)
+    (r314,) = small(stack_kernel, [r31, q4], [shape(5 * PAD, E)])
     mine, other = small(
-        pack_queries_kernel, [pos, q, qo, q4, send(q4, dc=1), r1, r2, r3, s1, s2, s3], [shape(ZN, PAD, E)] * 2
+        pack_queries_kernel,
+        [pos, q, qo, r2, r314, send(r2, dc=1), send(r314, dc=1)],
+        [shape(ZN, PAD, E)] * 2,
     )
     xh, xl = small(
         pack_items_kernel, [pos, own, near, across, far, y0, y_rest], [shape(LOCAL, E, dtype=bf16)] * 2
@@ -382,7 +386,6 @@
 
 
 def fold_kernel(lse_m, lse_o, g, a, b, o, held, *out):
-    held[...] = o[...]
     for d in range(4):
         at = slice(d * CUT, (d + 1) * CUT)
         out[d][:CUT] = g[d, :CUT] + a[at]
@@ -391,6 +394,19 @@
         out[d][HALF + 1 : HALF + 2] = a[4 * CUT : 4 * CUT + 1]
         out[d][HALF + 2 : HALF + 3] = b[4 * CUT : 4 * CUT + 1]
         out[d][HALF + 3 :] = jnp.zeros((5, E), f32)
+
+
+def fold(*operands):
+    anywhere = pl.BlockSpec(memory_space=pl.ANY)
+    return pl.pallas_call(
+        fold_kernel,
+        in_specs=[VMEM] * 5 + [anywhere],
+        out_specs=[anywhere] + [VMEM] * 4,
+        out_shape=[shape(ZN, ROWS, E)] + [shape(HALF + 8, E)] * 4,
+        input_output_aliases={5: 0},
+        compiler_params=params(10),
+        name="fold",
+    )(*operands)
 
 
 def land_kernel(m0, m1, m2, m3, out):
@@ -430,7 +446,7 @@
     oo, up, down, first = backward_a(pos, xh, xl, mine, other, *lse, sm1, so0, so1)
     a, b = send(up, dy=1), send(down, dy=-1)
     o, g = backward_b(pos, first, xh, xl, mine, other, *lse, sm0, sm1, so0, send(oo, dc=1))
-    o, m0, m1, m2, m3 = small(fold_kernel, [*lse, g, a, b, o], [shape(ZN, ROWS, E)] + [shape(HALF + 8, E)] * 4)
+    o, m0, m1, m2, m3 = fold(*lse, g, a, b, o)
     o = lax.all_to_all(o, "z", 0, 0, tiled=True)
     m2, m1, m3 = send(m2, dx=2), send(m1, dx=1), send(m3, dx=-1)
     (own,) = small(land_kernel, [m0, m1, m2, m3], [shape(HALF + 8, E)])

time: 131 us -> 129 us (0.985)
  waiting for transfers between devices: 40.3 us -> 43.8 us
  blocking collectives: 15.1 us -> 12.3 us
  starting transfers between devices: 31.2 us -> 29 us
    ppermute x8 -> x7, waiting for transfers between devices: 10.9 us -> 16.2 us  [twin(): lax.ppermute(a, AXES, [(down if i >> 6 & 1 else up)[i] for i in range(256)])]
    all_to_all x1, blocking collectives: 15.1 us -> 12.3 us  [body(): stats = lax.all_to_all(stats, 'z', 0, 0, tiled=True)]
    ppermute x17 -> x15, waiting for transfers between devices: 28.4 us -> 25.8 us  [send(): return lax.ppermute(a, AXES, pairs(**shift))]
    ppermute x8 -> x7, starting transfers between devices: 15.1 us -> 13.8 us  [twin(): lax.ppermute(a, AXES, [(down if i >> 6 & 1 else up)[i] for i in range(256)])]
    pallas_call x13 -> x14, Pallas kernels: 8.07 us -> 6.98 us  [small(): pl.pallas_call(kernel, in_specs=[SMEM if a.ndim == 1 else VMEM for a in i...]
    ppermute x17 -> x15, starting transfers between devices: 12.6 us -> 11.6 us  [send(): return lax.ppermute(a, AXES, pairs(**shift))]
  transfers between devices with their start and end apart: 26 -> 23, of which waited for: 16 -> 12; matrix products, arithmetic and copies ran while one was open for 0% -> 0% of each run, Pallas kernels for 16% -> 17%
where the time goes in v4:
time: 129 us; the launch traced here: 128 us
  waiting for transfers between devices  43.8 us (34%)
  Pallas kernels  39.9 us (31%)
  starting transfers between devices  29 us (22%)
  blocking collectives  12.3 us (10%)
  local copies, waits for them, and re-layouts  2.6 us (2%)
    ppermute x15, waiting for transfers between devices, send(): return lax.ppermute(a, AXES, pairs(**shift))  25.8 us
    ppermute x7, waiting for transfers between devices, twin(): lax.ppermute(a, AXES, [(down if i >> 6 & 1 else up)[i] for i in range(256)])  16.2 us
    ppermute x7, starting transfers between devices, twin(): lax.ppermute(a, AXES, [(down if i >> 6 & 1 else up)[i] for i in range(256)])  13.8 us
    all_to_all x1, blocking collectives, body(): stats = lax.all_to_all(stats, 'z', 0, 0, tiled=True)  12.3 us
    ppermute x15, starting transfers between devices, send(): return lax.ppermute(a, AXES, pairs(**shift))  11.6 us
    pallas_call x1, Pallas kernels, backward_b(): pl.pallas_call(backward_b_kernel, grid=(ZN,), in_specs=[SMEM, SMEM, X_SPE...  11.4 us
    pallas_call x2, Pallas kernels, forward(): pl.pallas_call(forward_kernel, grid=(4,), in_specs=[SMEM, pl.BlockSpec((L...  10.9 us
    pallas_call x1, Pallas kernels, backward_a(): pl.pallas_call(backward_a_kernel, grid=(ZN,), in_specs=[SMEM, X_SPEC, X_S...  10.5 us
  transfers between devices with their start and end apart: 23, of which 12 were waited for; matrix products, arithmetic and copies ran while one was open for 0% of the time, Pallas kernels for 17%

profile of v4, /device:TPU:24, one launch (start us, length us, event | category | flops | bytes accessed | tf_op | source)
XLA Modules:
  0.0 128.4 jit_solution(15052200374176608890)
XLA Ops:
  4.0 1.6 %collective-permute-start = (f32[512,256]{1,0:T(8,128)S(1)}, f32[512,256]{1,0:T(8,128)S(1)}, u32[]{:S(2)}, u32[]{:S(2)}) collective-permute-start(f32[512,256]{1,0:T(8,128)S(1)} %copy-done), channel_id=1, source_target_pairs={{0,8},{1,9},{2,10},{3,11},{4,12},{5,13},{6,14},{7,15},{8,16},{9,17... | collective-permute-start | bytes 1572872 | tf_op jit(solution)/shard_map/ppermute | solution.py:43
  6.1 3.3 %collective-permute-start.2 = (f32[272,256]{1,0:T(8,128)S(1)}, f32[272,256]{1,0:T(8,128)S(1)}, u32[]{:S(2)}, u32[]{:S(2)}) collective-permute-start(f32[272,256]{1,0:T(8,128)S(1)} %pair_kernel.1.refs_1_), channel_id=1, source_target_pairs={{0,2},{1,3},{2,4},{3,5},{4,6},{5,7},{6,0},{7,1},{8,10},{9,11},{10,... | collective-permute-start | bytes 835592 | tf_op jit(solution)/shard_map/ppermute | solution.py:43
  9.5 2.8 %collective-permute-start.4 = (f32[256,256]{1,0:T(8,128)S(1)}, f32[256,256]{1,0:T(8,128)S(1)}, u32[]{:S(2)}, u32[]{:S(2)}) collective-permute-start(f32[256,256]{1,0:T(8,128)S(1)} %get-tuple-element.31.own), channel_id=1, source_target_pairs={{0,16},{1,17},{2,18},{3,19},{4,20},{5,21},{6,22},{7,23},{8,24},{9,... | collective-permute-start | bytes 786440 | tf_op jit(solution)/shard_map/ppermute | solution.py:43
  12.5 5.1 %collective-permute-done.2.both.refs_0_.r2 = f32[272,256]{1,0:T(8,128)S(1)} collective-permute-done((f32[272,256]{1,0:T(8,128)S(1)}, f32[272,256]{1,0:T(8,128)S(1)}, u32[]{:S(2)}, u32[]{:S(2)}) %collective-permute-start.2) | collective-permute-done | bytes 278560 | tf_op jit(solution)/shard_map/ppermute | solution.py:43
  17.7 3.5 %collective-permute-start.7 = (f32[544,256]{1,0:T(8,128)S(1)}, f32[544,256]{1,0:T(8,128)S(1)}, u32[]{:S(2)}, u32[]{:S(2)}) collective-permute-start(f32[544,256]{1,0:T(8,128)S(1)} %stack_kernel.4), channel_id=1, source_target_pairs={{0,1},{1,2},{2,3},{3,4},{4,5},{5,6},{6,7},{7,0},{8,9},{9,10},{10,1... | collective-permute-start | bytes 1671176 | tf_op jit(solution)/shard_map/ppermute | solution.py:43
  24.3 2.1 %collective-permute-start.8 = (f32[136,256]{1,0:T(8,128)S(1)}, f32[136,256]{1,0:T(8,128)S(1)}, u32[]{:S(2)}, u32[]{:S(2)}) collective-permute-start(f32[136,256]{1,0:T(8,128)S(1)} %get-tuple-element.33.refs_0_), channel_id=1, source_target_pairs={{0,2},{1,3},{2,4},{3,5},{4,6},{5,7},{6,0},{7,1},{8,10},{9,11},{10,... | collective-permute-start | bytes 417800 | tf_op jit(solution)/shard_map/ppermute | solution.py:43
  26.7 6.2 %collective-permute-done.8.refs_1_ = f32[136,256]{1,0:T(8,128)S(1)} collective-permute-done((f32[136,256]{1,0:T(8,128)S(1)}, f32[136,256]{1,0:T(8,128)S(1)}, u32[]{:S(2)}, u32[]{:S(2)}) %collective-permute-start.8) | collective-permute-done | bytes 139296 | tf_op jit(solution)/shard_map/ppermute | solution.py:43
  33.5 4.9 %collective-permute-done.6.y_rest = f32[768,256]{1,0:T(8,128)S(1)} collective-permute-done((f32[768,256]{1,0:T(8,128)S(1)}, f32[768,256]{1,0:T(8,128)S(1)}, u32[]{:S(2)}, u32[]{:S(2)}) %collective-permute-start.6) | collective-permute-done | bytes 786464 | tf_op jit(solution)/shard_map/ppermute | solution.py:43
  40.1 5.5 %forward.3 = (f32[4,4,256,256]{3,2,1,0:T(8,128)S(1)}, f32[4,4,256,256]{3,2,1,0:T(8,128)S(1)}, f32[3,8,128]{2,1,0:T(8,128)S(1)}) custom-call(s32[4]{0:T(128)S(1)} %pad_add_fusion.pos_ref, bf16[2048,256]{1,0:T(8,128)(2,1)S(1)} %get-tuple-element.36.xh, bf16[2048,256]{1,0:T(8,128)(2,1)S(1)} %get-tuple-element.37.xl, ...), custom_call_target="tpu_custom_call" | custom-call | flops 3221225472 | bytes 10485760 | tf_op jit(solution)/shard_map/forward/pallas_call | solution.py:221
  45.6 3.3 %collective-permute-start.11 = (f32[3,8,128]{2,1,0:T(8,128)S(1)}, f32[3,8,128]{2,1,0:T(8,128)S(1)}, u32[]{:S(2)}, u32[]{:S(2)}) collective-permute-start(f32[3,8,128]{2,1,0:T(8,128)S(1)} %get-tuple-element.41), channel_id=1, source_target_pairs={{0,64},{1,65},{2,66},{3,67},{4,68},{5,69},{6,70},{7,71},{8,72},{9,... | collective-permute-start | bytes 36872 | tf_op jit(solution)/shard_map/ppermute | solution.py:38
  48.9 5.4 %forward.2 = (f32[4,4,256,256]{3,2,1,0:T(8,128)S(1)}, f32[4,4,256,256]{3,2,1,0:T(8,128)S(1)}, f32[3,8,128]{2,1,0:T(8,128)S(1)}) custom-call(s32[4]{0:T(128)S(1)} %pad_add_fusion.pos_ref, bf16[2048,256]{1,0:T(8,128)(2,1)S(1)} %get-tuple-element.36.xh, bf16[2048,256]{1,0:T(8,128)(2,1)S(1)} %get-tuple-element.37.xl, f32[8,136,256]{2,1,0:T(8,128)S(1)} %get-tuple-element.38.q_ref.mine), custom_call_target="tpu_custom_call" | custom-call | flops 3221225472 | bytes 10485760 | tf_op jit(solution)/shard_map/forward/pallas_call | solution.py:221
  54.4 12.3 %all_to_all.10.got = f32[8,3,8,128]{3,2,1,0:T(8,128)S(1)} all-to-all(f32[8,3,8,128]{3,2,1,0:T(8,128)S(1)} %spread_kernel.1), channel_id=1, replica_groups=mesh['yh'=2,'c'=2,'yl'=2,'x'=4,'z'=8] {'z'}, dimensions={0} | all-to-all | bytes 196608 | tf_op jit(solution)/shard_map/all_to_all | solution.py:443
  68.3 10.5 %backward_a.1 = (f32[8,128,256]{2,1,0:T(8,128)S(1)}, f32[520,256]{1,0:T(8,128)S(1)}, f32[520,256]{1,0:T(8,128)S(1)}, f32[1]{0:T(128)}) custom-call(s32[4]{0:T(128)S(1)} %pad_add_fusion.pos_ref, bf16[2048,256]{1,0:T(8,128)(2,1)S(1)} %get-tuple-element.36.xh, bf16[2048,256]{1,0:T(8,128)(2,1)S(1)} %get-tuple-element.37.xl, ...), custom_call_target="tpu_custom_call" | custom-call | flops 6442450944 | bytes 16777216 | tf_op jit(solution)/shard_map/backward_a/pallas_call | solution.py:332
  79.0 1.4 %collective-permute-start.14 = (f32[520,256]{1,0:T(8,128)S(1)}, f32[520,256]{1,0:T(8,128)S(1)}, u32[]{:S(2)}, u32[]{:S(2)}) collective-permute-start(f32[520,256]{1,0:T(8,128)S(1)} %get-tuple-element.49), channel_id=1, source_target_pairs={{0,32},{1,33},{2,34},{3,35},{4,36},{5,37},{6,38},{7,39},{8,40},{9,... | collective-permute-start | bytes 1597448 | tf_op jit(solution)/shard_map/ppermute | solution.py:38
  81.5 11.4 %backward_b.1 = (f32[8,128,256]{2,1,0:T(8,128)}, f32[4,256,256]{2,1,0:T(8,128)S(1)}) custom-call(s32[4]{0:T(128)S(1)} %pad_add_fusion.pos_ref, f32[1]{0:T(128)} %get-tuple-element.45.token, bf16[2048,256]{1,0:T(8,128)(2,1)S(1)} %get-tuple-element.36.xh, bf16[2048,256]{1,0:T(8,128)(2,1)S(1)} %get-tuple-element.37.xl, ...), custom_call_target="tpu_custom_call" | custom-call | flops 6442450944 | bytes 16777216 | tf_op jit(solution)/shard_map/backward_b/pallas_call | solution.py:347
  93.3 2.4 %collective-permute-done.15.b = f32[520,256]{1,0:T(8,128)S(1)} collective-permute-done((f32[520,256]{1,0:T(8,128)S(1)}, f32[520,256]{1,0:T(8,128)S(1)}, u32[]{:S(2)}, u32[]{:S(2)}) %collective-permute-start.15) | collective-permute-done | bytes 532512 | tf_op jit(solution)/shard_map/ppermute | solution.py:38
  95.8 3.6 %all-to-all-start.1 = ((f32[8,128,256]{2,1,0:T(8,128)}), f32[8,128,256]{2,1,0:T(8,128)S(1)}, u32[]{:S(2)}, u32[]{:S(2)}) async-start(f32[8,128,256]{2,1,0:T(8,128)} %get-tuple-element.57), calls=%async_computation.1 | async-start | bytes 2097152 | tf_op jit(solution)/shard_map/all_to_all | solution.py:450
  99.5 1.4 %collective-permute-start.17 = (f32[264,256]{1,0:T(8,128)S(1)}, f32[264,256]{1,0:T(8,128)S(1)}, u32[]{:S(2)}, u32[]{:S(2)}) collective-permute-start(f32[264,256]{1,0:T(8,128)S(1)} %get-tuple-element.54), channel_id=1, source_target_pairs={{0,16},{1,17},{2,18},{3,19},{4,20},{5,21},{6,22},{7,23},{8,24},{9,... | collective-permute-start | bytes 811016 | tf_op jit(solution)/shard_map/ppermute | solution.py:38
  100.9 2.0 %collective-permute-start.18 = (f32[264,256]{1,0:T(8,128)S(1)}, f32[264,256]{1,0:T(8,128)S(1)}, u32[]{:S(2)}, u32[]{:S(2)}) collective-permute-start(f32[264,256]{1,0:T(8,128)S(1)} %get-tuple-element.55), channel_id=1, source_target_pairs={{0,24},{1,25},{2,26},{3,27},{4,28},{5,29},{6,30},{7,31},{8,0},{9,1... | collective-permute-start | bytes 811016 | tf_op jit(solution)/shard_map/ppermute | solution.py:38
  102.9 11.2 %collective-permute-done.16.m1 = f32[264,256]{1,0:T(8,128)S(1)} collective-permute-done((f32[264,256]{1,0:T(8,128)S(1)}, f32[264,256]{1,0:T(8,128)S(1)}, u32[]{:S(2)}, u32[]{:S(2)}) %collective-permute-start.16) | collective-permute-done | bytes 270368 | tf_op jit(solution)/shard_map/ppermute | solution.py:38
  115.0 8.0 %collective-permute-done.19.mine2 = f32[264,256]{1,0:T(8,128)S(1)} collective-permute-done((f32[264,256]{1,0:T(8,128)S(1)}, f32[264,256]{1,0:T(8,128)S(1)}, u32[]{:S(2)}, u32[]{:S(2)}) %collective-permute-start.19) | collective-permute-done | bytes 270368 | tf_op jit(solution)/shard_map/ppermute | solution.py:38
  123.1 1.5 %collective-permute-done.21.other2 = f32[264,256]{1,0:T(8,128)S(1)} collective-permute-done((f32[264,256]{1,0:T(8,128)S(1)}, f32[264,256]{1,0:T(8,128)S(1)}, u32[]{:S(2)}, u32[]{:S(2)}) %collective-permute-start.21) | collective-permute-done | bytes 270368 | tf_op jit(solution)/shard_map/ppermute | solution.py:38
  124.6 1.4 %join_kernel.1 = (f32[512,256]{1,0:T(8,128)}, f32[1]{0:T(128)}) custom-call(s32[4]{0:T(128)S(1)} %pad_add_fusion.pos_ref, f32[264,256]{1,0:T(8,128)S(1)} %land_kernel.1.mine, f32[264,256]{1,0:T(8,128)S(1)} %collective-permute-done.19.mine2, f32[264,256]{1,0:T(8,128)S(1)} %collective-permute-done.20.other, f32[264,256]{1,0:T(8,128)S(1)} %collective-permute-done.21.other2), custom_call_target="tpu_custom_call" | custom-call | tf_op jit(solution)/shard_map/join_kernel/pallas_call | solution.py:88
  126.0 1.7 %all-to-all-done.1.got = f32[8,128,256]{2,1,0:T(8,128)S(1)} async-done(((f32[8,128,256]{2,1,0:T(8,128)}), f32[8,128,256]{2,1,0:T(8,128)S(1)}, u32[]{:S(2)}, u32[]{:S(2)}) %all-to-all-start.1) | async-done | bytes 1048608 | tf_op jit(solution)/shard_map/all_to_all | solution.py:450
  (49 shorter events, 15.1 us)
Async XLA Ops:
  0.7 1.0 copy-start
  3.9 1.7 %collective-permute-start.1 = (f32[136,256]{1,0:T(8,128)S(1)}, f32[136,256]{1,0:T(8,128)S(1)}, u32[]{:S(2)}, u32[]{:S(2)}) collective-permute-start(f32[136,256]{1,0:T(8,128)S(1)} %get-tuple-element.32.mine.q), channel_id=1, source_target_pairs={{0,64},{1,65},{2,66},{3,67},{4,68},{5,69},{6,70},{7,71},{8,72},{9,... | collective-permute-start | bytes 417800 | tf_op jit(solution)/shard_map/ppermute | solution.py:38
  4.0 18.4 %collective-permute-start = (f32[512,256]{1,0:T(8,128)S(1)}, f32[512,256]{1,0:T(8,128)S(1)}, u32[]{:S(2)}, u32[]{:S(2)}) collective-permute-start(f32[512,256]{1,0:T(8,128)S(1)} %copy-done), channel_id=1, source_target_pairs={{0,8},{1,9},{2,10},{3,11},{4,12},{5,13},{6,14},{7,15},{8,16},{9,17... | collective-permute-start | bytes 1572872 | tf_op jit(solution)/shard_map/ppermute | solution.py:43
  6.1 11.5 %collective-permute-start.2 = (f32[272,256]{1,0:T(8,128)S(1)}, f32[272,256]{1,0:T(8,128)S(1)}, u32[]{:S(2)}, u32[]{:S(2)}) collective-permute-start(f32[272,256]{1,0:T(8,128)S(1)} %pair_kernel.1.refs_1_), channel_id=1, source_target_pairs={{0,2},{1,3},{2,4},{3,5},{4,6},{5,7},{6,0},{7,1},{8,10},{9,11},{10,... | collective-permute-start | bytes 835592 | tf_op jit(solution)/shard_map/ppermute | solution.py:43
  9.5 11.7 %collective-permute-start.4 = (f32[256,256]{1,0:T(8,128)S(1)}, f32[256,256]{1,0:T(8,128)S(1)}, u32[]{:S(2)}, u32[]{:S(2)}) collective-permute-start(f32[256,256]{1,0:T(8,128)S(1)} %get-tuple-element.31.own), channel_id=1, source_target_pairs={{0,16},{1,17},{2,18},{3,19},{4,20},{5,21},{6,22},{7,23},{8,24},{9,... | collective-permute-start | bytes 786440 | tf_op jit(solution)/shard_map/ppermute | solution.py:43
  12.3 8.9 %collective-permute-start.3 = (f32[256,256]{1,0:T(8,128)S(1)}, f32[256,256]{1,0:T(8,128)S(1)}, u32[]{:S(2)}, u32[]{:S(2)}) collective-permute-start(f32[256,256]{1,0:T(8,128)S(1)} %get-tuple-element.31.own), channel_id=1, source_target_pairs={{0,32},{1,33},{2,34},{3,35},{4,36},{5,37},{6,38},{7,39},{8,40},{9,... | collective-permute-start | bytes 786440 | tf_op jit(solution)/shard_map/ppermute | solution.py:43
  17.7 15.2 %collective-permute-start.7 = (f32[544,256]{1,0:T(8,128)S(1)}, f32[544,256]{1,0:T(8,128)S(1)}, u32[]{:S(2)}, u32[]{:S(2)}) collective-permute-start(f32[544,256]{1,0:T(8,128)S(1)} %stack_kernel.4), channel_id=1, source_target_pairs={{0,1},{1,2},{2,3},{3,4},{4,5},{5,6},{6,7},{7,0},{8,9},{9,10},{10,1... | collective-permute-start | bytes 1671176 | tf_op jit(solution)/shard_map/ppermute | solution.py:43
  23.0 3.4 %collective-permute-start.5 = (f32[256,256]{1,0:T(8,128)S(1)}, f32[256,256]{1,0:T(8,128)S(1)}, u32[]{:S(2)}, u32[]{:S(2)}) collective-permute-start(f32[256,256]{1,0:T(8,128)S(1)} %get-tuple-element.35), channel_id=1, source_target_pairs={{0,64},{1,65},{2,66},{3,67},{4,68},{5,69},{6,70},{7,71},{8,72},{9,... | collective-permute-start | bytes 786440 | tf_op jit(solution)/shard_map/ppermute | solution.py:38
  24.3 8.6 %collective-permute-start.8 = (f32[136,256]{1,0:T(8,128)S(1)}, f32[136,256]{1,0:T(8,128)S(1)}, u32[]{:S(2)}, u32[]{:S(2)}) collective-permute-start(f32[136,256]{1,0:T(8,128)S(1)} %get-tuple-element.33.refs_0_), channel_id=1, source_target_pairs={{0,2},{1,3},{2,4},{3,5},{4,6},{5,7},{6,0},{7,1},{8,10},{9,11},{10,... | collective-permute-start | bytes 417800 | tf_op jit(solution)/shard_map/ppermute | solution.py:43
  26.4 12.1 %collective-permute-start.6 = (f32[768,256]{1,0:T(8,128)S(1)}, f32[768,256]{1,0:T(8,128)S(1)}, u32[]{:S(2)}, u32[]{:S(2)}) collective-permute-start(f32[768,256]{1,0:T(8,128)S(1)} %stack_kernel.3), channel_id=1, source_target_pairs={{0,32},{1,33},{2,34},{3,35},{4,36},{5,37},{6,38},{7,39},{8,40},{9,... | collective-permute-start | bytes 2359304 | tf_op jit(solution)/shard_map/ppermute | solution.py:43
  32.9 6.4 %collective-permute-start.10 = (f32[680,256]{1,0:T(8,128)S(1)}, f32[680,256]{1,0:T(8,128)S(1)}, u32[]{:S(2)}, u32[]{:S(2)}) collective-permute-start(f32[680,256]{1,0:T(8,128)S(1)} %stack_kernel.5.r314), channel_id=1, source_target_pairs={{0,64},{1,65},{2,66},{3,67},{4,68},{5,69},{6,70},{7,71},{8,72},{9,... | collective-permute-start | bytes 2088968 | tf_op jit(solution)/shard_map/ppermute | solution.py:38
  33.1 6.2 %collective-permute-start.9 = (f32[272,256]{1,0:T(8,128)S(1)}, f32[272,256]{1,0:T(8,128)S(1)}, u32[]{:S(2)}, u32[]{:S(2)}) collective-permute-start(f32[272,256]{1,0:T(8,128)S(1)} %collective-permute-done.2.both.refs_0_.r2), channel_id=1, source_target_pairs={{0,64},{1,65},{2,66},{3,67},{4,68},{5,69},{6,70},{7,71},{8,72},{9,... | collective-permute-start | bytes 835592 | tf_op jit(solution)/shard_map/ppermute | solution.py:38
  45.6 8.8 %collective-permute-start.11 = (f32[3,8,128]{2,1,0:T(8,128)S(1)}, f32[3,8,128]{2,1,0:T(8,128)S(1)}, u32[]{:S(2)}, u32[]{:S(2)}) collective-permute-start(f32[3,8,128]{2,1,0:T(8,128)S(1)} %get-tuple-element.41), channel_id=1, source_target_pairs={{0,64},{1,65},{2,66},{3,67},{4,68},{5,69},{6,70},{7,71},{8,72},{9,... | collective-permute-start | bytes 36872 | tf_op jit(solution)/shard_map/ppermute | solution.py:38
  66.8 1.4 %collective-permute-start.12 = (f32[16,128]{1,0:T(8,128)S(1)}, f32[16,128]{1,0:T(8,128)S(1)}, u32[]{:S(2)}, u32[]{:S(2)}) collective-permute-start(f32[16,128]{1,0:T(8,128)S(1)} %merge_kernel.1.lse_m), channel_id=1, source_target_pairs={{0,64},{1,65},{2,66},{3,67},{4,68},{5,69},{6,70},{7,71},{8,72},{9,... | collective-permute-start | bytes 24584 | tf_op jit(solution)/shard_map/ppermute | solution.py:38
  78.7 2.7 %collective-permute-start.13 = (f32[8,128,256]{2,1,0:T(8,128)S(1)}, f32[8,128,256]{2,1,0:T(8,128)S(1)}, u32[]{:S(2)}, u32[]{:S(2)}) collective-permute-start(f32[8,128,256]{2,1,0:T(8,128)S(1)} %get-tuple-element.47), channel_id=1, source_target_pairs={{0,64},{1,65},{2,66},{3,67},{4,68},{5,69},{6,70},{7,71},{8,72},{9,... | collective-permute-start | bytes 3145736 | tf_op jit(solution)/shard_map/ppermute | solution.py:38
  79.0 14.3 %collective-permute-start.14 = (f32[520,256]{1,0:T(8,128)S(1)}, f32[520,256]{1,0:T(8,128)S(1)}, u32[]{:S(2)}, u32[]{:S(2)}) collective-permute-start(f32[520,256]{1,0:T(8,128)S(1)} %get-tuple-element.49), channel_id=1, source_target_pairs={{0,32},{1,33},{2,34},{3,35},{4,36},{5,37},{6,38},{7,39},{8,40},{9,... | collective-permute-start | bytes 1597448 | tf_op jit(solution)/shard_map/ppermute | solution.py:38
  80.4 15.3 %collective-permute-start.15 = (f32[520,256]{1,0:T(8,128)S(1)}, f32[520,256]{1,0:T(8,128)S(1)}, u32[]{:S(2)}, u32[]{:S(2)}) collective-permute-start(f32[520,256]{1,0:T(8,128)S(1)} %get-tuple-element.50), channel_id=1, source_target_pairs={{0,160},{1,161},{2,162},{3,163},{4,164},{5,165},{6,166},{7,167},{8... | collective-permute-start | bytes 1597448 | tf_op jit(solution)/shard_map/ppermute | solution.py:38
  95.8 31.9 %all-to-all-start.1 = ((f32[8,128,256]{2,1,0:T(8,128)}), f32[8,128,256]{2,1,0:T(8,128)S(1)}, u32[]{:S(2)}, u32[]{:S(2)}) async-start(f32[8,128,256]{2,1,0:T(8,128)} %get-tuple-element.57), calls=%async_computation.1 | async-start | bytes 2097152 | tf_op jit(solution)/shard_map/all_to_all | solution.py:450
  99.4 14.7 %collective-permute-start.16 = (f32[264,256]{1,0:T(8,128)S(1)}, f32[264,256]{1,0:T(8,128)S(1)}, u32[]{:S(2)}, u32[]{:S(2)}) collective-permute-start(f32[264,256]{1,0:T(8,128)S(1)} %get-tuple-element.53), channel_id=1, source_target_pairs={{0,8},{1,9},{2,10},{3,11},{4,12},{5,13},{6,14},{7,15},{8,16},{9,17... | collective-permute-start | bytes 811016 | tf_op jit(solution)/shard_map/ppermute | solution.py:38
  99.5 14.6 %collective-permute-start.17 = (f32[264,256]{1,0:T(8,128)S(1)}, f32[264,256]{1,0:T(8,128)S(1)}, u32[]{:S(2)}, u32[]{:S(2)}) collective-permute-start(f32[264,256]{1,0:T(8,128)S(1)} %get-tuple-element.54), channel_id=1, source_target_pairs={{0,16},{1,17},{2,18},{3,19},{4,20},{5,21},{6,22},{7,23},{8,24},{9,... | collective-permute-start | bytes 811016 | tf_op jit(solution)/shard_map/ppermute | solution.py:38
  100.9 13.8 %collective-permute-start.18 = (f32[264,256]{1,0:T(8,128)S(1)}, f32[264,256]{1,0:T(8,128)S(1)}, u32[]{:S(2)}, u32[]{:S(2)}) collective-permute-start(f32[264,256]{1,0:T(8,128)S(1)} %get-tuple-element.55), channel_id=1, source_target_pairs={{0,24},{1,25},{2,26},{3,27},{4,28},{5,29},{6,30},{7,31},{8,0},{9,1... | collective-permute-start | bytes 811016 | tf_op jit(solution)/shard_map/ppermute | solution.py:38
  114.8 8.3 %collective-permute-start.19 = (f32[264,256]{1,0:T(8,128)S(1)}, f32[264,256]{1,0:T(8,128)S(1)}, u32[]{:S(2)}, u32[]{:S(2)}) collective-permute-start(f32[264,256]{1,0:T(8,128)S(1)} %land_kernel.1.mine), channel_id=1, source_target_pairs={{0,128},{1,129},{2,130},{3,131},{4,132},{5,133},{6,134},{7,135},{8... | collective-permute-start | bytes 811016 | tf_op jit(solution)/shard_map/ppermute | solution.py:38
  115.0 8.0 %collective-permute-start.20 = (f32[264,256]{1,0:T(8,128)S(1)}, f32[264,256]{1,0:T(8,128)S(1)}, u32[]{:S(2)}, u32[]{:S(2)}) collective-permute-start(f32[264,256]{1,0:T(8,128)S(1)} %land_kernel.1.mine), channel_id=1, source_target_pairs={{0,64},{1,65},{2,66},{3,67},{4,68},{5,69},{6,70},{7,71},{8,72},{9,... | collective-permute-start | bytes 811016 | tf_op jit(solution)/shard_map/ppermute | solution.py:38
  123.1 1.5 %collective-permute-start.21 = (f32[264,256]{1,0:T(8,128)S(1)}, f32[264,256]{1,0:T(8,128)S(1)}, u32[]{:S(2)}, u32[]{:S(2)}) collective-permute-start(f32[264,256]{1,0:T(8,128)S(1)} %collective-permute-done.19.mine2), channel_id=1, source_target_pairs={{0,64},{1,65},{2,66},{3,67},{4,68},{5,69},{6,70},{7,71},{8,72},{9,... | collective-permute-start | bytes 811016 | tf_op jit(solution)/shard_map/ppermute | solution.py:38
  (2 other events, 1.6 us)

commit v5 on v4

--- a/solution.py
+++ b/solution.py
@@ -11,6 +11,9 @@
 PAD = 136
 HALF = 256
 CUT = HALF // 2
+N = 4
+W = N * ROWS
+STEPS = 8 // N
 PIECES = 8
 LOCAL = PIECES * HALF
 AXES = ("yh", "c", "yl", "x", "z")
@@ -72,7 +75,7 @@
 
 
 def local_labels(pos_ref, q_ref):
-    lab = cat([q_ref[0, ROWS : ROWS + 1, :ROWS], q_ref[1, ROWS : ROWS + 1, :ROWS]], 1)
+    lab = cat([q_ref[k, ROWS : ROWS + 1, :ROWS] for k in range(N)], 1)
     lab = lab.astype(jnp.int32)
     z, c, yl, x = pos_ref[0], pos_ref[1], pos_ref[2], pos_ref[3]
     here = ((lab >> 9) & 7 == z) & ((lab >> 8) & 1 == c)
@@ -81,7 +84,7 @@
 
 
 def query_rows(q_ref):
-    return cat([q_ref[0, :ROWS, :], q_ref[1, :ROWS, :]], 0) * (E**-0.5)
+    return cat([q_ref[k, :ROWS, :] for k in range(N)], 0) * (E**-0.5)
 
 
 def small(kernel, ins, outs, smem_out=()):
@@ -190,15 +193,15 @@
     qh, ql = split(query_rows(q_ref))
     qcat = cat([qh, qh, ql], 1)
     lab = local_labels(pos_ref, q_ref)
-    rows = lax.broadcasted_iota(jnp.int32, (HALF, 256), 0)
+    rows = lax.broadcasted_iota(jnp.int32, (HALF, W), 0)
     top = total = None
-    pick = jnp.zeros((8, 256), f32)
+    pick = jnp.zeros((8, W), f32)
     for t in range(PIECES):
         at = slice(t * HALF, (t + 1) * HALF)
         s = dot(cat([xh[at], xl[at], xh[at]], 1), qcat, NT)
         (s0_ref, s1_ref)[t // 4][0, t % 4] = s
-        pick += jnp.sum(jnp.where(rows == lab - t * HALF, s, 0.0).reshape(32, 8, 256), axis=0)
-        s = s.reshape(32, 8, 256)
+        pick += jnp.sum(jnp.where(rows == lab - t * HALF, s, 0.0).reshape(32, 8, W), axis=0)
+        s = s.reshape(32, 8, W)
         best = jnp.max(s, axis=0)
         if top is None:
             total = jnp.sum(jnp.exp(s - best[None]), axis=0)
@@ -209,8 +212,8 @@
     best = jnp.max(top, axis=0, keepdims=True)
     total = jnp.sum(total * jnp.exp(top - best), axis=0, keepdims=True)
     pick = jnp.sum(pick, axis=0, keepdims=True)
-    for h in range(2):
-        z = 2 * pl.program_id(0) + h
+    for h in range(N):
+        z = N * pl.program_id(0) + h
         at = slice(h * ROWS, (h + 1) * ROWS)
         stat_ref[0, pl.ds(z, 1), :] = best[:, at]
         stat_ref[1, pl.ds(z, 1), :] = total[:, at]
@@ -220,20 +223,20 @@
 def forward(pos, xh, xl, q):
     return pl.pallas_call(
         forward_kernel,
-        grid=(4,),
+        grid=(STEPS,),
         in_specs=[
             SMEM,
             pl.BlockSpec((LOCAL, E), lambda i: (0, 0)),
             pl.BlockSpec((LOCAL, E), lambda i: (0, 0)),
-            pl.BlockSpec((2, PAD, E), lambda i: (i, 0, 0)),
+            pl.BlockSpec((N, PAD, E), lambda i: (i, 0, 0)),
         ],
         out_specs=[
-            pl.BlockSpec((1, 4, HALF, 256), lambda i: (i, 0, 0, 0)),
-            pl.BlockSpec((1, 4, HALF, 256), lambda i: (i, 0, 0, 0)),
+            pl.BlockSpec((1, 4, HALF, W), lambda i: (i, 0, 0, 0)),
+            pl.BlockSpec((1, 4, HALF, W), lambda i: (i, 0, 0, 0)),
             pl.BlockSpec((3, ZN, ROWS), lambda i: (0, 0, 0)),
         ],
-        out_shape=[shape(4, 4, HALF, 256)] * 2 + [shape(3, ZN, ROWS)],
-        compiler_params=params(12),
+        out_shape=[shape(STEPS, 4, HALF, W)] * 2 + [shape(3, ZN, ROWS)],
+        compiler_params=params(18),
         cost_estimate=pl.CostEstimate(flops=3 * 2**30, bytes_accessed=10 * 2**20, transcendentals=2**21),
         name="forward",
     )(pos, xh, xl, q)
@@ -241,7 +244,7 @@
 
 def block(i, pos_ref, lse_ref, q_ref):
     qh, ql = split(query_rows(q_ref))
-    lse = cat([lse_ref[pl.ds(2 * i, 1), :], lse_ref[pl.ds(2 * i + 1, 1), :]], 1)
+    lse = cat([lse_ref[pl.ds(N * i + k, 1), :] for k in range(N)], 1)
     return cat([qh, ql, qh], 0), local_labels(pos_ref, q_ref), lse
 
 
@@ -252,8 +255,8 @@
 
 def gradients(g_acc, x, s, operands, first, count, tiles):
     qcat, lab, lse = operands
-    rows = lax.broadcasted_iota(jnp.int32, (HALF, 256), 0)
-    o = jnp.zeros((256, E), f32)
+    rows = lax.broadcasted_iota(jnp.int32, (HALF, W), 0)
+    o = jnp.zeros((W, E), f32)
     for t in tiles:
         at = slice(t * HALF, (t + 1) * HALF)
         dh, dl = delta(s[t // 4][0, t % 4], lse, rows, lab, t * HALF)
@@ -272,18 +275,19 @@
         g_acc[...] = jnp.zeros_like(g_acc)
         token[0] = 0.0
 
-    @pl.when(i < 4)
+    @pl.when(i < STEPS)
     def _():
         operands = block(i, pos_ref, lse_m, mine)
         gradients(g_acc, None, (None, sm1), operands, 4, 4, range(4, 8))
 
-    @pl.when(i >= 4)
-    def _():
-        operands = block(i - 4, pos_ref, lse_o, other)
+    @pl.when(i >= STEPS)
+    def _():
+        operands = block(i - STEPS, pos_ref, lse_o, other)
         o = gradients(g_acc, (xh, xl), (so0, so1), operands, 4, 4, range(8))
-        oo[0], oo[1] = o[:ROWS], o[ROWS:]
-
-    @pl.when(i == ZN - 1)
+        for k in range(N):
+            oo[k] = o[k * ROWS : (k + 1) * ROWS]
+
+    @pl.when(i == 2 * STEPS - 1)
     def _():
         for d in range(4):
             up[d * CUT : (d + 1) * CUT, :] = g_acc[d, :CUT, :]
@@ -298,16 +302,17 @@
     def _():
         g_ref[...] = jnp.zeros_like(g_ref)
 
-    @pl.when(i < 4)
+    @pl.when(i < STEPS)
     def _():
         operands = block(i, pos_ref, lse_o, other)
         gradients(g_ref, None, (so0, None), operands, 0, 4, range(4))
 
-    @pl.when(i >= 4)
-    def _():
-        operands = block(i - 4, pos_ref, lse_m, mine)
+    @pl.when(i >= STEPS)
+    def _():
+        operands = block(i - STEPS, pos_ref, lse_m, mine)
         o = gradients(g_ref, (xh, xl), (sm0, sm1), operands, 0, 4, range(8))
-        om[0], om[1] = o[:ROWS] + got[0], o[ROWS:] + got[1]
+        for k in range(N):
+            om[k] = o[k * ROWS : (k + 1) * ROWS] + got[k]
 
 
 def whole(*dims):
@@ -315,29 +320,29 @@
 
 
 def early(*dims):
-    return pl.BlockSpec(dims, lambda i: (jnp.minimum(i, 3),) + (0,) * (len(dims) - 1))
+    return pl.BlockSpec(dims, lambda i: (jnp.minimum(i, STEPS - 1),) + (0,) * (len(dims) - 1))
 
 
 def late(*dims):
-    return pl.BlockSpec(dims, lambda i: (jnp.maximum(i, 4) - 4,) + (0,) * (len(dims) - 1))
+    return pl.BlockSpec(dims, lambda i: (jnp.maximum(i, STEPS) - STEPS,) + (0,) * (len(dims) - 1))
 
 
 X_SPEC = whole(LOCAL, E)
 LSE = whole(2 * ZN, ROWS)
-Q = (2, PAD, E)
-S = (1, 4, HALF, 256)
+Q = (N, PAD, E)
+S = (1, 4, HALF, W)
 
 
 def backward_a(pos, *operands):
     return pl.pallas_call(
         backward_a_kernel,
-        grid=(ZN,),
+        grid=(2 * STEPS,),
         in_specs=[SMEM, X_SPEC, X_SPEC, early(*Q), late(*Q), LSE, LSE]
         + [early(*S), late(*S), late(*S)],
-        out_specs=[late(2, ROWS, E)] + [whole(4 * CUT + 8, E)] * 2 + [SMEM],
+        out_specs=[late(N, ROWS, E)] + [whole(4 * CUT + 8, E)] * 2 + [SMEM],
         out_shape=[shape(ZN, ROWS, E)] + [shape(4 * CUT + 8, E)] * 2 + [shape(1)],
         scratch_shapes=[pltpu.VMEM((4, HALF, E), f32)],
-        compiler_params=params(14),
+        compiler_params=params(24),
         cost_estimate=pl.CostEstimate(flops=6 * 2**30, bytes_accessed=16 * 2**20, transcendentals=3 * 2**20),
         name="backward_a",
     )(pos, *operands)
@@ -346,12 +351,12 @@
 def backward_b(pos, *operands):
     return pl.pallas_call(
         backward_b_kernel,
-        grid=(ZN,),
+        grid=(2 * STEPS,),
         in_specs=[SMEM, SMEM, X_SPEC, X_SPEC, late(*Q), early(*Q), LSE, LSE]
-        + [late(*S), late(*S), early(*S), late(2, ROWS, E)],
-        out_specs=[late(2, ROWS, E), whole(4, HALF, E)],
+        + [late(*S), late(*S), early(*S), late(N, ROWS, E)],
+        out_specs=[late(N, ROWS, E), whole(4, HALF, E)],
         out_shape=[shape(ZN, ROWS, E), shape(4, HALF, E)],
-        compiler_params=params(14),
+        compiler_params=params(24),
         cost_estimate=pl.CostEstimate(flops=6 * 2**30, bytes_accessed=16 * 2**20, transcendentals=3 * 2**20),
         name="backward_b",
     )(pos, *operands)

time: 129 us -> 126 us (0.977)
  Pallas kernels: 39.9 us -> 36.8 us
    pallas_call x4, Pallas kernels: 32.8 us -> 29.7 us  [the longest x1 10.4 us: backward_b(): pl.pallas_call(backward_b_kernel, grid=(2 * STEPS,), in_specs=[SMEM, SMEM...]
  transfers between devices with their start and end apart: 23 -> 23, of which waited for: 12 -> 12; matrix products, arithmetic and copies ran while one was open for 0% -> 0% of each run, Pallas kernels for 17% -> 16%
where the time goes in v5:
time: 126 us
  waiting for transfers between devices  44.7 us (35%)
  Pallas kernels  36.8 us (29%)
  starting transfers between devices  29 us (23%)
  blocking collectives  12.3 us (10%)
  local copies, waits for them, and re-layouts  2.6 us (2%)
    ppermute x15, waiting for transfers between devices, send(): return lax.ppermute(a, AXES, pairs(**shift))  26.8 us
    ppermute x7, waiting for transfers between devices, twin(): lax.ppermute(a, AXES, [(down if i >> 6 & 1 else up)[i] for i in range(256)])  16.2 us
    ppermute x7, starting transfers between devices, twin(): lax.ppermute(a, AXES, [(down if i >> 6 & 1 else up)[i] for i in range(256)])  13.8 us
    all_to_all x1, blocking collectives, body(): stats = lax.all_to_all(stats, 'z', 0, 0, tiled=True)  12.3 us
    ppermute x15, starting transfers between devices, send(): return lax.ppermute(a, AXES, pairs(**shift))  11.6 us
    pallas_call x1, Pallas kernels, backward_b(): pl.pallas_call(backward_b_kernel, grid=(2 * STEPS,), in_specs=[SMEM, SMEM...  10.4 us
    pallas_call x2, Pallas kernels, forward(): pl.pallas_call(forward_kernel, grid=(STEPS,), in_specs=[SMEM, pl.BlockSpe...  9.65 us
    pallas_call x1, Pallas kernels, backward_a(): pl.pallas_call(backward_a_kernel, grid=(2 * STEPS,), in_specs=[SMEM, X_SP...  9.58 us
  transfers between devices with their start and end apart: 23, of which 12 were waited for; matrix products, arithmetic and copies ran while one was open for 0% of the time, Pallas kernels for 16%

profile of v5, /device:TPU:24, one launch (start us, length us, event | category | flops | bytes accessed | tf_op | source)
XLA Modules:
  0.0 126.2 jit_solution(4047593588627547487)
XLA Ops:
  4.0 1.6 %collective-permute-start = (f32[512,256]{1,0:T(8,128)S(1)}, f32[512,256]{1,0:T(8,128)S(1)}, u32[]{:S(2)}, u32[]{:S(2)}) collective-permute-start(f32[512,256]{1,0:T(8,128)S(1)} %copy-done), channel_id=1, source_target_pairs={{0,8},{1,9},{2,10},{3,11},{4,12},{5,13},{6,14},{7,15},{8,16},{9,17... | collective-permute-start | bytes 1572872 | tf_op jit(solution)/shard_map/ppermute | solution.py:46
  6.1 3.3 %collective-permute-start.2 = (f32[272,256]{1,0:T(8,128)S(1)}, f32[272,256]{1,0:T(8,128)S(1)}, u32[]{:S(2)}, u32[]{:S(2)}) collective-permute-start(f32[272,256]{1,0:T(8,128)S(1)} %pair_kernel.1.refs_1_), channel_id=1, source_target_pairs={{0,2},{1,3},{2,4},{3,5},{4,6},{5,7},{6,0},{7,1},{8,10},{9,11},{10,... | collective-permute-start | bytes 835592 | tf_op jit(solution)/shard_map/ppermute | solution.py:46
  9.5 2.8 %collective-permute-start.4 = (f32[256,256]{1,0:T(8,128)S(1)}, f32[256,256]{1,0:T(8,128)S(1)}, u32[]{:S(2)}, u32[]{:S(2)}) collective-permute-start(f32[256,256]{1,0:T(8,128)S(1)} %get-tuple-element.31.own), channel_id=1, source_target_pairs={{0,16},{1,17},{2,18},{3,19},{4,20},{5,21},{6,22},{7,23},{8,24},{9,... | collective-permute-start | bytes 786440 | tf_op jit(solution)/shard_map/ppermute | solution.py:46
  12.5 5.1 %collective-permute-done.2.both.refs_0_.r2 = f32[272,256]{1,0:T(8,128)S(1)} collective-permute-done((f32[272,256]{1,0:T(8,128)S(1)}, f32[272,256]{1,0:T(8,128)S(1)}, u32[]{:S(2)}, u32[]{:S(2)}) %collective-permute-start.2) | collective-permute-done | bytes 278560 | tf_op jit(solution)/shard_map/ppermute | solution.py:46
  17.7 3.5 %collective-permute-start.7 = (f32[544,256]{1,0:T(8,128)S(1)}, f32[544,256]{1,0:T(8,128)S(1)}, u32[]{:S(2)}, u32[]{:S(2)}) collective-permute-start(f32[544,256]{1,0:T(8,128)S(1)} %stack_kernel.4), channel_id=1, source_target_pairs={{0,1},{1,2},{2,3},{3,4},{4,5},{5,6},{6,7},{7,0},{8,9},{9,10},{10,1... | collective-permute-start | bytes 1671176 | tf_op jit(solution)/shard_map/ppermute | solution.py:46
  24.3 2.1 %collective-permute-start.8 = (f32[136,256]{1,0:T(8,128)S(1)}, f32[136,256]{1,0:T(8,128)S(1)}, u32[]{:S(2)}, u32[]{:S(2)}) collective-permute-start(f32[136,256]{1,0:T(8,128)S(1)} %get-tuple-element.33.refs_0_), channel_id=1, source_target_pairs={{0,2},{1,3},{2,4},{3,5},{4,6},{5,7},{6,0},{7,1},{8,10},{9,11},{10,... | collective-permute-start | bytes 417800 | tf_op jit(solution)/shard_map/ppermute | solution.py:46
  26.7 6.2 %collective-permute-done.8.refs_1_ = f32[136,256]{1,0:T(8,128)S(1)} collective-permute-done((f32[136,256]{1,0:T(8,128)S(1)}, f32[136,256]{1,0:T(8,128)S(1)}, u32[]{:S(2)}, u32[]{:S(2)}) %collective-permute-start.8) | collective-permute-done | bytes 139296 | tf_op jit(solution)/shard_map/ppermute | solution.py:46
  33.5 4.9 %collective-permute-done.6.y_rest = f32[768,256]{1,0:T(8,128)S(1)} collective-permute-done((f32[768,256]{1,0:T(8,128)S(1)}, f32[768,256]{1,0:T(8,128)S(1)}, u32[]{:S(2)}, u32[]{:S(2)}) %collective-permute-start.6) | collective-permute-done | bytes 786464 | tf_op jit(solution)/shard_map/ppermute | solution.py:46
  40.1 4.9 %forward.3 = (f32[2,4,256,512]{3,2,1,0:T(8,128)S(1)}, f32[2,4,256,512]{3,2,1,0:T(8,128)S(1)}, f32[3,8,128]{2,1,0:T(8,128)S(1)}) custom-call(s32[4]{0:T(128)S(1)} %pad_add_fusion.pos_ref, bf16[2048,256]{1,0:T(8,128)(2,1)S(1)} %get-tuple-element.36.xh, bf16[2048,256]{1,0:T(8,128)(2,1)S(1)} %get-tuple-element.37.xl, ...), custom_call_target="tpu_custom_call" | custom-call | flops 3221225472 | bytes 10485760 | tf_op jit(solution)/shard_map/forward/pallas_call | solution.py:224
  44.9 3.5 %collective-permute-start.11 = (f32[3,8,128]{2,1,0:T(8,128)S(1)}, f32[3,8,128]{2,1,0:T(8,128)S(1)}, u32[]{:S(2)}, u32[]{:S(2)}) collective-permute-start(f32[3,8,128]{2,1,0:T(8,128)S(1)} %get-tuple-element.41), channel_id=1, source_target_pairs={{0,64},{1,65},{2,66},{3,67},{4,68},{5,69},{6,70},{7,71},{8,72},{9,... | collective-permute-start | bytes 36872 | tf_op jit(solution)/shard_map/ppermute | solution.py:41
  48.5 4.8 %forward.2 = (f32[2,4,256,512]{3,2,1,0:T(8,128)S(1)}, f32[2,4,256,512]{3,2,1,0:T(8,128)S(1)}, f32[3,8,128]{2,1,0:T(8,128)S(1)}) custom-call(s32[4]{0:T(128)S(1)} %pad_add_fusion.pos_ref, bf16[2048,256]{1,0:T(8,128)(2,1)S(1)} %get-tuple-element.36.xh, bf16[2048,256]{1,0:T(8,128)(2,1)S(1)} %get-tuple-element.37.xl, f32[8,136,256]{2,1,0:T(8,128)S(1)} %get-tuple-element.38.q_ref.mine), custom_call_target="tpu_custom_call" | custom-call | flops 3221225472 | bytes 10485760 | tf_op jit(solution)/shard_map/forward/pallas_call | solution.py:224
  53.3 12.3 %all_to_all.10.got = f32[8,3,8,128]{3,2,1,0:T(8,128)S(1)} all-to-all(f32[8,3,8,128]{3,2,1,0:T(8,128)S(1)} %spread_kernel.1), channel_id=1, replica_groups=mesh['yh'=2,'c'=2,'yl'=2,'x'=4,'z'=8] {'z'}, dimensions={0} | all-to-all | bytes 196608 | tf_op jit(solution)/shard_map/all_to_all | solution.py:448
  67.0 9.6 %backward_a.1 = (f32[8,128,256]{2,1,0:T(8,128)S(1)}, f32[520,256]{1,0:T(8,128)S(1)}, f32[520,256]{1,0:T(8,128)S(1)}, f32[1]{0:T(128)}) custom-call(s32[4]{0:T(128)S(1)} %pad_add_fusion.pos_ref, bf16[2048,256]{1,0:T(8,128)(2,1)S(1)} %get-tuple-element.36.xh, bf16[2048,256]{1,0:T(8,128)(2,1)S(1)} %get-tuple-element.37.xl, ...), custom_call_target="tpu_custom_call" | custom-call | flops 6442450944 | bytes 16777216 | tf_op jit(solution)/shard_map/backward_a/pallas_call | solution.py:337
  76.8 1.4 %collective-permute-start.14 = (f32[520,256]{1,0:T(8,128)S(1)}, f32[520,256]{1,0:T(8,128)S(1)}, u32[]{:S(2)}, u32[]{:S(2)}) collective-permute-start(f32[520,256]{1,0:T(8,128)S(1)} %get-tuple-element.49), channel_id=1, source_target_pairs={{0,32},{1,33},{2,34},{3,35},{4,36},{5,37},{6,38},{7,39},{8,40},{9,... | collective-permute-start | bytes 1597448 | tf_op jit(solution)/shard_map/ppermute | solution.py:41
  79.3 10.4 %backward_b.1 = (f32[8,128,256]{2,1,0:T(8,128)}, f32[4,256,256]{2,1,0:T(8,128)S(1)}) custom-call(s32[4]{0:T(128)S(1)} %pad_add_fusion.pos_ref, f32[1]{0:T(128)} %get-tuple-element.45.token, bf16[2048,256]{1,0:T(8,128)(2,1)S(1)} %get-tuple-element.36.xh, bf16[2048,256]{1,0:T(8,128)(2,1)S(1)} %get-tuple-element.37.xl, ...), custom_call_target="tpu_custom_call" | custom-call | flops 6442450944 | bytes 16777216 | tf_op jit(solution)/shard_map/backward_b/pallas_call | solution.py:352
  89.7 1.4 %collective-permute-done.14.a = f32[520,256]{1,0:T(8,128)S(1)} collective-permute-done((f32[520,256]{1,0:T(8,128)S(1)}, f32[520,256]{1,0:T(8,128)S(1)}, u32[]{:S(2)}, u32[]{:S(2)}) %collective-permute-start.14) | collective-permute-done | bytes 532512 | tf_op jit(solution)/shard_map/ppermute | solution.py:41
  91.1 2.4 %collective-permute-done.15.b = f32[520,256]{1,0:T(8,128)S(1)} collective-permute-done((f32[520,256]{1,0:T(8,128)S(1)}, f32[520,256]{1,0:T(8,128)S(1)}, u32[]{:S(2)}, u32[]{:S(2)}) %collective-permute-start.15) | collective-permute-done | bytes 532512 | tf_op jit(solution)/shard_map/ppermute | solution.py:41
  93.6 3.6 %all-to-all-start.1 = ((f32[8,128,256]{2,1,0:T(8,128)}), f32[8,128,256]{2,1,0:T(8,128)S(1)}, u32[]{:S(2)}, u32[]{:S(2)}) async-start(f32[8,128,256]{2,1,0:T(8,128)} %get-tuple-element.57), calls=%async_computation.1 | async-start | bytes 2097152 | tf_op jit(solution)/shard_map/all_to_all | solution.py:455
  97.3 1.4 %collective-permute-start.17 = (f32[264,256]{1,0:T(8,128)S(1)}, f32[264,256]{1,0:T(8,128)S(1)}, u32[]{:S(2)}, u32[]{:S(2)}) collective-permute-start(f32[264,256]{1,0:T(8,128)S(1)} %get-tuple-element.54), channel_id=1, source_target_pairs={{0,16},{1,17},{2,18},{3,19},{4,20},{5,21},{6,22},{7,23},{8,24},{9,... | collective-permute-start | bytes 811016 | tf_op jit(solution)/shard_map/ppermute | solution.py:41
  98.7 2.0 %collective-permute-start.18 = (f32[264,256]{1,0:T(8,128)S(1)}, f32[264,256]{1,0:T(8,128)S(1)}, u32[]{:S(2)}, u32[]{:S(2)}) collective-permute-start(f32[264,256]{1,0:T(8,128)S(1)} %get-tuple-element.55), channel_id=1, source_target_pairs={{0,24},{1,25},{2,26},{3,27},{4,28},{5,29},{6,30},{7,31},{8,0},{9,1... | collective-permute-start | bytes 811016 | tf_op jit(solution)/shard_map/ppermute | solution.py:41
  100.8 11.1 %collective-permute-done.16.m1 = f32[264,256]{1,0:T(8,128)S(1)} collective-permute-done((f32[264,256]{1,0:T(8,128)S(1)}, f32[264,256]{1,0:T(8,128)S(1)}, u32[]{:S(2)}, u32[]{:S(2)}) %collective-permute-start.16) | collective-permute-done | bytes 270368 | tf_op jit(solution)/shard_map/ppermute | solution.py:41
  112.9 8.0 %collective-permute-done.19.mine2 = f32[264,256]{1,0:T(8,128)S(1)} collective-permute-done((f32[264,256]{1,0:T(8,128)S(1)}, f32[264,256]{1,0:T(8,128)S(1)}, u32[]{:S(2)}, u32[]{:S(2)}) %collective-permute-start.19) | collective-permute-done | bytes 270368 | tf_op jit(solution)/shard_map/ppermute | solution.py:41
  120.9 1.5 %collective-permute-done.21.other2 = f32[264,256]{1,0:T(8,128)S(1)} collective-permute-done((f32[264,256]{1,0:T(8,128)S(1)}, f32[264,256]{1,0:T(8,128)S(1)}, u32[]{:S(2)}, u32[]{:S(2)}) %collective-permute-start.21) | collective-permute-done | bytes 270368 | tf_op jit(solution)/shard_map/ppermute | solution.py:41
  123.8 1.7 %all-to-all-done.1.got = f32[8,128,256]{2,1,0:T(8,128)S(1)} async-done(((f32[8,128,256]{2,1,0:T(8,128)}), f32[8,128,256]{2,1,0:T(8,128)S(1)}, u32[]{:S(2)}, u32[]{:S(2)}) %all-to-all-start.1) | async-done | bytes 1048608 | tf_op jit(solution)/shard_map/all_to_all | solution.py:455
  (49 shorter events, 15.8 us)
Async XLA Ops:
  0.7 1.0 copy-start
  3.9 1.7 %collective-permute-start.1 = (f32[136,256]{1,0:T(8,128)S(1)}, f32[136,256]{1,0:T(8,128)S(1)}, u32[]{:S(2)}, u32[]{:S(2)}) collective-permute-start(f32[136,256]{1,0:T(8,128)S(1)} %get-tuple-element.32.mine.q), channel_id=1, source_target_pairs={{0,64},{1,65},{2,66},{3,67},{4,68},{5,69},{6,70},{7,71},{8,72},{9,... | collective-permute-start | bytes 417800 | tf_op jit(solution)/shard_map/ppermute | solution.py:41
  4.0 18.4 %collective-permute-start = (f32[512,256]{1,0:T(8,128)S(1)}, f32[512,256]{1,0:T(8,128)S(1)}, u32[]{:S(2)}, u32[]{:S(2)}) collective-permute-start(f32[512,256]{1,0:T(8,128)S(1)} %copy-done), channel_id=1, source_target_pairs={{0,8},{1,9},{2,10},{3,11},{4,12},{5,13},{6,14},{7,15},{8,16},{9,17... | collective-permute-start | bytes 1572872 | tf_op jit(solution)/shard_map/ppermute | solution.py:46
  6.1 11.5 %collective-permute-start.2 = (f32[272,256]{1,0:T(8,128)S(1)}, f32[272,256]{1,0:T(8,128)S(1)}, u32[]{:S(2)}, u32[]{:S(2)}) collective-permute-start(f32[272,256]{1,0:T(8,128)S(1)} %pair_kernel.1.refs_1_), channel_id=1, source_target_pairs={{0,2},{1,3},{2,4},{3,5},{4,6},{5,7},{6,0},{7,1},{8,10},{9,11},{10,... | collective-permute-start | bytes 835592 | tf_op jit(solution)/shard_map/ppermute | solution.py:46
  9.5 11.7 %collective-permute-start.4 = (f32[256,256]{1,0:T(8,128)S(1)}, f32[256,256]{1,0:T(8,128)S(1)}, u32[]{:S(2)}, u32[]{:S(2)}) collective-permute-start(f32[256,256]{1,0:T(8,128)S(1)} %get-tuple-element.31.own), channel_id=1, source_target_pairs={{0,16},{1,17},{2,18},{3,19},{4,20},{5,21},{6,22},{7,23},{8,24},{9,... | collective-permute-start | bytes 786440 | tf_op jit(solution)/shard_map/ppermute | solution.py:46
  12.3 8.9 %collective-permute-start.3 = (f32[256,256]{1,0:T(8,128)S(1)}, f32[256,256]{1,0:T(8,128)S(1)}, u32[]{:S(2)}, u32[]{:S(2)}) collective-permute-start(f32[256,256]{1,0:T(8,128)S(1)} %get-tuple-element.31.own), channel_id=1, source_target_pairs={{0,32},{1,33},{2,34},{3,35},{4,36},{5,37},{6,38},{7,39},{8,40},{9,... | collective-permute-start | bytes 786440 | tf_op jit(solution)/shard_map/ppermute | solution.py:46
  17.7 15.2 %collective-permute-start.7 = (f32[544,256]{1,0:T(8,128)S(1)}, f32[544,256]{1,0:T(8,128)S(1)}, u32[]{:S(2)}, u32[]{:S(2)}) collective-permute-start(f32[544,256]{1,0:T(8,128)S(1)} %stack_kernel.4), channel_id=1, source_target_pairs={{0,1},{1,2},{2,3},{3,4},{4,5},{5,6},{6,7},{7,0},{8,9},{9,10},{10,1... | collective-permute-start | bytes 1671176 | tf_op jit(solution)/shard_map/ppermute | solution.py:46
  23.0 3.4 %collective-permute-start.5 = (f32[256,256]{1,0:T(8,128)S(1)}, f32[256,256]{1,0:T(8,128)S(1)}, u32[]{:S(2)}, u32[]{:S(2)}) collective-permute-start(f32[256,256]{1,0:T(8,128)S(1)} %get-tuple-element.35), channel_id=1, source_target_pairs={{0,64},{1,65},{2,66},{3,67},{4,68},{5,69},{6,70},{7,71},{8,72},{9,... | collective-permute-start | bytes 786440 | tf_op jit(solution)/shard_map/ppermute | solution.py:41
  24.3 8.6 %collective-permute-start.8 = (f32[136,256]{1,0:T(8,128)S(1)}, f32[136,256]{1,0:T(8,128)S(1)}, u32[]{:S(2)}, u32[]{:S(2)}) collective-permute-start(f32[136,256]{1,0:T(8,128)S(1)} %get-tuple-element.33.refs_0_), channel_id=1, source_target_pairs={{0,2},{1,3},{2,4},{3,5},{4,6},{5,7},{6,0},{7,1},{8,10},{9,11},{10,... | collective-permute-start | bytes 417800 | tf_op jit(solution)/shard_map/ppermute | solution.py:46
  26.4 12.1 %collective-permute-start.6 = (f32[768,256]{1,0:T(8,128)S(1)}, f32[768,256]{1,0:T(8,128)S(1)}, u32[]{:S(2)}, u32[]{:S(2)}) collective-permute-start(f32[768,256]{1,0:T(8,128)S(1)} %stack_kernel.3), channel_id=1, source_target_pairs={{0,32},{1,33},{2,34},{3,35},{4,36},{5,37},{6,38},{7,39},{8,40},{9,... | collective-permute-start | bytes 2359304 | tf_op jit(solution)/shard_map/ppermute | solution.py:46
  32.9 6.4 %collective-permute-start.10 = (f32[680,256]{1,0:T(8,128)S(1)}, f32[680,256]{1,0:T(8,128)S(1)}, u32[]{:S(2)}, u32[]{:S(2)}) collective-permute-start(f32[680,256]{1,0:T(8,128)S(1)} %stack_kernel.5.r314), channel_id=1, source_target_pairs={{0,64},{1,65},{2,66},{3,67},{4,68},{5,69},{6,70},{7,71},{8,72},{9,... | collective-permute-start | bytes 2088968 | tf_op jit(solution)/shard_map/ppermute | solution.py:41
  33.1 6.2 %collective-permute-start.9 = (f32[272,256]{1,0:T(8,128)S(1)}, f32[272,256]{1,0:T(8,128)S(1)}, u32[]{:S(2)}, u32[]{:S(2)}) collective-permute-start(f32[272,256]{1,0:T(8,128)S(1)} %collective-permute-done.2.both.refs_0_.r2), channel_id=1, source_target_pairs={{0,64},{1,65},{2,66},{3,67},{4,68},{5,69},{6,70},{7,71},{8,72},{9,... | collective-permute-start | bytes 835592 | tf_op jit(solution)/shard_map/ppermute | solution.py:41
  44.9 8.3 %collective-permute-start.11 = (f32[3,8,128]{2,1,0:T(8,128)S(1)}, f32[3,8,128]{2,1,0:T(8,128)S(1)}, u32[]{:S(2)}, u32[]{:S(2)}) collective-permute-start(f32[3,8,128]{2,1,0:T(8,128)S(1)} %get-tuple-element.41), channel_id=1, source_target_pairs={{0,64},{1,65},{2,66},{3,67},{4,68},{5,69},{6,70},{7,71},{8,72},{9,... | collective-permute-start | bytes 36872 | tf_op jit(solution)/shard_map/ppermute | solution.py:41
  65.7 1.3 collective-permute-start.12
  76.5 2.7 %collective-permute-start.13 = (f32[8,128,256]{2,1,0:T(8,128)S(1)}, f32[8,128,256]{2,1,0:T(8,128)S(1)}, u32[]{:S(2)}, u32[]{:S(2)}) collective-permute-start(f32[8,128,256]{2,1,0:T(8,128)S(1)} %get-tuple-element.47), channel_id=1, source_target_pairs={{0,64},{1,65},{2,66},{3,67},{4,68},{5,69},{6,70},{7,71},{8,72},{9,... | collective-permute-start | bytes 3145736 | tf_op jit(solution)/shard_map/ppermute | solution.py:41
  76.8 14.3 %collective-permute-start.14 = (f32[520,256]{1,0:T(8,128)S(1)}, f32[520,256]{1,0:T(8,128)S(1)}, u32[]{:S(2)}, u32[]{:S(2)}) collective-permute-start(f32[520,256]{1,0:T(8,128)S(1)} %get-tuple-element.49), channel_id=1, source_target_pairs={{0,32},{1,33},{2,34},{3,35},{4,36},{5,37},{6,38},{7,39},{8,40},{9,... | collective-permute-start | bytes 1597448 | tf_op jit(solution)/shard_map/ppermute | solution.py:41
  78.2 15.3 %collective-permute-start.15 = (f32[520,256]{1,0:T(8,128)S(1)}, f32[520,256]{1,0:T(8,128)S(1)}, u32[]{:S(2)}, u32[]{:S(2)}) collective-permute-start(f32[520,256]{1,0:T(8,128)S(1)} %get-tuple-element.50), channel_id=1, source_target_pairs={{0,160},{1,161},{2,162},{3,163},{4,164},{5,165},{6,166},{7,167},{8... | collective-permute-start | bytes 1597448 | tf_op jit(solution)/shard_map/ppermute | solution.py:41
  93.6 31.9 %all-to-all-start.1 = ((f32[8,128,256]{2,1,0:T(8,128)}), f32[8,128,256]{2,1,0:T(8,128)S(1)}, u32[]{:S(2)}, u32[]{:S(2)}) async-start(f32[8,128,256]{2,1,0:T(8,128)} %get-tuple-element.57), calls=%async_computation.1 | async-start | bytes 2097152 | tf_op jit(solution)/shard_map/all_to_all | solution.py:455
  97.2 14.7 %collective-permute-start.16 = (f32[264,256]{1,0:T(8,128)S(1)}, f32[264,256]{1,0:T(8,128)S(1)}, u32[]{:S(2)}, u32[]{:S(2)}) collective-permute-start(f32[264,256]{1,0:T(8,128)S(1)} %get-tuple-element.53), channel_id=1, source_target_pairs={{0,8},{1,9},{2,10},{3,11},{4,12},{5,13},{6,14},{7,15},{8,16},{9,17... | collective-permute-start | bytes 811016 | tf_op jit(solution)/shard_map/ppermute | solution.py:41
  97.3 14.6 %collective-permute-start.17 = (f32[264,256]{1,0:T(8,128)S(1)}, f32[264,256]{1,0:T(8,128)S(1)}, u32[]{:S(2)}, u32[]{:S(2)}) collective-permute-start(f32[264,256]{1,0:T(8,128)S(1)} %get-tuple-element.54), channel_id=1, source_target_pairs={{0,16},{1,17},{2,18},{3,19},{4,20},{5,21},{6,22},{7,23},{8,24},{9,... | collective-permute-start | bytes 811016 | tf_op jit(solution)/shard_map/ppermute | solution.py:41
  98.7 13.8 %collective-permute-start.18 = (f32[264,256]{1,0:T(8,128)S(1)}, f32[264,256]{1,0:T(8,128)S(1)}, u32[]{:S(2)}, u32[]{:S(2)}) collective-permute-start(f32[264,256]{1,0:T(8,128)S(1)} %get-tuple-element.55), channel_id=1, source_target_pairs={{0,24},{1,25},{2,26},{3,27},{4,28},{5,29},{6,30},{7,31},{8,0},{9,1... | collective-permute-start | bytes 811016 | tf_op jit(solution)/shard_map/ppermute | solution.py:41
  112.6 8.3 %collective-permute-start.19 = (f32[264,256]{1,0:T(8,128)S(1)}, f32[264,256]{1,0:T(8,128)S(1)}, u32[]{:S(2)}, u32[]{:S(2)}) collective-permute-start(f32[264,256]{1,0:T(8,128)S(1)} %land_kernel.1.mine), channel_id=1, source_target_pairs={{0,128},{1,129},{2,130},{3,131},{4,132},{5,133},{6,134},{7,135},{8... | collective-permute-start | bytes 811016 | tf_op jit(solution)/shard_map/ppermute | solution.py:41
  112.9 8.0 %collective-permute-start.20 = (f32[264,256]{1,0:T(8,128)S(1)}, f32[264,256]{1,0:T(8,128)S(1)}, u32[]{:S(2)}, u32[]{:S(2)}) collective-permute-start(f32[264,256]{1,0:T(8,128)S(1)} %land_kernel.1.mine), channel_id=1, source_target_pairs={{0,64},{1,65},{2,66},{3,67},{4,68},{5,69},{6,70},{7,71},{8,72},{9,... | collective-permute-start | bytes 811016 | tf_op jit(solution)/shard_map/ppermute | solution.py:41
  120.9 1.5 %collective-permute-start.21 = (f32[264,256]{1,0:T(8,128)S(1)}, f32[264,256]{1,0:T(8,128)S(1)}, u32[]{:S(2)}, u32[]{:S(2)}) collective-permute-start(f32[264,256]{1,0:T(8,128)S(1)} %collective-permute-done.19.mine2), channel_id=1, source_target_pairs={{0,64},{1,65},{2,66},{3,67},{4,68},{5,69},{6,70},{7,71},{8,72},{9,... | collective-permute-start | bytes 811016 | tf_op jit(solution)/shard_map/ppermute | solution.py:41
  (2 other events, 1.6 us)

commit v6 on v5

--- a/solution.py
+++ b/solution.py
@@ -102,10 +102,13 @@
     return pl.ds(pl.multiple_of(start, 8), n)
 
 
-def start_kernel(pos_ref, queries, labels, items, q, own):
+def start_kernel(queries, labels, q):
     q[:ROWS, :] = queries[...]
     q[ROWS:, :ROWS] = jnp.broadcast_to(labels[...].astype(f32), (PAD - ROWS, ROWS))
     q[ROWS:, ROWS:] = jnp.zeros((PAD - ROWS, E - ROWS), f32)
+
+
+def own_kernel(pos_ref, items, own):
     own[...] = items[at(pos_ref[1] * HALF, HALF), :]
 
 
@@ -120,6 +123,22 @@
     n, c = mine.shape[0], pos_ref[1]
     mine[...] = both[at(c * n, n), :]
     other[...] = both[at((1 - c) * n, n), :]
+
+
+def third_kernel(pos_ref, both, after, after2, mine):
+    mine[...] = both[at(pos_ref[1] * PAD, PAD), :]
+
+
+def cut_third(*operands):
+    anywhere = pl.BlockSpec(memory_space=pl.ANY)
+    return pl.pallas_call(
+        third_kernel,
+        in_specs=[SMEM, VMEM, anywhere, anywhere],
+        out_specs=VMEM,
+        out_shape=shape(PAD, E),
+        compiler_params=params(10),
+        name="third",
+    )(*operands)
 
 
 def stack_kernel(*refs):
@@ -363,7 +382,7 @@
 
 
 def gather(pos, q, own, items):
-    chunk, two = shape(PAD, E), shape(2 * PAD, E)
+    two = shape(2 * PAD, E)
     half = shape(HALF, E)
     x1 = twin(items, "dx")
     qo = send(q, dc=1)
@@ -371,7 +390,7 @@
     r2 = twin(r0, "dz", 2)
     far = twin(own, "dx", 2)
     y0 = twin(own, "dy")
-    third, _ = small(part_kernel, [pos, r2, y0, far], [chunk, chunk])
+    third = cut_third(pos, r2, y0, far)
     (r20,) = small(stack_kernel, [r2, r0], [shape(4 * PAD, E)])
     r31, q4 = twin(r20, "dz"), twin(third, "dz", 2)
     near, rest = small(part_kernel, [pos, x1, third], [half, half])
@@ -438,9 +457,8 @@
 def body(queries, items, labels):
     core, y_lo, x_at, z_at = (lax.axis_index(a) for a in ("c", "yl", "x", "z"))
     pos = jnp.stack([z_at, core, y_lo, x_at]).astype(jnp.int32)
-    q, own = small(
-        start_kernel, [pos, queries, labels.reshape(1, ROWS), items], [shape(PAD, E), shape(HALF, E)]
-    )
+    (q,) = small(start_kernel, [queries, labels.reshape(1, ROWS)], [shape(PAD, E)])
+    (own,) = small(own_kernel, [pos, items], [shape(HALF, E)])
     mine, other, xh, xl = gather(pos, q, own, items)
     sm0, sm1, stat_m = forward(pos, xh, xl, mine)
     so0, so1, stat_o = forward(pos, xh, xl, other)

time: 126 us -> 124 us (0.984)
  waiting for transfers between devices: 44.7 us -> 41.9 us
  starting transfers between devices: 29 us -> 30.3 us
    ppermute x7, waiting for transfers between devices: 16.2 us -> 13.4 us  [twin(): lax.ppermute(a, AXES, [(down if i >> 6 & 1 else up)[i] for i in range(256)])]
where the time goes in v6:
time: 124 us
  waiting for transfers between devices  41.9 us (34%)
  Pallas kernels  36.1 us (29%)
  starting transfers between devices  30.3 us (24%)
  blocking collectives  12.3 us (10%)
  local copies, waits for them, and re-layouts  2.59 us (2%)
    ppermute x15, waiting for transfers between devices, send(): return lax.ppermute(a, AXES, pairs(**shift))  26.8 us
    ppermute x7, starting transfers between devices, twin(): lax.ppermute(a, AXES, [(down if i >> 6 & 1 else up)[i] for i in range(256)])  14.9 us
    ppermute x7, waiting for transfers between devices, twin(): lax.ppermute(a, AXES, [(down if i >> 6 & 1 else up)[i] for i in range(256)])  13.4 us
    all_to_all x1, blocking collectives, body(): stats = lax.all_to_all(stats, 'z', 0, 0, tiled=True)  12.3 us
    ppermute x15, starting transfers between devices, send(): return lax.ppermute(a, AXES, pairs(**shift))  11.9 us
    pallas_call x1, Pallas kernels, backward_b(): pl.pallas_call(backward_b_kernel, grid=(2 * STEPS,), in_specs=[SMEM, SMEM...  10.4 us
    pallas_call x2, Pallas kernels, forward(): pl.pallas_call(forward_kernel, grid=(STEPS,), in_specs=[SMEM, pl.BlockSpe...  9.65 us
    pallas_call x1, Pallas kernels, backward_a(): pl.pallas_call(backward_a_kernel, grid=(2 * STEPS,), in_specs=[SMEM, X_SP...  9.58 us
  transfers between devices with their start and end apart: 23, of which 12 were waited for; matrix products, arithmetic and copies ran while one was open for 0% of the time, Pallas kernels for 16%

profile of v6, /device:TPU:24, one launch (start us, length us, event | category | flops | bytes accessed | tf_op | source)
XLA Modules:
  0.0 124.1 jit_solution(10953490842760042476)
XLA Ops:
  2.3 1.6 %collective-permute-start = (f32[512,256]{1,0:T(8,128)}, f32[512,256]{1,0:T(8,128)S(1)}, u32[]{:S(2)}, u32[]{:S(2)}) collective-permute-start(f32[512,256]{1,0:T(8,128)} %items.1), channel_id=1, source_target_pairs={{0,8},{1,9},{2,10},{3,11},{4,12},{5,13},{6,14},{7,15},{8,16},{9,17... | collective-permute-start | bytes 1572872 | tf_op jit(solution)/shard_map/ppermute | solution.py:46
  4.5 3.3 %collective-permute-start.2 = (f32[272,256]{1,0:T(8,128)S(1)}, f32[272,256]{1,0:T(8,128)S(1)}, u32[]{:S(2)}, u32[]{:S(2)}) collective-permute-start(f32[272,256]{1,0:T(8,128)S(1)} %pair_kernel.1.refs_1_), channel_id=1, source_target_pairs={{0,2},{1,3},{2,4},{3,5},{4,6},{5,7},{6,0},{7,1},{8,10},{9,11},{10,... | collective-permute-start | bytes 835592 | tf_op jit(solution)/shard_map/ppermute | solution.py:46
  9.5 2.8 %collective-permute-start.4 = (f32[256,256]{1,0:T(8,128)S(1)}, f32[256,256]{1,0:T(8,128)S(1)}, u32[]{:S(2)}, u32[]{:S(2)}) collective-permute-start(f32[256,256]{1,0:T(8,128)S(1)} %own_kernel.1.own), channel_id=1, source_target_pairs={{0,16},{1,17},{2,18},{3,19},{4,20},{5,21},{6,22},{7,23},{8,24},{9,... | collective-permute-start | bytes 786440 | tf_op jit(solution)/shard_map/ppermute | solution.py:46
  12.5 3.5 %collective-permute-done.2.both.refs_0_.r2 = f32[272,256]{1,0:T(8,128)S(1)} collective-permute-done((f32[272,256]{1,0:T(8,128)S(1)}, f32[272,256]{1,0:T(8,128)S(1)}, u32[]{:S(2)}, u32[]{:S(2)}) %collective-permute-start.2) | collective-permute-done | bytes 278560 | tf_op jit(solution)/shard_map/ppermute | solution.py:46
  16.1 3.5 %collective-permute-start.7 = (f32[544,256]{1,0:T(8,128)S(1)}, f32[544,256]{1,0:T(8,128)S(1)}, u32[]{:S(2)}, u32[]{:S(2)}) collective-permute-start(f32[544,256]{1,0:T(8,128)S(1)} %stack_kernel.4), channel_id=1, source_target_pairs={{0,1},{1,2},{2,3},{3,4},{4,5},{5,6},{6,7},{7,0},{8,9},{9,10},{10,1... | collective-permute-start | bytes 1671176 | tf_op jit(solution)/shard_map/ppermute | solution.py:46
  20.7 1.9 %collective-permute-start.5 = (f32[256,256]{1,0:T(8,128)S(1)}, f32[256,256]{1,0:T(8,128)S(1)}, u32[]{:S(2)}, u32[]{:S(2)}) collective-permute-start(f32[256,256]{1,0:T(8,128)S(1)} %get-tuple-element.29), channel_id=1, source_target_pairs={{0,64},{1,65},{2,66},{3,67},{4,68},{5,69},{6,70},{7,71},{8,72},{9,... | collective-permute-start | bytes 786440 | tf_op jit(solution)/shard_map/ppermute | solution.py:41
  22.6 1.9 %collective-permute-start.8 = (f32[136,256]{1,0:T(8,128)S(1)}, f32[136,256]{1,0:T(8,128)S(1)}, u32[]{:S(2)}, u32[]{:S(2)}) collective-permute-start(f32[136,256]{1,0:T(8,128)S(1)} %third.1.refs_0_), channel_id=1, source_target_pairs={{0,2},{1,3},{2,4},{3,5},{4,6},{5,7},{6,0},{7,1},{8,10},{9,11},{10,... | collective-permute-start | bytes 417800 | tf_op jit(solution)/shard_map/ppermute | solution.py:46
  24.6 1.5 %collective-permute-start.6 = (f32[768,256]{1,0:T(8,128)S(1)}, f32[768,256]{1,0:T(8,128)S(1)}, u32[]{:S(2)}, u32[]{:S(2)}) collective-permute-start(f32[768,256]{1,0:T(8,128)S(1)} %stack_kernel.3), channel_id=1, source_target_pairs={{0,32},{1,33},{2,34},{3,35},{4,36},{5,37},{6,38},{7,39},{8,40},{9,... | collective-permute-start | bytes 2359304 | tf_op jit(solution)/shard_map/ppermute | solution.py:46
  26.1 5.7 %collective-permute-done.8.refs_1_ = f32[136,256]{1,0:T(8,128)S(1)} collective-permute-done((f32[136,256]{1,0:T(8,128)S(1)}, f32[136,256]{1,0:T(8,128)S(1)}, u32[]{:S(2)}, u32[]{:S(2)}) %collective-permute-start.8) | collective-permute-done | bytes 139296 | tf_op jit(solution)/shard_map/ppermute | solution.py:46
  32.4 4.2 %collective-permute-done.6.y_rest = f32[768,256]{1,0:T(8,128)S(1)} collective-permute-done((f32[768,256]{1,0:T(8,128)S(1)}, f32[768,256]{1,0:T(8,128)S(1)}, u32[]{:S(2)}, u32[]{:S(2)}) %collective-permute-start.6) | collective-permute-done | bytes 786464 | tf_op jit(solution)/shard_map/ppermute | solution.py:46
  38.2 4.9 %forward.3 = (f32[2,4,256,512]{3,2,1,0:T(8,128)S(1)}, f32[2,4,256,512]{3,2,1,0:T(8,128)S(1)}, f32[3,8,128]{2,1,0:T(8,128)S(1)}) custom-call(s32[4]{0:T(128)S(1)} %pad_add_fusion.pos_ref, bf16[2048,256]{1,0:T(8,128)(2,1)S(1)} %get-tuple-element.30.xh, bf16[2048,256]{1,0:T(8,128)(2,1)S(1)} %get-tuple-element.31.xl, ...), custom_call_target="tpu_custom_call" | custom-call | flops 3221225472 | bytes 10485760 | tf_op jit(solution)/shard_map/forward/pallas_call | solution.py:243
  43.1 3.2 %collective-permute-start.11 = (f32[3,8,128]{2,1,0:T(8,128)S(1)}, f32[3,8,128]{2,1,0:T(8,128)S(1)}, u32[]{:S(2)}, u32[]{:S(2)}) collective-permute-start(f32[3,8,128]{2,1,0:T(8,128)S(1)} %get-tuple-element.35), channel_id=1, source_target_pairs={{0,64},{1,65},{2,66},{3,67},{4,68},{5,69},{6,70},{7,71},{8,72},{9,... | collective-permute-start | bytes 36872 | tf_op jit(solution)/shard_map/ppermute | solution.py:41
  46.3 4.8 %forward.2 = (f32[2,4,256,512]{3,2,1,0:T(8,128)S(1)}, f32[2,4,256,512]{3,2,1,0:T(8,128)S(1)}, f32[3,8,128]{2,1,0:T(8,128)S(1)}) custom-call(s32[4]{0:T(128)S(1)} %pad_add_fusion.pos_ref, bf16[2048,256]{1,0:T(8,128)(2,1)S(1)} %get-tuple-element.30.xh, bf16[2048,256]{1,0:T(8,128)(2,1)S(1)} %get-tuple-element.31.xl, f32[8,136,256]{2,1,0:T(8,128)S(1)} %get-tuple-element.32.q_ref.mine), custom_call_target="tpu_custom_call" | custom-call | flops 3221225472 | bytes 10485760 | tf_op jit(solution)/shard_map/forward/pallas_call | solution.py:243
  51.1 12.3 %all_to_all.10.got = f32[8,3,8,128]{3,2,1,0:T(8,128)S(1)} all-to-all(f32[8,3,8,128]{3,2,1,0:T(8,128)S(1)} %spread_kernel.1), channel_id=1, replica_groups=mesh['yh'=2,'c'=2,'yl'=2,'x'=4,'z'=8] {'z'}, dimensions={0} | all-to-all | bytes 196608 | tf_op jit(solution)/shard_map/all_to_all | solution.py:466
  64.8 9.6 %backward_a.1 = (f32[8,128,256]{2,1,0:T(8,128)S(1)}, f32[520,256]{1,0:T(8,128)S(1)}, f32[520,256]{1,0:T(8,128)S(1)}, f32[1]{0:T(128)}) custom-call(s32[4]{0:T(128)S(1)} %pad_add_fusion.pos_ref, bf16[2048,256]{1,0:T(8,128)(2,1)S(1)} %get-tuple-element.30.xh, bf16[2048,256]{1,0:T(8,128)(2,1)S(1)} %get-tuple-element.31.xl, ...), custom_call_target="tpu_custom_call" | custom-call | flops 6442450944 | bytes 16777216 | tf_op jit(solution)/shard_map/backward_a/pallas_call | solution.py:356
  77.2 10.4 %backward_b.1 = (f32[8,128,256]{2,1,0:T(8,128)}, f32[4,256,256]{2,1,0:T(8,128)S(1)}) custom-call(s32[4]{0:T(128)S(1)} %pad_add_fusion.pos_ref, f32[1]{0:T(128)} %get-tuple-element.39.token, bf16[2048,256]{1,0:T(8,128)(2,1)S(1)} %get-tuple-element.30.xh, bf16[2048,256]{1,0:T(8,128)(2,1)S(1)} %get-tuple-element.31.xl, ...), custom_call_target="tpu_custom_call" | custom-call | flops 6442450944 | bytes 16777216 | tf_op jit(solution)/shard_map/backward_b/pallas_call | solution.py:371
  89.0 2.4 %collective-permute-done.15.b = f32[520,256]{1,0:T(8,128)S(1)} collective-permute-done((f32[520,256]{1,0:T(8,128)S(1)}, f32[520,256]{1,0:T(8,128)S(1)}, u32[]{:S(2)}, u32[]{:S(2)}) %collective-permute-start.15) | collective-permute-done | bytes 532512 | tf_op jit(solution)/shard_map/ppermute | solution.py:41
  91.5 3.6 %all-to-all-start.1 = ((f32[8,128,256]{2,1,0:T(8,128)}), f32[8,128,256]{2,1,0:T(8,128)S(1)}, u32[]{:S(2)}, u32[]{:S(2)}) async-start(f32[8,128,256]{2,1,0:T(8,128)} %get-tuple-element.51), calls=%async_computation.1 | async-start | bytes 2097152 | tf_op jit(solution)/shard_map/all_to_all | solution.py:473
  95.2 1.8 %collective-permute-start.17 = (f32[264,256]{1,0:T(8,128)S(1)}, f32[264,256]{1,0:T(8,128)S(1)}, u32[]{:S(2)}, u32[]{:S(2)}) collective-permute-start(f32[264,256]{1,0:T(8,128)S(1)} %get-tuple-element.48), channel_id=1, source_target_pairs={{0,16},{1,17},{2,18},{3,19},{4,20},{5,21},{6,22},{7,23},{8,24},{9,... | collective-permute-start | bytes 811016 | tf_op jit(solution)/shard_map/ppermute | solution.py:41
  97.0 1.6 %collective-permute-start.18 = (f32[264,256]{1,0:T(8,128)S(1)}, f32[264,256]{1,0:T(8,128)S(1)}, u32[]{:S(2)}, u32[]{:S(2)}) collective-permute-start(f32[264,256]{1,0:T(8,128)S(1)} %get-tuple-element.49), channel_id=1, source_target_pairs={{0,24},{1,25},{2,26},{3,27},{4,28},{5,29},{6,30},{7,31},{8,0},{9,1... | collective-permute-start | bytes 811016 | tf_op jit(solution)/shard_map/ppermute | solution.py:41
  98.6 11.2 %collective-permute-done.16.m1 = f32[264,256]{1,0:T(8,128)S(1)} collective-permute-done((f32[264,256]{1,0:T(8,128)S(1)}, f32[264,256]{1,0:T(8,128)S(1)}, u32[]{:S(2)}, u32[]{:S(2)}) %collective-permute-start.16) | collective-permute-done | bytes 270368 | tf_op jit(solution)/shard_map/ppermute | solution.py:41
  110.7 8.0 %collective-permute-done.19.mine2 = f32[264,256]{1,0:T(8,128)S(1)} collective-permute-done((f32[264,256]{1,0:T(8,128)S(1)}, f32[264,256]{1,0:T(8,128)S(1)}, u32[]{:S(2)}, u32[]{:S(2)}) %collective-permute-start.19) | collective-permute-done | bytes 270368 | tf_op jit(solution)/shard_map/ppermute | solution.py:41
  118.8 1.5 %collective-permute-done.21.other2 = f32[264,256]{1,0:T(8,128)S(1)} collective-permute-done((f32[264,256]{1,0:T(8,128)S(1)}, f32[264,256]{1,0:T(8,128)S(1)}, u32[]{:S(2)}, u32[]{:S(2)}) %collective-permute-start.21) | collective-permute-done | bytes 270368 | tf_op jit(solution)/shard_map/ppermute | solution.py:41
  121.7 1.7 %all-to-all-done.1.got = f32[8,128,256]{2,1,0:T(8,128)S(1)} async-done(((f32[8,128,256]{2,1,0:T(8,128)}), f32[8,128,256]{2,1,0:T(8,128)S(1)}, u32[]{:S(2)}, u32[]{:S(2)}) %all-to-all-start.1) | async-done | bytes 1048608 | tf_op jit(solution)/shard_map/all_to_all | solution.py:473
  (50 shorter events, 16.4 us)
Async XLA Ops:
  2.2 1.7 %collective-permute-start.1 = (f32[136,256]{1,0:T(8,128)S(1)}, f32[136,256]{1,0:T(8,128)S(1)}, u32[]{:S(2)}, u32[]{:S(2)}) collective-permute-start(f32[136,256]{1,0:T(8,128)S(1)} %start_kernel.1.mine.q), channel_id=1, source_target_pairs={{0,64},{1,65},{2,66},{3,67},{4,68},{5,69},{6,70},{7,71},{8,72},{9,... | collective-permute-start | bytes 417800 | tf_op jit(solution)/shard_map/ppermute | solution.py:41
  2.3 17.8 %collective-permute-start = (f32[512,256]{1,0:T(8,128)}, f32[512,256]{1,0:T(8,128)S(1)}, u32[]{:S(2)}, u32[]{:S(2)}) collective-permute-start(f32[512,256]{1,0:T(8,128)} %items.1), channel_id=1, source_target_pairs={{0,8},{1,9},{2,10},{3,11},{4,12},{5,13},{6,14},{7,15},{8,16},{9,17... | collective-permute-start | bytes 1572872 | tf_op jit(solution)/shard_map/ppermute | solution.py:46
  4.5 11.5 %collective-permute-start.2 = (f32[272,256]{1,0:T(8,128)S(1)}, f32[272,256]{1,0:T(8,128)S(1)}, u32[]{:S(2)}, u32[]{:S(2)}) collective-permute-start(f32[272,256]{1,0:T(8,128)S(1)} %pair_kernel.1.refs_1_), channel_id=1, source_target_pairs={{0,2},{1,3},{2,4},{3,5},{4,6},{5,7},{6,0},{7,1},{8,10},{9,11},{10,... | collective-permute-start | bytes 835592 | tf_op jit(solution)/shard_map/ppermute | solution.py:46
  7.9 1.0 copy-start
  9.5 10.1 %collective-permute-start.4 = (f32[256,256]{1,0:T(8,128)S(1)}, f32[256,256]{1,0:T(8,128)S(1)}, u32[]{:S(2)}, u32[]{:S(2)}) collective-permute-start(f32[256,256]{1,0:T(8,128)S(1)} %own_kernel.1.own), channel_id=1, source_target_pairs={{0,16},{1,17},{2,18},{3,19},{4,20},{5,21},{6,22},{7,23},{8,24},{9,... | collective-permute-start | bytes 786440 | tf_op jit(solution)/shard_map/ppermute | solution.py:46
  12.3 7.3 %collective-permute-start.3 = (f32[256,256]{1,0:T(8,128)S(1)}, f32[256,256]{1,0:T(8,128)S(1)}, u32[]{:S(2)}, u32[]{:S(2)}) collective-permute-start(f32[256,256]{1,0:T(8,128)S(1)} %own_kernel.1.own), channel_id=1, source_target_pairs={{0,32},{1,33},{2,34},{3,35},{4,36},{5,37},{6,38},{7,39},{8,40},{9,... | collective-permute-start | bytes 786440 | tf_op jit(solution)/shard_map/ppermute | solution.py:46
  16.1 15.7 %collective-permute-start.7 = (f32[544,256]{1,0:T(8,128)S(1)}, f32[544,256]{1,0:T(8,128)S(1)}, u32[]{:S(2)}, u32[]{:S(2)}) collective-permute-start(f32[544,256]{1,0:T(8,128)S(1)} %stack_kernel.4), channel_id=1, source_target_pairs={{0,1},{1,2},{2,3},{3,4},{4,5},{5,6},{6,7},{7,0},{8,9},{9,10},{10,1... | collective-permute-start | bytes 1671176 | tf_op jit(solution)/shard_map/ppermute | solution.py:46
  20.7 3.8 %collective-permute-start.5 = (f32[256,256]{1,0:T(8,128)S(1)}, f32[256,256]{1,0:T(8,128)S(1)}, u32[]{:S(2)}, u32[]{:S(2)}) collective-permute-start(f32[256,256]{1,0:T(8,128)S(1)} %get-tuple-element.29), channel_id=1, source_target_pairs={{0,64},{1,65},{2,66},{3,67},{4,68},{5,69},{6,70},{7,71},{8,72},{9,... | collective-permute-start | bytes 786440 | tf_op jit(solution)/shard_map/ppermute | solution.py:41
  22.6 9.2 %collective-permute-start.8 = (f32[136,256]{1,0:T(8,128)S(1)}, f32[136,256]{1,0:T(8,128)S(1)}, u32[]{:S(2)}, u32[]{:S(2)}) collective-permute-start(f32[136,256]{1,0:T(8,128)S(1)} %third.1.refs_0_), channel_id=1, source_target_pairs={{0,2},{1,3},{2,4},{3,5},{4,6},{5,7},{6,0},{7,1},{8,10},{9,11},{10,... | collective-permute-start | bytes 417800 | tf_op jit(solution)/shard_map/ppermute | solution.py:46
  24.6 12.1 %collective-permute-start.6 = (f32[768,256]{1,0:T(8,128)S(1)}, f32[768,256]{1,0:T(8,128)S(1)}, u32[]{:S(2)}, u32[]{:S(2)}) collective-permute-start(f32[768,256]{1,0:T(8,128)S(1)} %stack_kernel.3), channel_id=1, source_target_pairs={{0,32},{1,33},{2,34},{3,35},{4,36},{5,37},{6,38},{7,39},{8,40},{9,... | collective-permute-start | bytes 2359304 | tf_op jit(solution)/shard_map/ppermute | solution.py:46
  31.8 5.7 %collective-permute-start.10 = (f32[680,256]{1,0:T(8,128)S(1)}, f32[680,256]{1,0:T(8,128)S(1)}, u32[]{:S(2)}, u32[]{:S(2)}) collective-permute-start(f32[680,256]{1,0:T(8,128)S(1)} %stack_kernel.5.r314), channel_id=1, source_target_pairs={{0,64},{1,65},{2,66},{3,67},{4,68},{5,69},{6,70},{7,71},{8,72},{9,... | collective-permute-start | bytes 2088968 | tf_op jit(solution)/shard_map/ppermute | solution.py:41
  31.9 5.6 %collective-permute-start.9 = (f32[272,256]{1,0:T(8,128)S(1)}, f32[272,256]{1,0:T(8,128)S(1)}, u32[]{:S(2)}, u32[]{:S(2)}) collective-permute-start(f32[272,256]{1,0:T(8,128)S(1)} %collective-permute-done.2.both.refs_0_.r2), channel_id=1, source_target_pairs={{0,64},{1,65},{2,66},{3,67},{4,68},{5,69},{6,70},{7,71},{8,72},{9,... | collective-permute-start | bytes 835592 | tf_op jit(solution)/shard_map/ppermute | solution.py:41
  43.1 8.0 %collective-permute-start.11 = (f32[3,8,128]{2,1,0:T(8,128)S(1)}, f32[3,8,128]{2,1,0:T(8,128)S(1)}, u32[]{:S(2)}, u32[]{:S(2)}) collective-permute-start(f32[3,8,128]{2,1,0:T(8,128)S(1)} %get-tuple-element.35), channel_id=1, source_target_pairs={{0,64},{1,65},{2,66},{3,67},{4,68},{5,69},{6,70},{7,71},{8,72},{9,... | collective-permute-start | bytes 36872 | tf_op jit(solution)/shard_map/ppermute | solution.py:41
  63.6 1.3 %collective-permute-start.12 = (f32[16,128]{1,0:T(8,128)S(1)}, f32[16,128]{1,0:T(8,128)S(1)}, u32[]{:S(2)}, u32[]{:S(2)}) collective-permute-start(f32[16,128]{1,0:T(8,128)S(1)} %merge_kernel.1.lse_m), channel_id=1, source_target_pairs={{0,64},{1,65},{2,66},{3,67},{4,68},{5,69},{6,70},{7,71},{8,72},{9,... | collective-permute-start | bytes 24584 | tf_op jit(solution)/shard_map/ppermute | solution.py:41
  74.4 2.7 %collective-permute-start.13 = (f32[8,128,256]{2,1,0:T(8,128)S(1)}, f32[8,128,256]{2,1,0:T(8,128)S(1)}, u32[]{:S(2)}, u32[]{:S(2)}) collective-permute-start(f32[8,128,256]{2,1,0:T(8,128)S(1)} %get-tuple-element.41), channel_id=1, source_target_pairs={{0,64},{1,65},{2,66},{3,67},{4,68},{5,69},{6,70},{7,71},{8,72},{9,... | collective-permute-start | bytes 3145736 | tf_op jit(solution)/shard_map/ppermute | solution.py:41
  74.7 14.3 %collective-permute-start.14 = (f32[520,256]{1,0:T(8,128)S(1)}, f32[520,256]{1,0:T(8,128)S(1)}, u32[]{:S(2)}, u32[]{:S(2)}) collective-permute-start(f32[520,256]{1,0:T(8,128)S(1)} %get-tuple-element.43), channel_id=1, source_target_pairs={{0,32},{1,33},{2,34},{3,35},{4,36},{5,37},{6,38},{7,39},{8,40},{9,... | collective-permute-start | bytes 1597448 | tf_op jit(solution)/shard_map/ppermute | solution.py:41
  76.1 15.3 %collective-permute-start.15 = (f32[520,256]{1,0:T(8,128)S(1)}, f32[520,256]{1,0:T(8,128)S(1)}, u32[]{:S(2)}, u32[]{:S(2)}) collective-permute-start(f32[520,256]{1,0:T(8,128)S(1)} %get-tuple-element.44), channel_id=1, source_target_pairs={{0,160},{1,161},{2,162},{3,163},{4,164},{5,165},{6,166},{7,167},{8... | collective-permute-start | bytes 1597448 | tf_op jit(solution)/shard_map/ppermute | solution.py:41
  91.5 31.9 %all-to-all-start.1 = ((f32[8,128,256]{2,1,0:T(8,128)}), f32[8,128,256]{2,1,0:T(8,128)S(1)}, u32[]{:S(2)}, u32[]{:S(2)}) async-start(f32[8,128,256]{2,1,0:T(8,128)} %get-tuple-element.51), calls=%async_computation.1 | async-start | bytes 2097152 | tf_op jit(solution)/shard_map/all_to_all | solution.py:473
  95.1 14.7 %collective-permute-start.16 = (f32[264,256]{1,0:T(8,128)S(1)}, f32[264,256]{1,0:T(8,128)S(1)}, u32[]{:S(2)}, u32[]{:S(2)}) collective-permute-start(f32[264,256]{1,0:T(8,128)S(1)} %get-tuple-element.47), channel_id=1, source_target_pairs={{0,8},{1,9},{2,10},{3,11},{4,12},{5,13},{6,14},{7,15},{8,16},{9,17... | collective-permute-start | bytes 811016 | tf_op jit(solution)/shard_map/ppermute | solution.py:41
  95.2 14.6 %collective-permute-start.17 = (f32[264,256]{1,0:T(8,128)S(1)}, f32[264,256]{1,0:T(8,128)S(1)}, u32[]{:S(2)}, u32[]{:S(2)}) collective-permute-start(f32[264,256]{1,0:T(8,128)S(1)} %get-tuple-element.48), channel_id=1, source_target_pairs={{0,16},{1,17},{2,18},{3,19},{4,20},{5,21},{6,22},{7,23},{8,24},{9,... | collective-permute-start | bytes 811016 | tf_op jit(solution)/shard_map/ppermute | solution.py:41
  97.0 13.4 %collective-permute-start.18 = (f32[264,256]{1,0:T(8,128)S(1)}, f32[264,256]{1,0:T(8,128)S(1)}, u32[]{:S(2)}, u32[]{:S(2)}) collective-permute-start(f32[264,256]{1,0:T(8,128)S(1)} %get-tuple-element.49), channel_id=1, source_target_pairs={{0,24},{1,25},{2,26},{3,27},{4,28},{5,29},{6,30},{7,31},{8,0},{9,1... | collective-permute-start | bytes 811016 | tf_op jit(solution)/shard_map/ppermute | solution.py:41
  110.5 8.3 %collective-permute-start.19 = (f32[264,256]{1,0:T(8,128)S(1)}, f32[264,256]{1,0:T(8,128)S(1)}, u32[]{:S(2)}, u32[]{:S(2)}) collective-permute-start(f32[264,256]{1,0:T(8,128)S(1)} %land_kernel.1.mine), channel_id=1, source_target_pairs={{0,128},{1,129},{2,130},{3,131},{4,132},{5,133},{6,134},{7,135},{8... | collective-permute-start | bytes 811016 | tf_op jit(solution)/shard_map/ppermute | solution.py:41
  110.7 8.0 %collective-permute-start.20 = (f32[264,256]{1,0:T(8,128)S(1)}, f32[264,256]{1,0:T(8,128)S(1)}, u32[]{:S(2)}, u32[]{:S(2)}) collective-permute-start(f32[264,256]{1,0:T(8,128)S(1)} %land_kernel.1.mine), channel_id=1, source_target_pairs={{0,64},{1,65},{2,66},{3,67},{4,68},{5,69},{6,70},{7,71},{8,72},{9,... | collective-permute-start | bytes 811016 | tf_op jit(solution)/shard_map/ppermute | solution.py:41
  118.8 1.5 %collective-permute-start.21 = (f32[264,256]{1,0:T(8,128)S(1)}, f32[264,256]{1,0:T(8,128)S(1)}, u32[]{:S(2)}, u32[]{:S(2)}) collective-permute-start(f32[264,256]{1,0:T(8,128)S(1)} %collective-permute-done.19.mine2), channel_id=1, source_target_pairs={{0,64},{1,65},{2,66},{3,67},{4,68},{5,69},{6,70},{7,71},{8,72},{9,... | collective-permute-start | bytes 811016 | tf_op jit(solution)/shard_map/ppermute | solution.py:41
  (2 other events, 1.6 us)

commit v7 on v6

--- a/solution.py
+++ b/solution.py
@@ -161,7 +161,7 @@
             other[where] = ref[at(row + (1 - c) * PAD, PAD), :]
 
 
-def pack_items_kernel(pos_ref, own, near, across, far, y_own, y_rest, xh, xl):
+def pack_items_kernel(pos_ref, after, own, near, across, far, y_own, y_rest, xh, xl):
     c = pos_ref[1]
 
     def put(slot, rows):
@@ -175,6 +175,17 @@
     put(7 - 2 * c, y_rest[:HALF, :])
     put(5 + 2 * c, y_rest[HALF : 2 * HALF, :])
     put(6, y_rest[2 * HALF :, :])
+
+
+def pack_items(*operands):
+    return pl.pallas_call(
+        pack_items_kernel,
+        in_specs=[SMEM, pl.BlockSpec(memory_space=pl.ANY)] + [VMEM] * 6,
+        out_specs=[VMEM] * 2,
+        out_shape=[shape(LOCAL, E, dtype=bf16)] * 2,
+        compiler_params=params(10),
+        name="pack_items",
+    )(*operands)
 
 
 def join_stats(a, b):
@@ -403,9 +414,7 @@
         [pos, q, qo, r2, r314, send(r2, dc=1), send(r314, dc=1)],
         [shape(ZN, PAD, E)] * 2,
     )
-    xh, xl = small(
-        pack_items_kernel, [pos, own, near, across, far, y0, y_rest], [shape(LOCAL, E, dtype=bf16)] * 2
-    )
+    xh, xl = pack_items(pos, mine, own, near, across, far, y0, y_rest)
     return mine, other, xh, xl
 
 

time: 124 us -> 124 us (level)
    ppermute x7, waiting for transfers between devices: 13.4 us -> 10.7 us  [twin(): lax.ppermute(a, AXES, [(down if i >> 6 & 1 else up)[i] for i in range(256)])]
    ppermute x15, waiting for transfers between devices: 26.8 us -> 28.5 us  [send(): return lax.ppermute(a, AXES, pairs(**shift))]
    pallas_call x14 -> x13, Pallas kernels: 5.77 us -> 4.89 us  [small(): pl.pallas_call(kernel, in_specs=[SMEM if a.ndim == 1 else VMEM for a in i...]
  transfers between devices with their start and end apart: 23 -> 23, of which waited for: 12 -> 13; matrix products, arithmetic and copies ran while one was open for 0% -> 0% of each run, Pallas kernels for 16% -> 16%
where the time goes in v7:
time: 124 us
  waiting for transfers between devices  40.8 us (33%)
  Pallas kernels  37.1 us (30%)
  starting transfers between devices  30.3 us (24%)
  blocking collectives  12.3 us (10%)
  local copies, waits for them, and re-layouts  2.59 us (2%)
    ppermute x15, waiting for transfers between devices, send(): return lax.ppermute(a, AXES, pairs(**shift))  28.5 us
    ppermute x7, starting transfers between devices, twin(): lax.ppermute(a, AXES, [(down if i >> 6 & 1 else up)[i] for i in range(256)])  14.9 us
    all_to_all x1, blocking collectives, body(): stats = lax.all_to_all(stats, 'z', 0, 0, tiled=True)  12.3 us
    ppermute x15, starting transfers between devices, send(): return lax.ppermute(a, AXES, pairs(**shift))  11.9 us
    pallas_call x1, Pallas kernels, backward_b(): pl.pallas_call(backward_b_kernel, grid=(2 * STEPS,), in_specs=[SMEM, SMEM...  10.8 us
    ppermute x7, waiting for transfers between devices, twin(): lax.ppermute(a, AXES, [(down if i >> 6 & 1 else up)[i] for i in range(256)])  10.7 us
    pallas_call x2, Pallas kernels, forward(): pl.pallas_call(forward_kernel, grid=(STEPS,), in_specs=[SMEM, pl.BlockSpe...  10.1 us
    pallas_call x1, Pallas kernels, backward_a(): pl.pallas_call(backward_a_kernel, grid=(2 * STEPS,), in_specs=[SMEM, X_SP...  9.82 us
  transfers between devices with their start and end apart: 23, of which 13 were waited for; matrix products, arithmetic and copies ran while one was open for 0% of the time, Pallas kernels for 16%

profile of v7, /device:TPU:24, one launch (start us, length us, event | category | flops | bytes accessed | tf_op | source)
XLA Modules:
  0.0 124.0 jit_solution(17709327337248993144)
XLA Ops:
  2.3 1.6 %collective-permute-start.8 = (f32[512,256]{1,0:T(8,128)}, f32[512,256]{1,0:T(8,128)S(1)}, u32[]{:S(2)}, u32[]{:S(2)}) collective-permute-start(f32[512,256]{1,0:T(8,128)} %items.1), channel_id=1, source_target_pairs={{0,8},{1,9},{2,10},{3,11},{4,12},{5,13},{6,14},{7,15},{8,16},{9,17... | collective-permute-start | bytes 1572872 | tf_op jit(solution)/shard_map/ppermute | solution.py:46
  4.5 3.3 %collective-permute-start.1 = (f32[272,256]{1,0:T(8,128)S(1)}, f32[272,256]{1,0:T(8,128)S(1)}, u32[]{:S(2)}, u32[]{:S(2)}) collective-permute-start(f32[272,256]{1,0:T(8,128)S(1)} %pair_kernel.1.refs_1_), channel_id=1, source_target_pairs={{0,2},{1,3},{2,4},{3,5},{4,6},{5,7},{6,0},{7,1},{8,10},{9,11},{10,... | collective-permute-start | bytes 835592 | tf_op jit(solution)/shard_map/ppermute | solution.py:46
  9.5 2.8 %collective-permute-start.4 = (f32[256,256]{1,0:T(8,128)S(1)}, f32[256,256]{1,0:T(8,128)S(1)}, u32[]{:S(2)}, u32[]{:S(2)}) collective-permute-start(f32[256,256]{1,0:T(8,128)S(1)} %own_kernel.1.own), channel_id=1, source_target_pairs={{0,16},{1,17},{2,18},{3,19},{4,20},{5,21},{6,22},{7,23},{8,24},{9,... | collective-permute-start | bytes 786440 | tf_op jit(solution)/shard_map/ppermute | solution.py:46
  12.5 3.5 %collective-permute-done.1.refs_0_.both.r2 = f32[272,256]{1,0:T(8,128)S(1)} collective-permute-done((f32[272,256]{1,0:T(8,128)S(1)}, f32[272,256]{1,0:T(8,128)S(1)}, u32[]{:S(2)}, u32[]{:S(2)}) %collective-permute-start.1) | collective-permute-done | bytes 278560 | tf_op jit(solution)/shard_map/ppermute | solution.py:46
  16.1 3.5 %collective-permute-start.2 = (f32[544,256]{1,0:T(8,128)S(1)}, f32[544,256]{1,0:T(8,128)S(1)}, u32[]{:S(2)}, u32[]{:S(2)}) collective-permute-start(f32[544,256]{1,0:T(8,128)S(1)} %stack_kernel.3), channel_id=1, source_target_pairs={{0,1},{1,2},{2,3},{3,4},{4,5},{5,6},{6,7},{7,0},{8,9},{9,10},{10,1... | collective-permute-start | bytes 1671176 | tf_op jit(solution)/shard_map/ppermute | solution.py:46
  20.7 1.9 %collective-permute-start.9 = (f32[256,256]{1,0:T(8,128)S(1)}, f32[256,256]{1,0:T(8,128)S(1)}, u32[]{:S(2)}, u32[]{:S(2)}) collective-permute-start(f32[256,256]{1,0:T(8,128)S(1)} %get-tuple-element.30), channel_id=1, source_target_pairs={{0,64},{1,65},{2,66},{3,67},{4,68},{5,69},{6,70},{7,71},{8,72},{9,... | collective-permute-start | bytes 786440 | tf_op jit(solution)/shard_map/ppermute | solution.py:41
  22.6 1.9 %collective-permute-start.5 = (f32[136,256]{1,0:T(8,128)S(1)}, f32[136,256]{1,0:T(8,128)S(1)}, u32[]{:S(2)}, u32[]{:S(2)}) collective-permute-start(f32[136,256]{1,0:T(8,128)S(1)} %third.1.refs_0_), channel_id=1, source_target_pairs={{0,2},{1,3},{2,4},{3,5},{4,6},{5,7},{6,0},{7,1},{8,10},{9,11},{10,... | collective-permute-start | bytes 417800 | tf_op jit(solution)/shard_map/ppermute | solution.py:46
  24.6 1.5 %collective-permute-start.10 = (f32[768,256]{1,0:T(8,128)S(1)}, f32[768,256]{1,0:T(8,128)S(1)}, u32[]{:S(2)}, u32[]{:S(2)}) collective-permute-start(f32[768,256]{1,0:T(8,128)S(1)} %stack_kernel.5), channel_id=1, source_target_pairs={{0,32},{1,33},{2,34},{3,35},{4,36},{5,37},{6,38},{7,39},{8,40},{9,... | collective-permute-start | bytes 2359304 | tf_op jit(solution)/shard_map/ppermute | solution.py:46
  26.1 5.7 %collective-permute-done.5.refs_1_ = f32[136,256]{1,0:T(8,128)S(1)} collective-permute-done((f32[136,256]{1,0:T(8,128)S(1)}, f32[136,256]{1,0:T(8,128)S(1)}, u32[]{:S(2)}, u32[]{:S(2)}) %collective-permute-start.5) | collective-permute-done | bytes 139296 | tf_op jit(solution)/shard_map/ppermute | solution.py:46
  32.4 2.0 %collective-permute-done.6.s2 = f32[272,256]{1,0:T(8,128)S(1)} collective-permute-done((f32[272,256]{1,0:T(8,128)S(1)}, f32[272,256]{1,0:T(8,128)S(1)}, u32[]{:S(2)}, u32[]{:S(2)}) %collective-permute-start.6) | collective-permute-done | bytes 278560 | tf_op jit(solution)/shard_map/ppermute | solution.py:41
  37.5 5.0 %forward.3 = (f32[2,4,256,512]{3,2,1,0:T(8,128)S(1)}, f32[2,4,256,512]{3,2,1,0:T(8,128)S(1)}, f32[3,8,128]{2,1,0:T(8,128)S(1)}) custom-call(s32[4]{0:T(128)S(1)} %pad_add_fusion.pos_ref, bf16[2048,256]{1,0:T(8,128)(2,1)S(1)} %get-tuple-element.31.xh, bf16[2048,256]{1,0:T(8,128)(2,1)S(1)} %get-tuple-element.32.xl, ...), custom_call_target="tpu_custom_call" | custom-call | flops 3221225472 | bytes 10485760 | tf_op jit(solution)/shard_map/forward/pallas_call | solution.py:254
  42.6 3.2 %collective-permute-start.11 = (f32[3,8,128]{2,1,0:T(8,128)S(1)}, f32[3,8,128]{2,1,0:T(8,128)S(1)}, u32[]{:S(2)}, u32[]{:S(2)}) collective-permute-start(f32[3,8,128]{2,1,0:T(8,128)S(1)} %get-tuple-element.35), channel_id=1, source_target_pairs={{0,64},{1,65},{2,66},{3,67},{4,68},{5,69},{6,70},{7,71},{8,72},{9,... | collective-permute-start | bytes 36872 | tf_op jit(solution)/shard_map/ppermute | solution.py:41
  45.7 5.0 %forward.2 = (f32[2,4,256,512]{3,2,1,0:T(8,128)S(1)}, f32[2,4,256,512]{3,2,1,0:T(8,128)S(1)}, f32[3,8,128]{2,1,0:T(8,128)S(1)}) custom-call(s32[4]{0:T(128)S(1)} %pad_add_fusion.pos_ref, bf16[2048,256]{1,0:T(8,128)(2,1)S(1)} %get-tuple-element.31.xh, bf16[2048,256]{1,0:T(8,128)(2,1)S(1)} %get-tuple-element.32.xl, ...), custom_call_target="tpu_custom_call" | custom-call | flops 3221225472 | bytes 10485760 | tf_op jit(solution)/shard_map/forward/pallas_call | solution.py:254
  50.8 12.3 %all_to_all.10.got = f32[8,3,8,128]{3,2,1,0:T(8,128)S(1)} all-to-all(f32[8,3,8,128]{3,2,1,0:T(8,128)S(1)} %spread_kernel.1), channel_id=1, replica_groups=mesh['yh'=2,'c'=2,'yl'=2,'x'=4,'z'=8] {'z'}, dimensions={0} | all-to-all | bytes 196608 | tf_op jit(solution)/shard_map/all_to_all | solution.py:475
  64.5 9.8 %backward_a.1 = (f32[8,128,256]{2,1,0:T(8,128)S(1)}, f32[520,256]{1,0:T(8,128)S(1)}, f32[520,256]{1,0:T(8,128)S(1)}, f32[1]{0:T(128)}) custom-call(s32[4]{0:T(128)S(1)} %pad_add_fusion.pos_ref, bf16[2048,256]{1,0:T(8,128)(2,1)S(1)} %get-tuple-element.31.xh, bf16[2048,256]{1,0:T(8,128)(2,1)S(1)} %get-tuple-element.32.xl, ...), custom_call_target="tpu_custom_call" | custom-call | flops 6442450944 | bytes 16777216 | tf_op jit(solution)/shard_map/backward_a/pallas_call | solution.py:367
  77.1 10.8 %backward_b.1 = (f32[8,128,256]{2,1,0:T(8,128)}, f32[4,256,256]{2,1,0:T(8,128)S(1)}) custom-call(s32[4]{0:T(128)S(1)} %pad_add_fusion.pos_ref, f32[1]{0:T(128)} %get-tuple-element.39.token, bf16[2048,256]{1,0:T(8,128)(2,1)S(1)} %get-tuple-element.31.xh, bf16[2048,256]{1,0:T(8,128)(2,1)S(1)} %get-tuple-element.32.xl, ...), custom_call_target="tpu_custom_call" | custom-call | flops 6442450944 | bytes 16777216 | tf_op jit(solution)/shard_map/backward_b/pallas_call | solution.py:382
  88.9 2.4 %collective-permute-done.15.b = f32[520,256]{1,0:T(8,128)S(1)} collective-permute-done((f32[520,256]{1,0:T(8,128)S(1)}, f32[520,256]{1,0:T(8,128)S(1)}, u32[]{:S(2)}, u32[]{:S(2)}) %collective-permute-start.15) | collective-permute-done | bytes 532512 | tf_op jit(solution)/shard_map/ppermute | solution.py:41
  91.4 3.6 %all-to-all-start.1 = ((f32[8,128,256]{2,1,0:T(8,128)}), f32[8,128,256]{2,1,0:T(8,128)S(1)}, u32[]{:S(2)}, u32[]{:S(2)}) async-start(f32[8,128,256]{2,1,0:T(8,128)} %get-tuple-element.51), calls=%async_computation.1 | async-start | bytes 2097152 | tf_op jit(solution)/shard_map/all_to_all | solution.py:482
  95.1 1.8 %collective-permute-start.17 = (f32[264,256]{1,0:T(8,128)S(1)}, f32[264,256]{1,0:T(8,128)S(1)}, u32[]{:S(2)}, u32[]{:S(2)}) collective-permute-start(f32[264,256]{1,0:T(8,128)S(1)} %get-tuple-element.48), channel_id=1, source_target_pairs={{0,16},{1,17},{2,18},{3,19},{4,20},{5,21},{6,22},{7,23},{8,24},{9,... | collective-permute-start | bytes 811016 | tf_op jit(solution)/shard_map/ppermute | solution.py:41
  96.9 1.6 %collective-permute-start.18 = (f32[264,256]{1,0:T(8,128)S(1)}, f32[264,256]{1,0:T(8,128)S(1)}, u32[]{:S(2)}, u32[]{:S(2)}) collective-permute-start(f32[264,256]{1,0:T(8,128)S(1)} %get-tuple-element.49), channel_id=1, source_target_pairs={{0,24},{1,25},{2,26},{3,27},{4,28},{5,29},{6,30},{7,31},{8,0},{9,1... | collective-permute-start | bytes 811016 | tf_op jit(solution)/shard_map/ppermute | solution.py:41
  98.6 11.1 %collective-permute-done.16.m1 = f32[264,256]{1,0:T(8,128)S(1)} collective-permute-done((f32[264,256]{1,0:T(8,128)S(1)}, f32[264,256]{1,0:T(8,128)S(1)}, u32[]{:S(2)}, u32[]{:S(2)}) %collective-permute-start.16) | collective-permute-done | bytes 270368 | tf_op jit(solution)/shard_map/ppermute | solution.py:41
  110.6 8.0 %collective-permute-done.19.mine2 = f32[264,256]{1,0:T(8,128)S(1)} collective-permute-done((f32[264,256]{1,0:T(8,128)S(1)}, f32[264,256]{1,0:T(8,128)S(1)}, u32[]{:S(2)}, u32[]{:S(2)}) %collective-permute-start.19) | collective-permute-done | bytes 270368 | tf_op jit(solution)/shard_map/ppermute | solution.py:41
  118.7 1.5 %collective-permute-done.21.other2 = f32[264,256]{1,0:T(8,128)S(1)} collective-permute-done((f32[264,256]{1,0:T(8,128)S(1)}, f32[264,256]{1,0:T(8,128)S(1)}, u32[]{:S(2)}, u32[]{:S(2)}) %collective-permute-start.21) | collective-permute-done | bytes 270368 | tf_op jit(solution)/shard_map/ppermute | solution.py:41
  121.6 1.7 %all-to-all-done.1.got = f32[8,128,256]{2,1,0:T(8,128)S(1)} async-done(((f32[8,128,256]{2,1,0:T(8,128)}), f32[8,128,256]{2,1,0:T(8,128)S(1)}, u32[]{:S(2)}, u32[]{:S(2)}) %all-to-all-start.1) | async-done | bytes 1048608 | tf_op jit(solution)/shard_map/all_to_all | solution.py:482
  (50 shorter events, 17.5 us)
Async XLA Ops:
  2.2 1.7 %collective-permute-start = (f32[136,256]{1,0:T(8,128)S(1)}, f32[136,256]{1,0:T(8,128)S(1)}, u32[]{:S(2)}, u32[]{:S(2)}) collective-permute-start(f32[136,256]{1,0:T(8,128)S(1)} %start_kernel.1.mine.q), channel_id=1, source_target_pairs={{0,64},{1,65},{2,66},{3,67},{4,68},{5,69},{6,70},{7,71},{8,72},{9,... | collective-permute-start | bytes 417800 | tf_op jit(solution)/shard_map/ppermute | solution.py:41
  2.3 17.8 %collective-permute-start.8 = (f32[512,256]{1,0:T(8,128)}, f32[512,256]{1,0:T(8,128)S(1)}, u32[]{:S(2)}, u32[]{:S(2)}) collective-permute-start(f32[512,256]{1,0:T(8,128)} %items.1), channel_id=1, source_target_pairs={{0,8},{1,9},{2,10},{3,11},{4,12},{5,13},{6,14},{7,15},{8,16},{9,17... | collective-permute-start | bytes 1572872 | tf_op jit(solution)/shard_map/ppermute | solution.py:46
  4.5 11.5 %collective-permute-start.1 = (f32[272,256]{1,0:T(8,128)S(1)}, f32[272,256]{1,0:T(8,128)S(1)}, u32[]{:S(2)}, u32[]{:S(2)}) collective-permute-start(f32[272,256]{1,0:T(8,128)S(1)} %pair_kernel.1.refs_1_), channel_id=1, source_target_pairs={{0,2},{1,3},{2,4},{3,5},{4,6},{5,7},{6,0},{7,1},{8,10},{9,11},{10,... | collective-permute-start | bytes 835592 | tf_op jit(solution)/shard_map/ppermute | solution.py:46
  7.9 1.0 copy-start
  9.5 10.1 %collective-permute-start.4 = (f32[256,256]{1,0:T(8,128)S(1)}, f32[256,256]{1,0:T(8,128)S(1)}, u32[]{:S(2)}, u32[]{:S(2)}) collective-permute-start(f32[256,256]{1,0:T(8,128)S(1)} %own_kernel.1.own), channel_id=1, source_target_pairs={{0,16},{1,17},{2,18},{3,19},{4,20},{5,21},{6,22},{7,23},{8,24},{9,... | collective-permute-start | bytes 786440 | tf_op jit(solution)/shard_map/ppermute | solution.py:46
  12.3 7.3 %collective-permute-start.3 = (f32[256,256]{1,0:T(8,128)S(1)}, f32[256,256]{1,0:T(8,128)S(1)}, u32[]{:S(2)}, u32[]{:S(2)}) collective-permute-start(f32[256,256]{1,0:T(8,128)S(1)} %own_kernel.1.own), channel_id=1, source_target_pairs={{0,32},{1,33},{2,34},{3,35},{4,36},{5,37},{6,38},{7,39},{8,40},{9,... | collective-permute-start | bytes 786440 | tf_op jit(solution)/shard_map/ppermute | solution.py:46
  16.1 15.7 %collective-permute-start.2 = (f32[544,256]{1,0:T(8,128)S(1)}, f32[544,256]{1,0:T(8,128)S(1)}, u32[]{:S(2)}, u32[]{:S(2)}) collective-permute-start(f32[544,256]{1,0:T(8,128)S(1)} %stack_kernel.3), channel_id=1, source_target_pairs={{0,1},{1,2},{2,3},{3,4},{4,5},{5,6},{6,7},{7,0},{8,9},{9,10},{10,1... | collective-permute-start | bytes 1671176 | tf_op jit(solution)/shard_map/ppermute | solution.py:46
  20.7 3.8 %collective-permute-start.9 = (f32[256,256]{1,0:T(8,128)S(1)}, f32[256,256]{1,0:T(8,128)S(1)}, u32[]{:S(2)}, u32[]{:S(2)}) collective-permute-start(f32[256,256]{1,0:T(8,128)S(1)} %get-tuple-element.30), channel_id=1, source_target_pairs={{0,64},{1,65},{2,66},{3,67},{4,68},{5,69},{6,70},{7,71},{8,72},{9,... | collective-permute-start | bytes 786440 | tf_op jit(solution)/shard_map/ppermute | solution.py:41
  22.6 9.2 %collective-permute-start.5 = (f32[136,256]{1,0:T(8,128)S(1)}, f32[136,256]{1,0:T(8,128)S(1)}, u32[]{:S(2)}, u32[]{:S(2)}) collective-permute-start(f32[136,256]{1,0:T(8,128)S(1)} %third.1.refs_0_), channel_id=1, source_target_pairs={{0,2},{1,3},{2,4},{3,5},{4,6},{5,7},{6,0},{7,1},{8,10},{9,11},{10,... | collective-permute-start | bytes 417800 | tf_op jit(solution)/shard_map/ppermute | solution.py:46
  24.6 12.1 %collective-permute-start.10 = (f32[768,256]{1,0:T(8,128)S(1)}, f32[768,256]{1,0:T(8,128)S(1)}, u32[]{:S(2)}, u32[]{:S(2)}) collective-permute-start(f32[768,256]{1,0:T(8,128)S(1)} %stack_kernel.5), channel_id=1, source_target_pairs={{0,32},{1,33},{2,34},{3,35},{4,36},{5,37},{6,38},{7,39},{8,40},{9,... | collective-permute-start | bytes 2359304 | tf_op jit(solution)/shard_map/ppermute | solution.py:46
  31.8 2.6 %collective-permute-start.7 = (f32[680,256]{1,0:T(8,128)S(1)}, f32[680,256]{1,0:T(8,128)S(1)}, u32[]{:S(2)}, u32[]{:S(2)}) collective-permute-start(f32[680,256]{1,0:T(8,128)S(1)} %stack_kernel.4.r314), channel_id=1, source_target_pairs={{0,64},{1,65},{2,66},{3,67},{4,68},{5,69},{6,70},{7,71},{8,72},{9,... | collective-permute-start | bytes 2088968 | tf_op jit(solution)/shard_map/ppermute | solution.py:41
  31.9 2.5 %collective-permute-start.6 = (f32[272,256]{1,0:T(8,128)S(1)}, f32[272,256]{1,0:T(8,128)S(1)}, u32[]{:S(2)}, u32[]{:S(2)}) collective-permute-start(f32[272,256]{1,0:T(8,128)S(1)} %collective-permute-done.1.refs_0_.both.r2), channel_id=1, source_target_pairs={{0,64},{1,65},{2,66},{3,67},{4,68},{5,69},{6,70},{7,71},{8,72},{9,... | collective-permute-start | bytes 835592 | tf_op jit(solution)/shard_map/ppermute | solution.py:41
  42.6 8.2 %collective-permute-start.11 = (f32[3,8,128]{2,1,0:T(8,128)S(1)}, f32[3,8,128]{2,1,0:T(8,128)S(1)}, u32[]{:S(2)}, u32[]{:S(2)}) collective-permute-start(f32[3,8,128]{2,1,0:T(8,128)S(1)} %get-tuple-element.35), channel_id=1, source_target_pairs={{0,64},{1,65},{2,66},{3,67},{4,68},{5,69},{6,70},{7,71},{8,72},{9,... | collective-permute-start | bytes 36872 | tf_op jit(solution)/shard_map/ppermute | solution.py:41
  63.2 1.3 %collective-permute-start.12 = (f32[16,128]{1,0:T(8,128)S(1)}, f32[16,128]{1,0:T(8,128)S(1)}, u32[]{:S(2)}, u32[]{:S(2)}) collective-permute-start(f32[16,128]{1,0:T(8,128)S(1)} %merge_kernel.1.lse_m), channel_id=1, source_target_pairs={{0,64},{1,65},{2,66},{3,67},{4,68},{5,69},{6,70},{7,71},{8,72},{9,... | collective-permute-start | bytes 24584 | tf_op jit(solution)/shard_map/ppermute | solution.py:41
  74.3 2.7 %collective-permute-start.13 = (f32[8,128,256]{2,1,0:T(8,128)S(1)}, f32[8,128,256]{2,1,0:T(8,128)S(1)}, u32[]{:S(2)}, u32[]{:S(2)}) collective-permute-start(f32[8,128,256]{2,1,0:T(8,128)S(1)} %get-tuple-element.41), channel_id=1, source_target_pairs={{0,64},{1,65},{2,66},{3,67},{4,68},{5,69},{6,70},{7,71},{8,72},{9,... | collective-permute-start | bytes 3145736 | tf_op jit(solution)/shard_map/ppermute | solution.py:41
  74.6 14.3 %collective-permute-start.14 = (f32[520,256]{1,0:T(8,128)S(1)}, f32[520,256]{1,0:T(8,128)S(1)}, u32[]{:S(2)}, u32[]{:S(2)}) collective-permute-start(f32[520,256]{1,0:T(8,128)S(1)} %get-tuple-element.43), channel_id=1, source_target_pairs={{0,32},{1,33},{2,34},{3,35},{4,36},{5,37},{6,38},{7,39},{8,40},{9,... | collective-permute-start | bytes 1597448 | tf_op jit(solution)/shard_map/ppermute | solution.py:41
  76.0 15.3 %collective-permute-start.15 = (f32[520,256]{1,0:T(8,128)S(1)}, f32[520,256]{1,0:T(8,128)S(1)}, u32[]{:S(2)}, u32[]{:S(2)}) collective-permute-start(f32[520,256]{1,0:T(8,128)S(1)} %get-tuple-element.44), channel_id=1, source_target_pairs={{0,160},{1,161},{2,162},{3,163},{4,164},{5,165},{6,166},{7,167},{8... | collective-permute-start | bytes 1597448 | tf_op jit(solution)/shard_map/ppermute | solution.py:41
  91.4 31.9 %all-to-all-start.1 = ((f32[8,128,256]{2,1,0:T(8,128)}), f32[8,128,256]{2,1,0:T(8,128)S(1)}, u32[]{:S(2)}, u32[]{:S(2)}) async-start(f32[8,128,256]{2,1,0:T(8,128)} %get-tuple-element.51), calls=%async_computation.1 | async-start | bytes 2097152 | tf_op jit(solution)/shard_map/all_to_all | solution.py:482
  95.0 14.7 %collective-permute-start.16 = (f32[264,256]{1,0:T(8,128)S(1)}, f32[264,256]{1,0:T(8,128)S(1)}, u32[]{:S(2)}, u32[]{:S(2)}) collective-permute-start(f32[264,256]{1,0:T(8,128)S(1)} %get-tuple-element.47), channel_id=1, source_target_pairs={{0,8},{1,9},{2,10},{3,11},{4,12},{5,13},{6,14},{7,15},{8,16},{9,17... | collective-permute-start | bytes 811016 | tf_op jit(solution)/shard_map/ppermute | solution.py:41
  95.1 14.6 %collective-permute-start.17 = (f32[264,256]{1,0:T(8,128)S(1)}, f32[264,256]{1,0:T(8,128)S(1)}, u32[]{:S(2)}, u32[]{:S(2)}) collective-permute-start(f32[264,256]{1,0:T(8,128)S(1)} %get-tuple-element.48), channel_id=1, source_target_pairs={{0,16},{1,17},{2,18},{3,19},{4,20},{5,21},{6,22},{7,23},{8,24},{9,... | collective-permute-start | bytes 811016 | tf_op jit(solution)/shard_map/ppermute | solution.py:41
  96.9 13.4 %collective-permute-start.18 = (f32[264,256]{1,0:T(8,128)S(1)}, f32[264,256]{1,0:T(8,128)S(1)}, u32[]{:S(2)}, u32[]{:S(2)}) collective-permute-start(f32[264,256]{1,0:T(8,128)S(1)} %get-tuple-element.49), channel_id=1, source_target_pairs={{0,24},{1,25},{2,26},{3,27},{4,28},{5,29},{6,30},{7,31},{8,0},{9,1... | collective-permute-start | bytes 811016 | tf_op jit(solution)/shard_map/ppermute | solution.py:41
  110.4 8.3 %collective-permute-start.19 = (f32[264,256]{1,0:T(8,128)S(1)}, f32[264,256]{1,0:T(8,128)S(1)}, u32[]{:S(2)}, u32[]{:S(2)}) collective-permute-start(f32[264,256]{1,0:T(8,128)S(1)} %land_kernel.1.mine), channel_id=1, source_target_pairs={{0,128},{1,129},{2,130},{3,131},{4,132},{5,133},{6,134},{7,135},{8... | collective-permute-start | bytes 811016 | tf_op jit(solution)/shard_map/ppermute | solution.py:41
  110.6 8.0 %collective-permute-start.20 = (f32[264,256]{1,0:T(8,128)S(1)}, f32[264,256]{1,0:T(8,128)S(1)}, u32[]{:S(2)}, u32[]{:S(2)}) collective-permute-start(f32[264,256]{1,0:T(8,128)S(1)} %land_kernel.1.mine), channel_id=1, source_target_pairs={{0,64},{1,65},{2,66},{3,67},{4,68},{5,69},{6,70},{7,71},{8,72},{9,... | collective-permute-start | bytes 811016 | tf_op jit(solution)/shard_map/ppermute | solution.py:41
  118.7 1.5 %collective-permute-start.21 = (f32[264,256]{1,0:T(8,128)S(1)}, f32[264,256]{1,0:T(8,128)S(1)}, u32[]{:S(2)}, u32[]{:S(2)}) collective-permute-start(f32[264,256]{1,0:T(8,128)S(1)} %collective-permute-done.19.mine2), channel_id=1, source_target_pairs={{0,64},{1,65},{2,66},{3,67},{4,68},{5,69},{6,70},{7,71},{8,72},{9,... | collective-permute-start | bytes 811016 | tf_op jit(solution)/shard_map/ppermute | solution.py:41
  (2 other events, 1.6 us)
